TPU v7x, 32 devices: a whole 2x2x4 slice. The times are simulated.
32 devices in a mesh: seq: 8 (over z, x), head: 4 (over y, core).
Axes of the slice: x: 2, y: 2, z: 4, core: 2. Of those that a mesh axis runs over, the one named last changes fastest.
Arguments:
- vis_in: bfloat16 [8, 256, 1280], P('seq'), may hold values from -6 to 6
- live_tiles: int32 [8], P('seq'), may hold values from 1 to 4
- ln1_gain: float32 [1280], replicated, may hold values from 0.5 to 1.5
- w_qkv: bfloat16 [3, 1280, 1280], P(None, None, 'head'), may hold values from -0.15625 to 0.15625
- w_out: bfloat16 [1280, 1280], P('head'), may hold values from -0.15625 to 0.15625
- ln2_gain: float32 [1280], replicated, may hold values from 0.5 to 1.5
- w_fc1: bfloat16 [1280, 5120], P(None, 'head'), may hold values from -0.15625 to 0.15625
- w_fc2: bfloat16 [5120, 1280], P('head'), may hold values from -0.078125 to 0.078125
- w_kv: bfloat16 [1280, 2, 1024], replicated, may hold values from -0.15625 to 0.15625
- k_gain: float32 [128], replicated, may hold values from 0.5 to 1.5
- q_gain: float32 [128], replicated, may hold values from 0.5 to 1.5
- text_queries: bfloat16 [2048, 8192], P('seq', 'head'), may hold values from -6 to 6
- block_mask: int32 [16, 8], P('seq'), may hold values from 0 to 1, as said below
Outputs:
- attended: bfloat16 [2048, 8192], P('seq', 'head')
Inputs may be any that keep to these rules, and one draw needn't show every extreme that they name: `block_mask`: some blocks of text tokens attend to no image.
All inputs are finite; a program needn't handle non-finite values.
Results may differ from a plain program's by a relative error of at most 0.0085.
Values may be sent and summed in bfloat16 or wider, within the bound.
No kernel may reach another device: no remote copies, remote signals or barrier semaphores. Data moves between devices by JAX's collectives and lax.ppermute only.
A program may use at most 128 MiB of HBM per device.

v0:
```python
import math

import jax
import jax.numpy as jnp
from jax import lax
from jax.sharding import PartitionSpec as P

KVH = 8
HD = 128
TILE_TOK = 64
QB = 128
VHD = 80


def layer_norm(values, gain):
    center = values - jnp.mean(values, axis=-1, keepdims=True)
    spread = jnp.mean(center * center, axis=-1, keepdims=True)
    return center / jnp.sqrt(spread + 1e-05) * gain


def rms_norm(values, gain):
    return values / jnp.sqrt(jnp.mean(values * values, axis=-1, keepdims=True) + 1e-05) * gain


def finish_kv(projected, head_total, k_gain):
    shaped = projected.reshape(projected.shape[0], 2, head_total, HD)
    keys = rms_norm(shaped[:, 0], k_gain).astype(jnp.bfloat16)
    values = shaped[:, 1].astype(jnp.bfloat16)
    return jnp.stack([keys, values], axis=1)


def per_device(
    vis_in,
    live_tiles,
    ln1_gain,
    w_qkv,
    w_out,
    ln2_gain,
    w_fc1,
    w_fc2,
    w_kv,
    k_gain,
    q_gain,
    text_queries,
    block_mask,
):
    head_count = lax.axis_size("head")
    head_index = lax.axis_index("head")
    local_images, key_rows, width = vis_in.shape
    total_rows = local_images * key_rows
    share = total_rows // head_count
    hidden_in = vis_in.astype(jnp.float32).reshape(total_rows, width)
    normed = layer_norm(hidden_in, ln1_gain).astype(jnp.bfloat16)
    local_heads = w_qkv.shape[2] // VHD
    projected = jnp.einsum("rc,jcd->jrd", normed, w_qkv, preferred_element_type=jnp.float32).astype(
        jnp.bfloat16
    )
    projected = projected.reshape(3, local_images, key_rows, local_heads, VHD)
    tile_of = jnp.arange(key_rows, dtype=jnp.int32) // TILE_TOK
    live = (tile_of[None, :] < live_tiles[:, None]).astype(jnp.float32)
    scores = jnp.einsum(
        "iqhd,ikhd->ihqk", projected[0], projected[1], preferred_element_type=jnp.float32
    ) / math.sqrt(VHD)
    expo = jnp.exp(scores) * live[:, None, None, :]
    probs = (expo / jnp.sum(expo, axis=-1, keepdims=True)).astype(jnp.bfloat16)
    mixed = jnp.einsum(
        "ihqk,ikhd->iqhd", probs, projected[2], preferred_element_type=jnp.float32
    ).astype(jnp.bfloat16)
    mixed = mixed.reshape(total_rows, local_heads * VHD)
    attn_rows = lax.psum_scatter(
        jnp.dot(mixed, w_out, preferred_element_type=jnp.float32).astype(jnp.bfloat16),
        "head",
        scatter_dimension=0,
        tiled=True,
    ).astype(jnp.float32)
    own_rows = lax.dynamic_slice_in_dim(hidden_in, head_index * share, share, 0)
    resid = own_rows + attn_rows
    normed2 = layer_norm(resid, ln2_gain).astype(jnp.bfloat16)
    inner = jax.nn.gelu(
        jnp.dot(
            lax.all_gather(normed2, "head", axis=0, tiled=True),
            w_fc1,
            preferred_element_type=jnp.float32,
        ),
        approximate=False,
    ).astype(jnp.bfloat16)
    vision_out = (
        resid
        + lax.psum_scatter(
            jnp.dot(inner, w_fc2, preferred_element_type=jnp.float32).astype(jnp.bfloat16),
            "head",
            scatter_dimension=0,
            tiled=True,
        ).astype(jnp.float32)
    ).astype(jnp.bfloat16)
    kv_local = KVH // head_count
    split_weight = w_kv.reshape(width, 2, KVH, HD)
    own_weight = lax.dynamic_slice_in_dim(split_weight, head_index * kv_local, kv_local, 2).reshape(
        width, 2 * kv_local * HD
    )
    key_value = finish_kv(
        jnp.dot(
            lax.all_gather(vision_out, "head", axis=0, tiled=True),
            own_weight,
            preferred_element_type=jnp.float32,
        ),
        kv_local,
        k_gain,
    )
    key_value = key_value.reshape(local_images, key_rows, 2, kv_local, HD)
    text_rows = text_queries.shape[0]
    q_local = text_queries.shape[1] // HD
    group_size = q_local // kv_local
    queries = (
        rms_norm(text_queries.astype(jnp.float32).reshape(text_rows, q_local, HD), q_gain)
        / math.sqrt(HD)
    ).astype(jnp.bfloat16)
    queries = queries.reshape(text_rows, kv_local, group_size, HD)
    row_mask = jnp.repeat(block_mask, QB, axis=0)
    flag_rows = jnp.sum(row_mask, axis=1) > 0
    start_totals = (
        jnp.zeros((kv_local, group_size, text_rows), jnp.float32),
        jnp.zeros((kv_local, group_size, text_rows, HD), jnp.float32),
    )
    kv_part = lax.all_gather(key_value, "seq", axis=0, tiled=True)
    tiles_part = lax.all_gather(live_tiles, "seq", axis=0, tiled=True)

    def one_image(position, inner_totals):
        image_kv = lax.dynamic_index_in_dim(kv_part, position, 0, keepdims=False)
        image_tiles = lax.dynamic_index_in_dim(tiles_part, position, 0, keepdims=False)
        column = lax.dynamic_index_in_dim(row_mask, position, 1, keepdims=False)
        denom, accum = inner_totals
        key_live = (jnp.arange(key_rows, dtype=jnp.int32) // TILE_TOK < image_tiles).astype(
            jnp.float32
        )
        sims = jnp.einsum(
            "tkgd,skd->kgts", queries, image_kv[:, 0], preferred_element_type=jnp.float32
        )
        expo2 = jnp.exp(sims) * (
            column.astype(jnp.float32)[None, None, :, None] * key_live[None, None, None, :]
        )
        accum = accum + jnp.einsum(
            "kgts,skd->kgtd",
            expo2.astype(jnp.bfloat16),
            image_kv[:, 1],
            preferred_element_type=jnp.float32,
        )
        return (denom + jnp.sum(expo2, axis=-1), accum)

    denom, accum = lax.fori_loop(0, kv_part.shape[0], one_image, start_totals)
    safe = jnp.where(flag_rows[None, None, :], denom, jnp.float32(1.0))
    result = jnp.where(flag_rows[None, None, :, None], accum / safe[..., None], jnp.float32(0.0))
    return result.transpose(2, 0, 1, 3).reshape(text_rows, q_local * HD).astype(jnp.bfloat16)


def solution(mesh):
    placed = (
        P("seq", None, None),
        P("seq"),
        P(),
        P(None, None, "head"),
        P("head", None),
        P(),
        P(None, "head"),
        P("head", None),
        P(),
        P(),
        P(),
        P("seq", "head"),
        P("seq", None),
    )
    return jax.shard_map(
        per_device, mesh=mesh, in_specs=placed, out_specs=P("seq", "head"), check_vma=False
    )
```

profile of v0, /device:TPU:0, one launch (start us, length us, event | category | flops | bytes accessed | tf_op | source)
XLA Modules:
  0.0 280.7 jit_solution(14068544573872733256)
XLA Ops:
  21.5 23.0 %reduce-scatter.3.cloned.1.call-done = bf16[64,1280]{1,0:T(8,128)(2,1)} async-done(((bf16[256,1280]{1,0:T(8,128)(2,1)}), bf16[64,1280]{1,0:T(8,128)(2,1)}) %reduce-scatter.3.cloned.1.call-update) | async-done | bytes 163856 | tf_op jit(solution)/shard_map/reduce_scatter | solution.py:70
  48.2 7.9 %all_gather.12 = bf16[256,1280]{1,0:T(8,128)(2,1)} all-gather(bf16[64,1280]{1,0:T(8,128)(2,1)S(1)} %multiply_convert_fusion.2), channel_id=1, replica_groups=mesh['seq'=8,'head'=4] {'head'}, dimensions={0}, use_global_device_ids=true | all-gather | bytes 819200 | tf_op jit(solution)/shard_map/all_gather | solution.py:81
  56.1 7.4 %convolution_convert_fusion = bf16[256,1280]{1,0:T(8,128)(2,1)} fusion(bf16[1280,1280]{1,0:T(8,128)(2,1)S(1)} %copy-done, bf16[256,1280]{1,0:T(8,128)(2,1)} %all_gather.12, bf16[1280,1280]{1,0:T(8,128)(2,1)} %param.21), kind=kOutput, calls=%fused_computation.18 | convolution fusion | flops 1699348480 | bytes 7864320 | tf_op jit(solution)/shard_map/dot_general | solution.py:90
  63.6 9.3 %reshape.224 = bf16[1280,2,8,128]{3,2,1,0:T(8,128)(2,1)} reshape(bf16[1280,2,1024]{2,1,0:T(2,128)(2,1)} %param.23) | data formatting | bytes 10485760 | tf_op jit(solution)/shard_map/reshape | solution.py:97
  72.8 4.0 %constant_dynamic-slice_fusion = bf16[1280,2,2,128]{3,2,1,0:T(2,128)(2,1)} fusion(bf16[1280,2,8,128]{3,2,1,0:T(8,128)(2,1)} %reshape.224, s32[]{:T(128)S(6)} %select_n.53), kind=kLoop, calls=%fused_computation.115 | loop fusion | bytes 2621444 | tf_op jit(solution)/shard_map/dynamic_slice | solution.py:98
  76.9 4.3 %copy.21 = bf16[1280,2,2,128]{0,3,2,1:T(8,128)(2,1)} copy(bf16[1280,2,2,128]{3,2,1,0:T(2,128)(2,1)} %constant_dynamic-slice_fusion) | data formatting | bytes 2621440 | tf_op jit(solution)/shard_map/dynamic_slice | solution.py:98
  81.2 5.3 %reduce-scatter.5.cloned.1.call-done = bf16[64,1280]{1,0:T(8,128)(2,1)} async-done(((bf16[256,1280]{1,0:T(8,128)(2,1)}), bf16[64,1280]{1,0:T(8,128)(2,1)}) %reduce-scatter.5.cloned.1.call-update) | async-done | bytes 163856 | tf_op jit(solution)/shard_map/reduce_scatter | solution.py:89
  87.7 7.5 %all_gather.13 = bf16[256,1280]{1,0:T(8,128)(2,1)S(1)} all-gather(bf16[64,1280]{1,0:T(8,128)(2,1)S(1)} %add_convert_fusion), channel_id=1, replica_groups=mesh['seq'=8,'head'=4] {'head'}, dimensions={0}, use_global_device_ids=true | all-gather | bytes 819200 | tf_op jit(solution)/shard_map/all_gather | solution.py:103
  98.1 12.0 %all-reduce = s32[8]{0:T(128)} all-reduce(s32[8]{0:T(128)S(1)} %dynamic-update-slice), channel_id=1, replica_groups=mesh['seq'=8,'head'=4] {'seq'}, use_global_device_ids=true, to_apply=%add | all-reduce | flops 8 | bytes 64
  119.1 29.2 %all-gather.3.cloned.1.call-done = bf16[2048,2,2,128]{0,3,2,1:T(8,128)(2,1)} async-done(((bf16[256,2,2,128]{0,3,2,1:T(8,128)(2,1)}), bf16[2048,2,2,128]{0,3,2,1:T(8,128)(2,1)}) %all-gather.3.cloned.1.call-update) | async-done | bytes 2097168 | tf_op jit(solution)/shard_map/all_gather | solution.py:125
  152.0 4.6 %copy.23 = bf16[8,256,2,2,128]{4,1,3,2,0:T(8,128)(2,1)} copy(bf16[8,256,2,2,128]{1,0,4,3,2:T(8,128)(2,1)} %bitcast.126) | data formatting | bytes 4194304
  156.5 113.0 %while.18 = (s32[]{:T(128)}, f32[2,8,256]{2,1,0:T(8,128)}, f32[2,8,256,128]{3,2,1,0:T(8,128)}, bf16[8,256,2,2,128]{4,1,3,2,0:T(8,128)(2,1)}, bf16[256,2,8,128]{3...) while((s32[]{:T(128)}, f32[2,8,256]{2,1,0:T(8,128)}, ...), condition=%wide.region_12.13_spmd.clone, body=%wide.region_10.12_spmd.clone.sunk | while | flops 542186240 | bytes 16323748 | solution.py:150
  160.2 4.0 %fusion.113 = (f32[2,8,256]{2,1,0:T(8,128)S(1)}, f32[2,256,256,8]{2,1,3,0:T(8,128)}) fusion(f32[256,256]{0,1:T(8,128)S(1)} %broadcast_multiply_fusion.4, bf16[256,2,8,128]{3,0,2,1:T(8,128)(2,1)} %get-tuple-element.311, bf16[256,2,2,128]{3,0,2,1:T(8,128)(2,1)S(1)} %dynamic-slice_bitcast_fusion.2), kind=kOutput, calls=%fused_computation.2.clone.1 | convolution fusion | flops 270528512 | bytes 5652480 | tf_op jit(solution)/shard_map/while/body/eval_jaxpr/tkgd,skd->kgts/dot_general | solution.py:136
  164.8 4.6 %select_add_fusion.5 = f32[2,8,256,128]{3,2,1,0:T(8,128)} fusion(f32[2,8,256,128]{3,2,1,0:T(8,128)} %get-tuple-element.300, f32[2,256,256,8]{2,1,3,0:T(8,128)} %get-tuple-element.288, f32[256,256]{0,1:T(8,128)S(1)} %broadcast_multiply_fusion.4, pred[]{:T(512)S(6)} %compare.13, bf16[256,2,2,128]{3,0,2,1:T(8,128)(2,1)} %copy-done.1), kind=kOutput, calls=%fused_computation.4.clone.1 | convolution fusion | flops 271581184 | bytes 8781825 | tf_op jit(solution)/shard_map/while/body/eval_jaxpr/kgts,skd->kgtd/dot_general | solution.py:142
  173.1 4.0 %fusion.113 = (f32[2,8,256]{2,1,0:T(8,128)S(1)}, f32[2,256,256,8]{2,1,3,0:T(8,128)}) fusion(f32[256,256]{0,1:T(8,128)S(1)} %broadcast_multiply_fusion.4, bf16[256,2,8,128]{3,0,2,1:T(8,128)(2,1)} %get-tuple-element.311, bf16[256,2,2,128]{3,0,2,1:T(8,128)(2,1)S(1)} %dynamic-slice_bitcast_fusion.2), kind=kOutput, calls=%fused_computation.2.clone.1 | convolution fusion | flops 270528512 | bytes 5652480 | tf_op jit(solution)/shard_map/while/body/eval_jaxpr/tkgd,skd->kgts/dot_general | solution.py:136
  178.4 5.3 %select_add_fusion.5 = f32[2,8,256,128]{3,2,1,0:T(8,128)} fusion(f32[2,8,256,128]{3,2,1,0:T(8,128)} %get-tuple-element.300, f32[2,256,256,8]{2,1,3,0:T(8,128)} %get-tuple-element.288, f32[256,256]{0,1:T(8,128)S(1)} %broadcast_multiply_fusion.4, pred[]{:T(512)S(6)} %compare.13, bf16[256,2,2,128]{3,0,2,1:T(8,128)(2,1)} %copy-done.1), kind=kOutput, calls=%fused_computation.4.clone.1 | convolution fusion | flops 271581184 | bytes 8781825 | tf_op jit(solution)/shard_map/while/body/eval_jaxpr/kgts,skd->kgtd/dot_general | solution.py:142
  187.4 4.0 %fusion.113 = (f32[2,8,256]{2,1,0:T(8,128)S(1)}, f32[2,256,256,8]{2,1,3,0:T(8,128)}) fusion(f32[256,256]{0,1:T(8,128)S(1)} %broadcast_multiply_fusion.4, bf16[256,2,8,128]{3,0,2,1:T(8,128)(2,1)} %get-tuple-element.311, bf16[256,2,2,128]{3,0,2,1:T(8,128)(2,1)S(1)} %dynamic-slice_bitcast_fusion.2), kind=kOutput, calls=%fused_computation.2.clone.1 | convolution fusion | flops 270528512 | bytes 5652480 | tf_op jit(solution)/shard_map/while/body/eval_jaxpr/tkgd,skd->kgts/dot_general | solution.py:136
  192.7 5.3 %select_add_fusion.5 = f32[2,8,256,128]{3,2,1,0:T(8,128)} fusion(f32[2,8,256,128]{3,2,1,0:T(8,128)} %get-tuple-element.300, f32[2,256,256,8]{2,1,3,0:T(8,128)} %get-tuple-element.288, f32[256,256]{0,1:T(8,128)S(1)} %broadcast_multiply_fusion.4, pred[]{:T(512)S(6)} %compare.13, bf16[256,2,2,128]{3,0,2,1:T(8,128)(2,1)} %copy-done.1), kind=kOutput, calls=%fused_computation.4.clone.1 | convolution fusion | flops 271581184 | bytes 8781825 | tf_op jit(solution)/shard_map/while/body/eval_jaxpr/kgts,skd->kgtd/dot_general | solution.py:142
  207.0 5.3 %select_add_fusion.5 = f32[2,8,256,128]{3,2,1,0:T(8,128)} fusion(f32[2,8,256,128]{3,2,1,0:T(8,128)} %get-tuple-element.300, f32[2,256,256,8]{2,1,3,0:T(8,128)} %get-tuple-element.288, f32[256,256]{0,1:T(8,128)S(1)} %broadcast_multiply_fusion.4, pred[]{:T(512)S(6)} %compare.13, bf16[256,2,2,128]{3,0,2,1:T(8,128)(2,1)} %copy-done.1), kind=kOutput, calls=%fused_computation.4.clone.1 | convolution fusion | flops 271581184 | bytes 8781825 | tf_op jit(solution)/shard_map/while/body/eval_jaxpr/kgts,skd->kgtd/dot_general | solution.py:142
  216.0 4.0 %fusion.113 = (f32[2,8,256]{2,1,0:T(8,128)S(1)}, f32[2,256,256,8]{2,1,3,0:T(8,128)}) fusion(f32[256,256]{0,1:T(8,128)S(1)} %broadcast_multiply_fusion.4, bf16[256,2,8,128]{3,0,2,1:T(8,128)(2,1)} %get-tuple-element.311, bf16[256,2,2,128]{3,0,2,1:T(8,128)(2,1)S(1)} %dynamic-slice_bitcast_fusion.2), kind=kOutput, calls=%fused_computation.2.clone.1 | convolution fusion | flops 270528512 | bytes 5652480 | tf_op jit(solution)/shard_map/while/body/eval_jaxpr/tkgd,skd->kgts/dot_general | solution.py:136
  221.3 5.3 %select_add_fusion.5 = f32[2,8,256,128]{3,2,1,0:T(8,128)} fusion(f32[2,8,256,128]{3,2,1,0:T(8,128)} %get-tuple-element.300, f32[2,256,256,8]{2,1,3,0:T(8,128)} %get-tuple-element.288, f32[256,256]{0,1:T(8,128)S(1)} %broadcast_multiply_fusion.4, pred[]{:T(512)S(6)} %compare.13, bf16[256,2,2,128]{3,0,2,1:T(8,128)(2,1)} %copy-done.1), kind=kOutput, calls=%fused_computation.4.clone.1 | convolution fusion | flops 271581184 | bytes 8781825 | tf_op jit(solution)/shard_map/while/body/eval_jaxpr/kgts,skd->kgtd/dot_general | solution.py:142
  235.6 5.3 %select_add_fusion.5 = f32[2,8,256,128]{3,2,1,0:T(8,128)} fusion(f32[2,8,256,128]{3,2,1,0:T(8,128)} %get-tuple-element.300, f32[2,256,256,8]{2,1,3,0:T(8,128)} %get-tuple-element.288, f32[256,256]{0,1:T(8,128)S(1)} %broadcast_multiply_fusion.4, pred[]{:T(512)S(6)} %compare.13, bf16[256,2,2,128]{3,0,2,1:T(8,128)(2,1)} %copy-done.1), kind=kOutput, calls=%fused_computation.4.clone.1 | convolution fusion | flops 271581184 | bytes 8781825 | tf_op jit(solution)/shard_map/while/body/eval_jaxpr/kgts,skd->kgtd/dot_general | solution.py:142
  249.9 5.3 %select_add_fusion.5 = f32[2,8,256,128]{3,2,1,0:T(8,128)} fusion(f32[2,8,256,128]{3,2,1,0:T(8,128)} %get-tuple-element.300, f32[2,256,256,8]{2,1,3,0:T(8,128)} %get-tuple-element.288, f32[256,256]{0,1:T(8,128)S(1)} %broadcast_multiply_fusion.4, pred[]{:T(512)S(6)} %compare.13, bf16[256,2,2,128]{3,0,2,1:T(8,128)(2,1)} %copy-done.1), kind=kOutput, calls=%fused_computation.4.clone.1 | convolution fusion | flops 271581184 | bytes 8781825 | tf_op jit(solution)/shard_map/while/body/eval_jaxpr/kgts,skd->kgtd/dot_general | solution.py:142
  264.2 5.3 %select_add_fusion.5 = f32[2,8,256,128]{3,2,1,0:T(8,128)} fusion(f32[2,8,256,128]{3,2,1,0:T(8,128)} %get-tuple-element.300, f32[2,256,256,8]{2,1,3,0:T(8,128)} %get-tuple-element.288, f32[256,256]{0,1:T(8,128)S(1)} %broadcast_multiply_fusion.4, pred[]{:T(512)S(6)} %compare.13, bf16[256,2,2,128]{3,0,2,1:T(8,128)(2,1)} %copy-done.1), kind=kOutput, calls=%fused_computation.4.clone.1 | convolution fusion | flops 271581184 | bytes 8781825 | tf_op jit(solution)/shard_map/while/body/eval_jaxpr/kgts,skd->kgtd/dot_general | solution.py:142
  (138 shorter events, 94.5 us)
Async XLA Ops:
  6.5 49.6 %copy-start = (bf16[1280,1280]{1,0:T(8,128)(2,1)S(1)}, bf16[1280,1280]{1,0:T(8,128)(2,1)}, u32[]{:S(2)}) copy-start(bf16[1280,1280]{1,0:T(8,128)(2,1)} %param.22) | copy-start | bytes 9830404
  6.5 2.8 %copy-start.10 = (f32[1280]{0:T(1024)S(1)}, f32[1280]{0:T(1024)}, u32[]{:S(2)}) copy-start(f32[1280]{0:T(1024)} %param.17) | copy-start | bytes 15364
  6.5 37.9 %reduce-scatter.3.cloned.1.call-start = ((), (), s32[]{:S(2)}) async-start(), calls=%async_computation.2 | async-start | bytes 819200 | tf_op jit(solution)/shard_map/reduce_scatter | solution.py:70
  6.5 2.8 %copy-start.3 = (bf16[1,256,1280]{2,1,0:T(8,128)(2,1)S(1)}, bf16[1,256,1280]{2,1,0:T(8,128)(2,1)}, u32[]{:S(2)}) copy-start(bf16[1,256,1280]{2,1,0:T(8,128)(2,1)} %param.15) | copy-start | bytes 1966084
  19.2 67.4 %reduce-scatter.5.cloned.1.call-start = ((), (), s32[]{:S(2)}) async-start(), calls=%async_computation.3 | async-start | bytes 819200 | tf_op jit(solution)/shard_map/reduce_scatter | solution.py:89
  19.2 27.8 %copy-start.6 = (f32[1280]{0:T(1024)S(1)}, f32[1280]{0:T(1024)}, u32[]{:S(2)}) copy-start(f32[1280]{0:T(1024)} %param.20) | copy-start | bytes 15364
  63.5 84.9 %all-gather.3.cloned.1.call-start = ((), (), s32[]{:S(2)}) async-start(), calls=%async_computation.4 | async-start | bytes 2359296 | tf_op jit(solution)/shard_map/all_gather | solution.py:125
  76.9 9.7 %copy-start.5 = (bf16[64,1280]{1,0:T(8,128)(2,1)S(1)}, bf16[64,1280]{1,0:T(8,128)(2,1)}, u32[]{:S(2)}) copy-start(bf16[64,1280]{1,0:T(8,128)(2,1)} %reduce-scatter.3.cloned.1.call-done) | copy-start | bytes 491524
  86.5 8.7 %copy-start.4 = (bf16[1280,2,2,128]{0,3,2,1:T(8,128)(2,1)S(1)}, bf16[1280,2,2,128]{0,3,2,1:T(8,128)(2,1)}, u32[]{:S(2)}) copy-start(bf16[1280,2,2,128]{0,3,2,1:T(8,128)(2,1)} %copy.21) | copy-start | bytes 3932164
  95.2 0.7 copy-start.8
  95.8 1.0 copy-start.11
  110.1 3.9 %copy-start.9 = (f32[128]{0:T(128)S(1)}, f32[128]{0:T(128)}, u32[]{:S(2)}) copy-start(f32[128]{0:T(128)} %param.25) | copy-start | bytes 1540
  112.4 1.6 copy-start.2
  115.3 2.4 copy-start.7
  160.2 4.0 %copy-start.1 = (bf16[256,2,2,128]{3,0,2,1:T(8,128)(2,1)}, bf16[256,2,2,128]{3,0,2,1:T(8,128)(2,1)S(1)}, u32[]{:S(2)}) copy-start(bf16[256,2,2,128]{3,0,2,1:T(8,128)(2,1)S(1)} %dynamic-slice_bitcast_fusion.2) | copy-start | bytes 786436 | tf_op jit(solution)/shard_map/while
  173.1 4.0 %copy-start.1 = (bf16[256,2,2,128]{3,0,2,1:T(8,128)(2,1)}, bf16[256,2,2,128]{3,0,2,1:T(8,128)(2,1)S(1)}, u32[]{:S(2)}) copy-start(bf16[256,2,2,128]{3,0,2,1:T(8,128)(2,1)S(1)} %dynamic-slice_bitcast_fusion.2) | copy-start | bytes 786436 | tf_op jit(solution)/shard_map/while
  187.4 4.0 %copy-start.1 = (bf16[256,2,2,128]{3,0,2,1:T(8,128)(2,1)}, bf16[256,2,2,128]{3,0,2,1:T(8,128)(2,1)S(1)}, u32[]{:S(2)}) copy-start(bf16[256,2,2,128]{3,0,2,1:T(8,128)(2,1)S(1)} %dynamic-slice_bitcast_fusion.2) | copy-start | bytes 786436 | tf_op jit(solution)/shard_map/while
  201.7 4.0 %copy-start.1 = (bf16[256,2,2,128]{3,0,2,1:T(8,128)(2,1)}, bf16[256,2,2,128]{3,0,2,1:T(8,128)(2,1)S(1)}, u32[]{:S(2)}) copy-start(bf16[256,2,2,128]{3,0,2,1:T(8,128)(2,1)S(1)} %dynamic-slice_bitcast_fusion.2) | copy-start | bytes 786436 | tf_op jit(solution)/shard_map/while
  216.0 4.0 %copy-start.1 = (bf16[256,2,2,128]{3,0,2,1:T(8,128)(2,1)}, bf16[256,2,2,128]{3,0,2,1:T(8,128)(2,1)S(1)}, u32[]{:S(2)}) copy-start(bf16[256,2,2,128]{3,0,2,1:T(8,128)(2,1)S(1)} %dynamic-slice_bitcast_fusion.2) | copy-start | bytes 786436 | tf_op jit(solution)/shard_map/while
  230.3 4.0 %copy-start.1 = (bf16[256,2,2,128]{3,0,2,1:T(8,128)(2,1)}, bf16[256,2,2,128]{3,0,2,1:T(8,128)(2,1)S(1)}, u32[]{:S(2)}) copy-start(bf16[256,2,2,128]{3,0,2,1:T(8,128)(2,1)S(1)} %dynamic-slice_bitcast_fusion.2) | copy-start | bytes 786436 | tf_op jit(solution)/shard_map/while
  244.6 4.0 %copy-start.1 = (bf16[256,2,2,128]{3,0,2,1:T(8,128)(2,1)}, bf16[256,2,2,128]{3,0,2,1:T(8,128)(2,1)S(1)}, u32[]{:S(2)}) copy-start(bf16[256,2,2,128]{3,0,2,1:T(8,128)(2,1)S(1)} %dynamic-slice_bitcast_fusion.2) | copy-start | bytes 786436 | tf_op jit(solution)/shard_map/while
  258.9 4.0 %copy-start.1 = (bf16[256,2,2,128]{3,0,2,1:T(8,128)(2,1)}, bf16[256,2,2,128]{3,0,2,1:T(8,128)(2,1)S(1)}, u32[]{:S(2)}) copy-start(bf16[256,2,2,128]{3,0,2,1:T(8,128)(2,1)S(1)} %dynamic-slice_bitcast_fusion.2) | copy-start | bytes 786436 | tf_op jit(solution)/shard_map/while
Sparse Core Ops, SparseCore 0:
  19.3 25.1 reduce-scatter.2
  63.6 22.8 reduce-scatter.4
  96.9 51.4 all-gather.2
where the time goes:
time: 283 us; the launch traced here: 281 us
  matrix products  89.7 us (32%)
  waiting for transfers between devices  57.6 us (20%)
  local copies, waits for them, and re-layouts  53.6 us (19%)
  other arithmetic  38.1 us (13%)
  blocking collectives  27.4 us (10%)
  between operations  14 us (5%)
    dot_general x8, matrix products, one_image(): jnp.einsum('kgts,skd->kgtd', expo2.astype(jnp.bfloat16), image_kv[:, 1],...  41.5 us
    dot_general x8, matrix products, one_image(): jnp.einsum('tkgd,skd->kgts', queries, image_kv[:, 0], preferred_element_t...  31.9 us
    all_gather x1, waiting for transfers between devices, per_device(): kv_part = lax.all_gather(key_value, 'seq', axis=0, tiled=True)  29.2 us
    reduce_scatter x1, waiting for transfers between devices, per_device(): lax.psum_scatter(jnp.dot(mixed, w_out, preferred_element_type=jnp.float32...  23 us
    unnamed x30, local copies, waits for them, and re-layouts  15.4 us
    unnamed x1, blocking collectives  12 us
    dynamic_slice x8, local copies, waits for them, and re-layouts, one_image(): lax.dynamic_index_in_dim(tiles_part, position, 0, keepdims=False)  10 us
    add x8, other arithmetic, one_image(): return (denom + jnp.sum(expo2, axis=-1), accum)  9.83 us
  transfers between devices with their start and end apart: 3, of which 3 were waited for; matrix products, arithmetic and copies ran while one was open for 11% of the time, Pallas kernels for 0%

commit v1 on v0

v1 whole, which is shorter than its diff:
```python
import functools
import math

import jax
import jax.numpy as jnp
from jax import lax
from jax.experimental import pallas as pl
from jax.experimental.pallas import tpu as pltpu
from jax.sharding import PartitionSpec as P

KVH = 8
HD = 128
TILE_TOK = 64
QB = 128
VHD = 80
DEAD = 1e30
F32 = jnp.float32
BF16 = jnp.bfloat16

NT = (((1,), (1,)), ((), ()))
VM = pl.BlockSpec(memory_space=pltpu.VMEM)
SM = pl.BlockSpec(memory_space=pltpu.SMEM)


def params(mib):
    return pltpu.CompilerParams(vmem_limit_bytes=mib * 1024 * 1024)


def cost(flops, size, transcendentals=0):
    return pl.CostEstimate(flops=flops, bytes_accessed=size, transcendentals=transcendentals)


def layer_norm(values, gain):
    center = values - jnp.mean(values, axis=-1, keepdims=True)
    spread = jnp.mean(center * center, axis=-1, keepdims=True)
    return center / jnp.sqrt(spread + 1e-05) * gain


def rms_norm(values, gain):
    return values / jnp.sqrt(jnp.mean(values * values, axis=-1, keepdims=True) + 1e-05) * gain


def encode_kernel(core_ref, live_ref, x_ref, gain_ref, wqkv_ref, wout_ref, send_ref, keep_ref):
    rows = x_ref.shape[0]
    half = rows // 2
    normed = layer_norm(x_ref[...].astype(F32), gain_ref[...]).astype(BF16)
    q, k, v = [
        lax.dot_general(normed, wqkv_ref[j], NT, preferred_element_type=F32).astype(BF16)
        for j in range(3)
    ]
    width = q.shape[1]
    lane = lax.broadcasted_iota(jnp.int32, (1, width), 1)
    slot = lax.broadcasted_iota(jnp.int32, (1, rows), 1)
    live = jnp.where(slot < live_ref[0] * TILE_TOK, 1.0, 0.0).astype(F32)
    zero = jnp.zeros_like(q)
    mixed = jnp.zeros((rows, width), F32)
    for head in range(width // VHD):
        own = (lane >= head * VHD) & (lane < (head + 1) * VHD)
        scores = lax.dot_general(
            jnp.where(own, q, zero), k, NT, preferred_element_type=F32
        ) / math.sqrt(VHD)
        expo = jnp.exp(scores) * live
        probs = (expo / jnp.sum(expo, axis=-1, keepdims=True)).astype(BF16)
        mixed = mixed + jnp.dot(probs, jnp.where(own, v, zero), preferred_element_type=F32)
    keep_ref[...] = jnp.dot(mixed.astype(BF16), wout_ref[...], preferred_element_type=F32)
    core = core_ref[0]
    send_ref[...] = keep_ref[pl.ds(pl.multiple_of((1 - core) * half, half), half), :].astype(BF16)


def encode(core, live_tiles, x, gain, w_qkv_t, w_out):
    rows, width = x.shape
    own = w_out.shape[0]
    return pl.pallas_call(
        encode_kernel,
        in_specs=[SM, SM, VM, VM, VM, VM],
        out_specs=[VM, VM],
        out_shape=[
            jax.ShapeDtypeStruct((rows // 2, width), BF16),
            jax.ShapeDtypeStruct((rows, width), F32),
        ],
        compiler_params=params(32),
        cost_estimate=cost(2 * rows * width * 4 * own, 8 * width * own, rows * rows * own // VHD),
        name="encode",
    )(core, live_tiles, x, gain, w_qkv_t, w_out)


def mid_kernel(core_ref, x_ref, first_ref, second_ref, gain_ref, resid_ref, normed_ref):
    half = first_ref.shape[0]
    own = pl.ds(pl.multiple_of(core_ref[0] * half, half), half)
    resid = x_ref[own, :].astype(F32) + (first_ref[...].astype(F32) + second_ref[...].astype(F32))
    resid_ref[...] = resid
    normed_ref[...] = layer_norm(resid, gain_ref[...]).astype(BF16)


def mid(core, x, first, second, gain):
    half, width = first.shape
    return pl.pallas_call(
        mid_kernel,
        in_specs=[SM, VM, VM, VM, VM],
        out_specs=[VM, VM],
        out_shape=[
            jax.ShapeDtypeStruct((half, width), F32),
            jax.ShapeDtypeStruct((half, width), BF16),
        ],
        compiler_params=params(16),
        cost_estimate=cost(10 * half * width, 14 * half * width),
        name="mid",
    )(core, x, first, second, gain)


def mlp_kernel(own_ref, other_ref, w1_ref, w2_ref, send_ref, keep_ref):
    half = own_ref.shape[0]
    normed = jnp.concatenate([own_ref[...], other_ref[...]], axis=0)
    hidden = jnp.dot(normed, w1_ref[...], preferred_element_type=F32)
    inner = (0.5 * hidden * (1.0 + lax.erf(hidden * math.sqrt(0.5)))).astype(BF16)
    result = jnp.dot(inner, w2_ref[...], preferred_element_type=F32)
    keep_ref[...] = result[:half]
    send_ref[...] = result[half:].astype(BF16)


def mlp(own, other, w1, w2):
    half, width = own.shape
    return pl.pallas_call(
        mlp_kernel,
        in_specs=[VM, VM, VM, VM],
        out_specs=[VM, VM],
        out_shape=[
            jax.ShapeDtypeStruct((half, width), BF16),
            jax.ShapeDtypeStruct((half, width), F32),
        ],
        compiler_params=params(32),
        cost_estimate=cost(8 * half * w1.size, 4 * w1.size, 2 * half * w1.shape[1]),
        name="mlp",
    )(own, other, w1, w2)


def kv_kernel(
    core_ref, live_ref, resid_ref, first_ref, second_ref, w_ref, gain_ref, own_ref, send_ref, work
):
    half, width = resid_ref.shape
    block = own_ref.shape[1] // 2
    core = core_ref[0]
    vision = (
        resid_ref[...] + (first_ref[...].astype(F32) + second_ref[...].astype(F32))
    ).astype(BF16)
    work[...] = jnp.dot(vision, w_ref[...], preferred_element_type=F32)
    slot = lax.broadcasted_iota(jnp.int32, (half, 1), 0) + core * half
    live = slot < live_ref[0] * TILE_TOK
    gain = gain_ref[...]

    def write(ref, which):
        for head in range(block // HD):
            at = pl.multiple_of(which * block + head * HD, HD)
            keys = rms_norm(work[:, pl.ds(at, HD)], gain)
            ref[:, head * HD : (head + 1) * HD] = keys.astype(BF16)
            values = work[:, pl.ds(2 * block + at, HD)]
            ref[:, block + head * HD : block + (head + 1) * HD] = jnp.where(
                live, values, DEAD
            ).astype(BF16)

    write(send_ref, 1 - core)
    write(own_ref, core)


def project_kv(core, live_tiles, resid, first, second, w_chip, gain):
    half, width = resid.shape
    columns = w_chip.shape[1]
    return pl.pallas_call(
        kv_kernel,
        in_specs=[SM, SM, VM, VM, VM, VM, VM],
        out_specs=[VM, VM],
        out_shape=[jax.ShapeDtypeStruct((half, columns // 2), BF16)] * 2,
        scratch_shapes=[pltpu.VMEM((half, columns), F32)],
        compiler_params=params(24),
        cost_estimate=cost(2 * half * width * columns, 2 * width * columns),
        name="project_kv",
    )(core, live_tiles, resid, first, second, w_chip, gain)


def query_kernel(text_ref, gain_ref, out_ref):
    kv_local, blocks, rows, _ = out_ref.shape
    group = rows // QB
    gain = gain_ref[...]
    for head in range(kv_local):
        for block in range(blocks):
            for member in range(group):
                at = (head * group + member) * HD
                part = text_ref[block * QB : (block + 1) * QB, at : at + HD].astype(F32)
                out_ref[head, block, member * QB : (member + 1) * QB, :] = (
                    rms_norm(part, gain) / math.sqrt(HD)
                ).astype(BF16)


def norm_queries(text, gain, kv_local):
    rows, columns = text.shape
    group = columns // HD // kv_local
    return pl.pallas_call(
        query_kernel,
        in_specs=[VM, VM],
        out_specs=VM,
        out_shape=jax.ShapeDtypeStruct((kv_local, rows // QB, group * QB, HD), BF16),
        compiler_params=params(16),
        cost_estimate=cost(8 * rows * columns, 4 * rows * columns),
        name="norm_queries",
    )(text, gain)


def cross_kernel(slots, mask_ref, order_ref, q_ref, *refs):
    kv_refs, out_ref, acc, vals = refs[:slots], refs[slots], refs[slots + 1], refs[slots + 2]
    kv_local, blocks, rows, _ = q_ref.shape
    group = rows // QB
    images = mask_ref.shape[1]
    keys = kv_refs[0].shape[-2]
    acc[...] = jnp.zeros_like(acc)
    stacked = len(kv_refs) == 1

    def one_image(image, kv):
        for head in range(kv_local):
            values = kv[:, (kv_local + head) * HD : (kv_local + head + 1) * HD]
            live = values < DEAD * 0.5
            vals[:, :HD] = jnp.where(live, values, jnp.zeros_like(values))
            vals[:, HD:] = jnp.where(live, 1.0, 0.0).astype(BF16)
            for block in range(blocks):

                @pl.when(mask_ref[block, order_ref[image]] > 0)
                def _(head=head, block=block):
                    for member in range(group):
                        at = slice(member * QB, (member + 1) * QB)
                        sims = lax.dot_general(
                            q_ref[head, block, at, :],
                            kv[:, head * HD : (head + 1) * HD],
                            NT,
                            preferred_element_type=F32,
                        )
                        expo = jnp.exp(sims).astype(BF16)
                        acc[head, block, at, :] += jnp.dot(
                            expo, vals[...], preferred_element_type=F32
                        )

    if stacked:

        @pl.loop(0, images)
        def _(image):
            one_image(image, kv_refs[0].at[image])
    else:
        for image, kv in enumerate(kv_refs):
            one_image(image, kv)

    for block in range(blocks):
        seen = lax.fori_loop(
            0, images, lambda i, s, block=block: s + mask_ref[block, i], jnp.int32(0)
        )
        for head in range(kv_local):
            for member in range(group):
                at = slice(member * QB, (member + 1) * QB)
                total = acc[head, block, at, :HD]
                denom = acc[head, block, at, HD:]
                column = (head * group + member) * HD
                out_ref[block * QB : (block + 1) * QB, column : column + HD] = jnp.where(
                    seen > 0, total / jnp.where(seen > 0, denom, 1.0), 0.0
                ).astype(BF16)


def cross(mask, order, queries, kv_list):
    kv_local, blocks, rows, _ = queries.shape
    keys = kv_list[0].shape[-2]
    images = mask.shape[1]
    columns = kv_local * (rows // QB) * HD
    work = kv_local * blocks * rows * images * keys
    return pl.pallas_call(
        functools.partial(cross_kernel, len(kv_list)),
        in_specs=[SM, SM, VM] + [VM] * len(kv_list),
        out_specs=VM,
        out_shape=jax.ShapeDtypeStruct((blocks * QB, columns), BF16),
        scratch_shapes=[
            pltpu.VMEM((kv_local, blocks, rows, 2 * HD), F32),
            pltpu.VMEM((keys, 2 * HD), BF16),
        ],
        compiler_params=params(32),
        cost_estimate=cost(4 * work * HD, 4 * queries.size, work),
        name="cross",
    )(mask, order, queries, *kv_list)


def gather_line(block):
    def by(pairs):
        return functools.partial(lax.ppermute, axis_name="seq", perm=pairs)

    swap_x = by([(s, s ^ 1) for s in range(8)])
    swap_z = by([(s, s ^ 2) for s in range(8)])
    middle = by([(s, s ^ 6) for s in (2, 3, 4, 5)])
    outward = by([(2, 0), (3, 1), (4, 6), (5, 7)])
    seq = lax.axis_index("seq")
    z, x = seq // 2, seq % 2
    inside = (z == 1) | (z == 2)
    near = swap_z(block)
    side = swap_x(block)
    over = middle(block)
    near_side = swap_x(near)
    far = jnp.where(inside, over, outward(over))
    over_near = middle(near)
    far_side = swap_x(far)
    last = jnp.where(inside, over_near, outward(over_near))
    last_side = swap_x(last)
    far_z = jnp.where(z < 2, 2, 1)
    last_z = jnp.where(z < 2, 3, 0)
    order = [2 * z + x, 2 * z + 1 - x]
    for at in (z ^ 1, far_z, last_z):
        order += [2 * at + x, 2 * at + 1 - x]
    return [block, side, near, near_side, far, far_side, last, last_side], jnp.stack(order)


def per_device(
    vis_in,
    live_tiles,
    ln1_gain,
    w_qkv,
    w_out,
    ln2_gain,
    w_fc1,
    w_fc2,
    w_kv,
    k_gain,
    q_gain,
    text_queries,
    block_mask,
):
    head_count = lax.axis_size("head")
    head_index = lax.axis_index("head")
    core = head_index % 2
    core_arg = core.astype(jnp.int32).reshape(1)
    kv_local = KVH // head_count
    swap_core = functools.partial(
        lax.ppermute, axis_name="head", perm=[(i, i ^ 1) for i in range(head_count)]
    )

    def swap_chip(value, bit):
        return lax.ppermute(value, "head", [(i, i ^ bit) for i in range(head_count)])

    def sum_chips(value):
        bit = 2
        other = swap_chip(value, bit)
        while 2 * bit < head_count:
            bit *= 2
            value = (value.astype(F32) + other.astype(F32)).astype(BF16)
            other = swap_chip(value, bit)
        return value, other

    x = vis_in.reshape(vis_in.shape[0] * vis_in.shape[1], vis_in.shape[2])
    rows, width = x.shape
    half = rows // 2

    send, partial = encode(
        core_arg, live_tiles, x, ln1_gain.reshape(1, -1), jnp.swapaxes(w_qkv, 1, 2), w_out
    )
    kept = lax.dynamic_slice_in_dim(partial, core * half, half, 0)
    first, second = sum_chips((kept + swap_core(send).astype(F32)).astype(BF16))
    resid, normed = mid(core_arg, x, first, second, ln2_gain.reshape(1, -1))
    send, kept = mlp(normed, swap_core(normed), w_fc1, w_fc2)
    first, second = sum_chips((kept + swap_core(send).astype(F32)).astype(BF16))

    chip_columns = 2 * kv_local * HD
    w_chip = lax.dynamic_slice_in_dim(w_kv, (head_index // 2) * chip_columns, chip_columns, 2)
    w_chip = jnp.concatenate([w_chip[:, 0], w_chip[:, 1]], axis=1)
    own, send = project_kv(
        core_arg, live_tiles, resid, first, second, w_chip, k_gain.reshape(1, -1)
    )
    kv = jnp.concatenate([own, swap_core(send)], axis=0)

    queries = norm_queries(text_queries, q_gain.reshape(1, -1), kv_local)
    if lax.axis_size("seq") == 8:
        kv_list, order = gather_line(kv)
    else:
        kv_list = [lax.all_gather(kv, "seq", axis=0)]
        order = jnp.arange(block_mask.shape[1], dtype=jnp.int32)
    return cross(block_mask, order, queries, kv_list)


def solution(mesh):
    placed = (
        P("seq", None, None),
        P("seq"),
        P(),
        P(None, None, "head"),
        P("head", None),
        P(),
        P(None, "head"),
        P("head", None),
        P(),
        P(),
        P(),
        P("seq", "head"),
        P("seq", None),
    )
    return jax.shard_map(
        per_device, mesh=mesh, in_specs=placed, out_specs=P("seq", "head"), check_vma=False
    )
```

time: 283 us -> 97.2 us (0.34)
  the two profiles are of different devices: /device:TPU:0 before, /device:TPU:18 now
where the time goes in v1:
time: 97.2 us; the launch traced here: 96.3 us
  waiting for transfers between devices  49.3 us (51%)
  Pallas kernels  16.3 us (17%)
  starting transfers between devices  16.2 us (17%)
  local copies, waits for them, and re-layouts  13.2 us (14%)
    ppermute x2, waiting for transfers between devices, swap_chip(): lax.ppermute(value, 'head', [(i, i ^ bit) for i in range(head_count)])  16.3 us
    pallas_call x1, Pallas kernels, cross(): pl.pallas_call(functools.partial(cross_kernel, len(kv_list)), in_specs=[S...  8.88 us
    slice x1, local copies, waits for them, and re-layouts, per_device(): w_chip = jnp.concatenate([w_chip[:, 0], w_chip[:, 1]], axis=1)  7.63 us
    ppermute x1, waiting for transfers between devices, gather_line(): near_side = swap_x(near)  5.62 us
    ppermute x1, waiting for transfers between devices, gather_line(): far_side = swap_x(far)  5.62 us
    ppermute x1, waiting for transfers between devices, gather_line(): over_near = middle(near)  4.93 us
    ppermute x1, waiting for transfers between devices, gather_line(): near = swap_z(block)  4.87 us
    unnamed x23, local copies, waits for them, and re-layouts  3.97 us
  transfers between devices with their start and end apart: 15, of which 13 were waited for; matrix products, arithmetic and copies ran while one was open for 9% of the time, Pallas kernels for 1%

profile of v1, /device:TPU:18, one launch (start us, length us, event | category | flops | bytes accessed | tf_op | source)
XLA Modules:
  0.0 96.3 jit_solution(18395115425485409005)
XLA Ops:
  2.4 1.7 %copy-done.4 = bf16[3,1280,320]{1,2,0:T(8,128)(2,1)S(1)} copy-done((bf16[3,1280,320]{1,2,0:T(8,128)(2,1)S(1)}, bf16[3,1280,320]{1,2,0:T(8,128)(2,1)}, u32[]{:S(2)}) %copy-start.4) | copy-done | bytes 2457624
  5.3 3.2 %encode.1 = (bf16[128,1280]{1,0:T(8,128)(2,1)S(1)}, f32[256,1280]{1,0:T(8,128)S(1)}) custom-call(s32[1]{0:T(128)} %bitcast.9.core_ref, s32[1]{0:T(128)S(6)} %copy.21.live_ref, bf16[256,1280]{1,0:T(8,128)(2,1)S(1)} %bitcast.17, f32[1,1280]{1,0:T(1,128)S(1)} %reshape.21.gain_ref, bf16[3,320,1280]{2,1,0:T(8,128)(2,1)S(1)} %bitcast.19, ...), custom_call_target="tpu_custom_call" | custom-call | flops 838860800 | bytes 3276800 | tf_op jit(solution)/shard_map/encode/pallas_call | solution.py:73
  8.6 1.6 %collective-permute-done = bf16[128,1280]{1,0:T(8,128)(2,1)S(1)} collective-permute-done((bf16[128,1280]{1,0:T(8,128)(2,1)S(1)}, bf16[128,1280]{1,0:T(8,128)(2,1)S(1)}, u32[]{:S(2)}, u32[]{:S(2)}) %collective-permute-start) | collective-permute-done | bytes 327712 | tf_op jit(solution)/shard_map/ppermute | solution.py:357
  10.3 1.6 %collective-permute-start.1 = (bf16[128,1280]{1,0:T(8,128)(2,1)S(1)}, bf16[128,1280]{1,0:T(8,128)(2,1)S(1)}, u32[]{:S(2)}, u32[]{:S(2)}) collective-permute-start(bf16[128,1280]{1,0:T(8,128)(2,1)S(1)} %add_convert_fusion.1.first_ref), channel_id=1, source_target_pairs={{0,2},{1,3},{2,0},{3,1},{4,6},{5,7},{6,4},{7,5},{8,10},{9,11},{10,... | collective-permute-start | bytes 983048 | tf_op jit(solution)/shard_map/ppermute | solution.py:338
  11.9 8.2 %collective-permute-done.1.second_ref = bf16[128,1280]{1,0:T(8,128)(2,1)S(1)} collective-permute-done((bf16[128,1280]{1,0:T(8,128)(2,1)S(1)}, bf16[128,1280]{1,0:T(8,128)(2,1)S(1)}, u32[]{:S(2)}, u32[]{:S(2)}) %collective-permute-start.1) | collective-permute-done | bytes 327712 | tf_op jit(solution)/shard_map/ppermute | solution.py:338
  20.6 7.6 %constant_dynamic-slice_fusion = (bf16[1280,1,512]{2,1,0:T(2,128)(2,1)S(1)}, bf16[1280,1,512]{2,1,0:T(2,128)(2,1)S(1)}) fusion(bf16[1280,2,1024]{2,1,0:T(2,128)(2,1)} %param.21, s32[]{:T(128)S(6)} %select_n.50, s32[]{:T(128)S(6)} %add.59), kind=kLoop, calls=%fused_computation.9 | loop fusion | bytes 5242888 | tf_op jit(solution)/shard_map/slice | solution.py:364
  28.2 2.0 %mlp.1 = (bf16[128,1280]{1,0:T(8,128)(2,1)S(1)}, f32[128,1280]{1,0:T(8,128)S(1)}) custom-call(bf16[128,1280]{1,0:T(8,128)(2,1)S(1)} %get-tuple-element.16.own_ref, bf16[128,1280]{1,0:T(8,128)(2,1)S(1)} %collective-permute-done.2.other_ref, bf16[1280,1280]{1,0:T(8,128)(2,1)S(1)} %copy-done, bf16[1280,1280]{1,0:T(8,128)(2,1)S(1)} %copy-done.1), custom_call_target="tpu_custom_call" | custom-call | flops 1677721600 | bytes 6553600 | tf_op jit(solution)/shard_map/mlp/pallas_call | solution.py:123
  32.5 1.6 %collective-permute-start.4 = (bf16[128,1280]{1,0:T(8,128)(2,1)S(1)}, bf16[128,1280]{1,0:T(8,128)(2,1)S(1)}, u32[]{:S(2)}, u32[]{:S(2)}) collective-permute-start(bf16[128,1280]{1,0:T(8,128)(2,1)S(1)} %add_convert_fusion.first_ref), channel_id=1, source_target_pairs={{0,2},{1,3},{2,0},{3,1},{4,6},{5,7},{6,4},{7,5},{8,10},{9,11},{10,... | collective-permute-start | bytes 983048 | tf_op jit(solution)/shard_map/ppermute | solution.py:338
  34.5 8.1 %collective-permute-done.4.second_ref = bf16[128,1280]{1,0:T(8,128)(2,1)S(1)} collective-permute-done((bf16[128,1280]{1,0:T(8,128)(2,1)S(1)}, bf16[128,1280]{1,0:T(8,128)(2,1)S(1)}, u32[]{:S(2)}, u32[]{:S(2)}) %collective-permute-start.4) | collective-permute-done | bytes 327712 | tf_op jit(solution)/shard_map/ppermute | solution.py:338
  43.4 1.3 %collective-permute-done.5 = bf16[128,512]{1,0:T(8,128)(2,1)S(1)} collective-permute-done((bf16[128,512]{1,0:T(8,128)(2,1)S(1)}, bf16[128,512]{1,0:T(8,128)(2,1)S(1)}, u32[]{:S(2)}, u32[]{:S(2)}) %collective-permute-start.5) | collective-permute-done | bytes 131104 | tf_op jit(solution)/shard_map/ppermute | solution.py:368
  44.8 1.6 %collective-permute-start.7 = (bf16[256,512]{1,0:T(8,128)(2,1)S(1)}, bf16[256,512]{1,0:T(8,128)(2,1)S(1)}, u32[]{:S(2)}, u32[]{:S(2)}) collective-permute-start(bf16[256,512]{1,0:T(8,128)(2,1)S(1)} %constant_dynamic-update-slice_fusion.refs_0_), channel_id=1, source_target_pairs={{0,8},{4,12},{8,0},{12,4},{16,24},{20,28},{24,16},{28,20},{1,9},{5... | collective-permute-start | bytes 786440 | tf_op jit(solution)/shard_map/ppermute | solution.py:296
  46.4 1.9 %collective-permute-start.9 = (bf16[256,512]{1,0:T(8,128)(2,1)S(1)}, bf16[256,512]{1,0:T(8,128)(2,1)S(1)}, u32[]{:S(2)}, u32[]{:S(2)}) collective-permute-start(bf16[256,512]{1,0:T(8,128)(2,1)S(1)} %constant_dynamic-update-slice_fusion.refs_0_), channel_id=1, source_target_pairs={{8,16},{12,20},{16,8},{20,12},{9,17},{13,21},{17,9},{21,13},{10,18... | collective-permute-start | bytes 786440 | tf_op jit(solution)/shard_map/ppermute | solution.py:298
  48.3 4.9 %collective-permute-done.7.refs_2_ = bf16[256,512]{1,0:T(8,128)(2,1)S(1)} collective-permute-done((bf16[256,512]{1,0:T(8,128)(2,1)S(1)}, bf16[256,512]{1,0:T(8,128)(2,1)S(1)}, u32[]{:S(2)}, u32[]{:S(2)}) %collective-permute-start.7) | collective-permute-done | bytes 262176 | tf_op jit(solution)/shard_map/ppermute | solution.py:296
  53.2 2.3 %collective-permute-start.12 = (bf16[256,512]{1,0:T(8,128)(2,1)S(1)}, bf16[256,512]{1,0:T(8,128)(2,1)S(1)}, u32[]{:S(2)}, u32[]{:S(2)}) collective-permute-start(bf16[256,512]{1,0:T(8,128)(2,1)S(1)} %collective-permute-done.7.refs_2_), channel_id=1, source_target_pairs={{8,16},{12,20},{16,8},{20,12},{9,17},{13,21},{17,9},{21,13},{10,18... | collective-permute-start | bytes 786440 | tf_op jit(solution)/shard_map/ppermute | solution.py:301
  56.4 1.3 %collective-permute-start.10 = (bf16[256,512]{1,0:T(8,128)(2,1)S(1)}, bf16[256,512]{1,0:T(8,128)(2,1)S(1)}, u32[]{:S(2)}, u32[]{:S(2)}) collective-permute-start(bf16[256,512]{1,0:T(8,128)(2,1)S(1)} %collective-permute-done.9), channel_id=1, source_target_pairs={{8,0},{12,4},{16,24},{20,28},{9,1},{13,5},{17,25},{21,29},{10,2},{... | collective-permute-start | bytes 786440 | tf_op jit(solution)/shard_map/ppermute | solution.py:300
  57.7 4.9 %collective-permute-done.12 = bf16[256,512]{1,0:T(8,128)(2,1)S(1)} collective-permute-done((bf16[256,512]{1,0:T(8,128)(2,1)S(1)}, bf16[256,512]{1,0:T(8,128)(2,1)S(1)}, u32[]{:S(2)}, u32[]{:S(2)}) %collective-permute-start.12) | collective-permute-done | bytes 262176 | tf_op jit(solution)/shard_map/ppermute | solution.py:301
  62.6 1.3 %collective-permute-start.13 = (bf16[256,512]{1,0:T(8,128)(2,1)S(1)}, bf16[256,512]{1,0:T(8,128)(2,1)S(1)}, u32[]{:S(2)}, u32[]{:S(2)}) collective-permute-start(bf16[256,512]{1,0:T(8,128)(2,1)S(1)} %collective-permute-done.12), channel_id=1, source_target_pairs={{8,0},{12,4},{16,24},{20,28},{9,1},{13,5},{17,25},{21,29},{10,2},{... | collective-permute-start | bytes 786440 | tf_op jit(solution)/shard_map/ppermute | solution.py:303
  64.5 1.5 %collective-permute-start.8 = (bf16[256,512]{1,0:T(8,128)(2,1)S(1)}, bf16[256,512]{1,0:T(8,128)(2,1)S(1)}, u32[]{:S(2)}, u32[]{:S(2)}) collective-permute-start(bf16[256,512]{1,0:T(8,128)(2,1)S(1)} %collective-permute-done.7.refs_2_), channel_id=1, source_target_pairs={{0,4},{4,0},{8,12},{12,8},{16,20},{20,16},{24,28},{28,24},{1,5},{5... | collective-permute-start | bytes 786440 | tf_op jit(solution)/shard_map/ppermute | solution.py:299
  66.7 1.6 %collective-permute-done.13 = bf16[256,512]{1,0:T(8,128)(2,1)S(1)} collective-permute-done((bf16[256,512]{1,0:T(8,128)(2,1)S(1)}, bf16[256,512]{1,0:T(8,128)(2,1)S(1)}, u32[]{:S(2)}, u32[]{:S(2)}) %collective-permute-start.13) | collective-permute-done | bytes 262176 | tf_op jit(solution)/shard_map/ppermute | solution.py:303
  70.1 3.1 %collective-permute-done.6.refs_1_ = bf16[256,512]{1,0:T(8,128)(2,1)S(1)} collective-permute-done((bf16[256,512]{1,0:T(8,128)(2,1)S(1)}, bf16[256,512]{1,0:T(8,128)(2,1)S(1)}, u32[]{:S(2)}, u32[]{:S(2)}) %collective-permute-start.6) | collective-permute-done | bytes 262176 | tf_op jit(solution)/shard_map/ppermute | solution.py:297
  73.2 5.6 %collective-permute-done.8.refs_3_ = bf16[256,512]{1,0:T(8,128)(2,1)S(1)} collective-permute-done((bf16[256,512]{1,0:T(8,128)(2,1)S(1)}, bf16[256,512]{1,0:T(8,128)(2,1)S(1)}, u32[]{:S(2)}, u32[]{:S(2)}) %collective-permute-start.8) | collective-permute-done | bytes 262176 | tf_op jit(solution)/shard_map/ppermute | solution.py:299
  78.9 5.6 %collective-permute-done.11.refs_5_ = bf16[256,512]{1,0:T(8,128)(2,1)S(1)} collective-permute-done((bf16[256,512]{1,0:T(8,128)(2,1)S(1)}, bf16[256,512]{1,0:T(8,128)(2,1)S(1)}, u32[]{:S(2)}, u32[]{:S(2)}) %collective-permute-start.11) | collective-permute-done | bytes 262176 | tf_op jit(solution)/shard_map/ppermute | solution.py:302
  84.5 3.0 %collective-permute-done.14.refs_7_ = bf16[256,512]{1,0:T(8,128)(2,1)S(1)} collective-permute-done((bf16[256,512]{1,0:T(8,128)(2,1)S(1)}, bf16[256,512]{1,0:T(8,128)(2,1)S(1)}, u32[]{:S(2)}, u32[]{:S(2)}) %collective-permute-start.14) | collective-permute-done | bytes 262176 | tf_op jit(solution)/shard_map/ppermute | solution.py:304
  87.5 8.9 %cross.1 = bf16[256,2048]{1,0:T(8,128)(2,1)} custom-call(s32[2,8]{1,0:T(2,128)S(1)} %copy-done.9, s32[8]{0:T(128)S(1)} %stack.35.order_ref, bf16[2,2,1024,128]{3,2,1,0:T(8,128)(2,1)S(1)} %norm_queries.1.q_ref, bf16[256,512]{1,0:T(8,128)(2,1)S(1)} %constant_dynamic-update-slice_fusion.refs_0_, bf16[256,512]{1,0:T(8,128)(2,1)S(1)} %collective-permute-done.6.refs_1_, ...), custom_call_target="tpu_custom_call" | custom-call | flops 4294967296 | bytes 2097152 | tf_op jit(solution)/shard_map/cross/pallas_call | solution.py:270
  (46 shorter events, 10.9 us)
Async XLA Ops:
  2.4 1.7 %copy-start.4 = (bf16[3,1280,320]{1,2,0:T(8,128)(2,1)S(1)}, bf16[3,1280,320]{1,2,0:T(8,128)(2,1)}, u32[]{:S(2)}) copy-start(bf16[3,1280,320]{1,2,0:T(8,128)(2,1)} %param.16) | copy-start | bytes 7372804
  5.3 6.6 %copy-start.10 = (f32[1280]{0:T(1024)S(1)}, f32[1280]{0:T(1024)}, u32[]{:S(2)}) copy-start(f32[1280]{0:T(1024)} %param.18) | copy-start | bytes 15364
  5.3 14.8 %copy-start.3 = (bf16[1,256,1280]{2,1,0:T(8,128)(2,1)S(1)}, bf16[1,256,1280]{2,1,0:T(8,128)(2,1)}, u32[]{:S(2)}) copy-start(bf16[1,256,1280]{2,1,0:T(8,128)(2,1)} %param.13) | copy-start | bytes 1966084
  8.5 1.7 %collective-permute-start = (bf16[128,1280]{1,0:T(8,128)(2,1)S(1)}, bf16[128,1280]{1,0:T(8,128)(2,1)S(1)}, u32[]{:S(2)}, u32[]{:S(2)}) collective-permute-start(bf16[128,1280]{1,0:T(8,128)(2,1)S(1)} %get-tuple-element.14), channel_id=1, source_target_pairs={{0,1},{1,0},{2,3},{3,2},{4,5},{5,4},{6,7},{7,6},{8,9},{9,8},{10,11... | collective-permute-start | bytes 983048 | tf_op jit(solution)/shard_map/ppermute | solution.py:357
  10.3 9.8 %collective-permute-start.1 = (bf16[128,1280]{1,0:T(8,128)(2,1)S(1)}, bf16[128,1280]{1,0:T(8,128)(2,1)S(1)}, u32[]{:S(2)}, u32[]{:S(2)}) collective-permute-start(bf16[128,1280]{1,0:T(8,128)(2,1)S(1)} %add_convert_fusion.1.first_ref), channel_id=1, source_target_pairs={{0,2},{1,3},{2,0},{3,1},{4,6},{5,7},{6,4},{7,5},{8,10},{9,11},{10,... | collective-permute-start | bytes 983048 | tf_op jit(solution)/shard_map/ppermute | solution.py:338
  20.4 7.8 %copy-start = (bf16[1280,1280]{1,0:T(8,128)(2,1)S(1)}, bf16[1280,1280]{1,0:T(8,128)(2,1)}, u32[]{:S(2)}) copy-start(bf16[1280,1280]{1,0:T(8,128)(2,1)} %w1_ref.1) | copy-start | bytes 9830404
  20.5 7.8 %copy-start.1 = (bf16[1280,1280]{1,0:T(8,128)(2,1)S(1)}, bf16[1280,1280]{1,0:T(8,128)(2,1)}, u32[]{:S(2)}) copy-start(bf16[1280,1280]{1,0:T(8,128)(2,1)} %w2_ref.1) | copy-start | bytes 9830404
  20.5 7.7 %collective-permute-start.2 = (bf16[128,1280]{1,0:T(8,128)(2,1)S(1)}, bf16[128,1280]{1,0:T(8,128)(2,1)S(1)}, u32[]{:S(2)}, u32[]{:S(2)}) collective-permute-start(bf16[128,1280]{1,0:T(8,128)(2,1)S(1)} %get-tuple-element.16.own_ref), channel_id=1, source_target_pairs={{0,1},{1,0},{2,3},{3,2},{4,5},{5,4},{6,7},{7,6},{8,9},{9,8},{10,11... | collective-permute-start | bytes 983048 | tf_op jit(solution)/shard_map/ppermute | solution.py:359
  30.2 2.2 %collective-permute-start.3 = (bf16[128,1280]{1,0:T(8,128)(2,1)S(1)}, bf16[128,1280]{1,0:T(8,128)(2,1)S(1)}, u32[]{:S(2)}, u32[]{:S(2)}) collective-permute-start(bf16[128,1280]{1,0:T(8,128)(2,1)S(1)} %get-tuple-element.18), channel_id=1, source_target_pairs={{0,1},{1,0},{2,3},{3,2},{4,5},{5,4},{6,7},{7,6},{8,9},{9,8},{10,11... | collective-permute-start | bytes 983048 | tf_op jit(solution)/shard_map/ppermute | solution.py:360
  32.5 10.1 %collective-permute-start.4 = (bf16[128,1280]{1,0:T(8,128)(2,1)S(1)}, bf16[128,1280]{1,0:T(8,128)(2,1)S(1)}, u32[]{:S(2)}, u32[]{:S(2)}) collective-permute-start(bf16[128,1280]{1,0:T(8,128)(2,1)S(1)} %add_convert_fusion.first_ref), channel_id=1, source_target_pairs={{0,2},{1,3},{2,0},{3,1},{4,6},{5,7},{6,4},{7,5},{8,10},{9,11},{10,... | collective-permute-start | bytes 983048 | tf_op jit(solution)/shard_map/ppermute | solution.py:338
  34.1 8.5 %copy-start.7 = (f32[128]{0:T(128)S(1)}, f32[128]{0:T(128)}, u32[]{:S(2)}) copy-start(f32[128]{0:T(128)} %param.22) | copy-start | bytes 1540
  42.6 26.4 %copy-start.5 = (bf16[256,2048]{1,0:T(8,128)(2,1)S(1)}, bf16[256,2048]{1,0:T(8,128)(2,1)}, u32[]{:S(2)}) copy-start(bf16[256,2048]{1,0:T(8,128)(2,1)} %text_ref.1) | copy-start | bytes 3145732
  42.6 26.4 %copy-start.8 = (f32[128]{0:T(128)S(1)}, f32[128]{0:T(128)}, u32[]{:S(2)}) copy-start(f32[128]{0:T(128)} %param.23) | copy-start | bytes 1540
  43.3 44.1 %copy-start.9 = (s32[2,8]{1,0:T(2,128)S(1)}, s32[2,8]{1,0:T(2,128)}, u32[]{:S(2)}) copy-start(s32[2,8]{1,0:T(2,128)} %mask_ref.1) | copy-start | bytes 196
  43.3 1.4 %collective-permute-start.5 = (bf16[128,512]{1,0:T(8,128)(2,1)S(1)}, bf16[128,512]{1,0:T(8,128)(2,1)S(1)}, u32[]{:S(2)}, u32[]{:S(2)}) collective-permute-start(bf16[128,512]{1,0:T(8,128)(2,1)S(1)} %get-tuple-element.20), channel_id=1, source_target_pairs={{0,1},{1,0},{2,3},{3,2},{4,5},{5,4},{6,7},{7,6},{8,9},{9,8},{10,11... | collective-permute-start | bytes 393224 | tf_op jit(solution)/shard_map/ppermute | solution.py:368
  44.8 8.4 %collective-permute-start.7 = (bf16[256,512]{1,0:T(8,128)(2,1)S(1)}, bf16[256,512]{1,0:T(8,128)(2,1)S(1)}, u32[]{:S(2)}, u32[]{:S(2)}) collective-permute-start(bf16[256,512]{1,0:T(8,128)(2,1)S(1)} %constant_dynamic-update-slice_fusion.refs_0_), channel_id=1, source_target_pairs={{0,8},{4,12},{8,0},{12,4},{16,24},{20,28},{24,16},{28,20},{1,9},{5... | collective-permute-start | bytes 786440 | tf_op jit(solution)/shard_map/ppermute | solution.py:296
  46.4 10.0 %collective-permute-start.9 = (bf16[256,512]{1,0:T(8,128)(2,1)S(1)}, bf16[256,512]{1,0:T(8,128)(2,1)S(1)}, u32[]{:S(2)}, u32[]{:S(2)}) collective-permute-start(bf16[256,512]{1,0:T(8,128)(2,1)S(1)} %constant_dynamic-update-slice_fusion.refs_0_), channel_id=1, source_target_pairs={{8,16},{12,20},{16,8},{20,12},{9,17},{13,21},{17,9},{21,13},{10,18... | collective-permute-start | bytes 786440 | tf_op jit(solution)/shard_map/ppermute | solution.py:298
  53.2 9.4 %collective-permute-start.12 = (bf16[256,512]{1,0:T(8,128)(2,1)S(1)}, bf16[256,512]{1,0:T(8,128)(2,1)S(1)}, u32[]{:S(2)}, u32[]{:S(2)}) collective-permute-start(bf16[256,512]{1,0:T(8,128)(2,1)S(1)} %collective-permute-done.7.refs_2_), channel_id=1, source_target_pairs={{8,16},{12,20},{16,8},{20,12},{9,17},{13,21},{17,9},{21,13},{10,18... | collective-permute-start | bytes 786440 | tf_op jit(solution)/shard_map/ppermute | solution.py:301
  56.4 9.7 %collective-permute-start.10 = (bf16[256,512]{1,0:T(8,128)(2,1)S(1)}, bf16[256,512]{1,0:T(8,128)(2,1)S(1)}, u32[]{:S(2)}, u32[]{:S(2)}) collective-permute-start(bf16[256,512]{1,0:T(8,128)(2,1)S(1)} %collective-permute-done.9), channel_id=1, source_target_pairs={{8,0},{12,4},{16,24},{20,28},{9,1},{13,5},{17,25},{21,29},{10,2},{... | collective-permute-start | bytes 786440 | tf_op jit(solution)/shard_map/ppermute | solution.py:300
  62.6 5.7 %collective-permute-start.13 = (bf16[256,512]{1,0:T(8,128)(2,1)S(1)}, bf16[256,512]{1,0:T(8,128)(2,1)S(1)}, u32[]{:S(2)}, u32[]{:S(2)}) collective-permute-start(bf16[256,512]{1,0:T(8,128)(2,1)S(1)} %collective-permute-done.12), channel_id=1, source_target_pairs={{8,0},{12,4},{16,24},{20,28},{9,1},{13,5},{17,25},{21,29},{10,2},{... | collective-permute-start | bytes 786440 | tf_op jit(solution)/shard_map/ppermute | solution.py:303
  63.9 9.3 %collective-permute-start.6 = (bf16[256,512]{1,0:T(8,128)(2,1)S(1)}, bf16[256,512]{1,0:T(8,128)(2,1)S(1)}, u32[]{:S(2)}, u32[]{:S(2)}) collective-permute-start(bf16[256,512]{1,0:T(8,128)(2,1)S(1)} %constant_dynamic-update-slice_fusion.refs_0_), channel_id=1, source_target_pairs={{0,4},{4,0},{8,12},{12,8},{16,20},{20,16},{24,28},{28,24},{1,5},{5... | collective-permute-start | bytes 786440 | tf_op jit(solution)/shard_map/ppermute | solution.py:297
  64.5 14.3 %collective-permute-start.8 = (bf16[256,512]{1,0:T(8,128)(2,1)S(1)}, bf16[256,512]{1,0:T(8,128)(2,1)S(1)}, u32[]{:S(2)}, u32[]{:S(2)}) collective-permute-start(bf16[256,512]{1,0:T(8,128)(2,1)S(1)} %collective-permute-done.7.refs_2_), channel_id=1, source_target_pairs={{0,4},{4,0},{8,12},{12,8},{16,20},{20,16},{24,28},{28,24},{1,5},{5... | collective-permute-start | bytes 786440 | tf_op jit(solution)/shard_map/ppermute | solution.py:299
  66.1 18.4 %collective-permute-start.11 = (bf16[256,512]{1,0:T(8,128)(2,1)S(1)}, bf16[256,512]{1,0:T(8,128)(2,1)S(1)}, u32[]{:S(2)}, u32[]{:S(2)}) collective-permute-start(bf16[256,512]{1,0:T(8,128)(2,1)S(1)} %broadcast_select_fusion.1.refs_4_), channel_id=1, source_target_pairs={{0,4},{4,0},{8,12},{12,8},{16,20},{20,16},{24,28},{28,24},{1,5},{5... | collective-permute-start | bytes 786440 | tf_op jit(solution)/shard_map/ppermute | solution.py:302
  68.3 19.1 %collective-permute-start.14 = (bf16[256,512]{1,0:T(8,128)(2,1)S(1)}, bf16[256,512]{1,0:T(8,128)(2,1)S(1)}, u32[]{:S(2)}, u32[]{:S(2)}) collective-permute-start(bf16[256,512]{1,0:T(8,128)(2,1)S(1)} %broadcast_select_fusion.refs_6_), channel_id=1, source_target_pairs={{0,4},{4,0},{8,12},{12,8},{16,20},{20,16},{24,28},{28,24},{1,5},{5... | collective-permute-start | bytes 786440 | tf_op jit(solution)/shard_map/ppermute | solution.py:304
  (2 other events, 2.2 us)

commit v2 on v1

v2 whole, which is shorter than its diff:
```python
import functools
import math

import jax
import jax.numpy as jnp
from jax import lax
from jax.experimental import pallas as pl
from jax.experimental.pallas import tpu as pltpu
from jax.sharding import PartitionSpec as P

KVH = 8
HD = 128
TILE_TOK = 64
QB = 128
VHD = 80
KI = 256
DEAD = 1e30
FIRST = 64
PARTS = [[0], [2, 1], [4, 3], [5, 6], [7]]
F32 = jnp.float32
BF16 = jnp.bfloat16

NT = (((1,), (1,)), ((), ()))
VM = pl.BlockSpec(memory_space=pltpu.VMEM)
SM = pl.BlockSpec(memory_space=pltpu.SMEM)
HB = pl.BlockSpec(memory_space=pltpu.HBM)
AN = pl.BlockSpec(memory_space=pl.ANY)


def params(mib):
    return pltpu.CompilerParams(vmem_limit_bytes=mib * 1024 * 1024)


def in_hbm(value):
    return pltpu.with_memory_space_constraint(value, pltpu.HBM)


def cost(flops, size, transcendentals=0):
    return pl.CostEstimate(flops=flops, bytes_accessed=size, transcendentals=transcendentals)


def layer_norm(values, gain):
    center = values - jnp.mean(values, axis=-1, keepdims=True)
    spread = jnp.mean(center * center, axis=-1, keepdims=True)
    return center / jnp.sqrt(spread + 1e-05) * gain


def rms_norm(values, gain):
    return values / jnp.sqrt(jnp.mean(values * values, axis=-1, keepdims=True) + 1e-05) * gain


def encode_kernel(
    core_ref,
    live_ref,
    gain_hbm,
    x_hbm,
    wqkv_hbm,
    wout_hbm,
    send_ref,
    keep_ref,
    own_ref,
    gain_ref,
    x_ref,
    wqkv_ref,
    wout_ref,
    mixed_ref,
    sems,
):
    loads = [pltpu.make_async_copy(x_hbm, x_ref, sems.at[0])]
    loads += [
        pltpu.make_async_copy(wqkv_hbm.at[j], wqkv_ref.at[j], sems.at[1 + j]) for j in range(3)
    ]
    loads.append(pltpu.make_async_copy(wout_hbm, wout_ref, sems.at[4]))
    loads.append(pltpu.make_async_copy(gain_hbm, gain_ref, sems.at[5]))
    for load in loads:
        load.start()
    rows, width = mixed_ref.shape
    half = rows // 2
    core = core_ref[0]
    own_rows = pl.ds(pl.multiple_of(core * half, half), half)
    other_rows = pl.ds(pl.multiple_of((1 - core) * half, half), half)

    loads[0].wait()
    loads[5].wait()
    own_ref[...] = x_ref[own_rows, :]
    normed = layer_norm(x_ref[...].astype(F32), gain_ref[...].reshape(1, -1)).astype(BF16)
    qkv = []
    for j in range(3):
        loads[1 + j].wait()
        qkv.append(
            lax.dot_general(normed, wqkv_ref[j], NT, preferred_element_type=F32).astype(BF16)
        )
    q, k, v = qkv
    lane = lax.broadcasted_iota(jnp.int32, (1, width), 1)
    slot = lax.broadcasted_iota(jnp.int32, (1, rows), 1)
    live = jnp.where(slot < live_ref[0] * TILE_TOK, 1.0, 0.0).astype(F32)
    zero = jnp.zeros_like(q)
    mixed = jnp.zeros((rows, width), F32)
    for head in range(width // VHD):
        own = (lane >= head * VHD) & (lane < (head + 1) * VHD)
        scores = lax.dot_general(
            jnp.where(own, q, zero), k, NT, preferred_element_type=F32
        ) / math.sqrt(VHD)
        expo = jnp.exp(scores) * live
        probs = (expo / jnp.sum(expo, axis=-1, keepdims=True)).astype(BF16)
        mixed = mixed + jnp.dot(probs, jnp.where(own, v, zero), preferred_element_type=F32)
    mixed_ref[...] = mixed.astype(BF16)
    loads[4].wait()
    send_ref[...] = jnp.dot(
        mixed_ref[other_rows, :], wout_ref[...], preferred_element_type=F32
    ).astype(BF16)
    keep_ref[...] = jnp.dot(mixed_ref[own_rows, :], wout_ref[...], preferred_element_type=F32)


def encode(core, live_tiles, x, gain, w_qkv_t, w_out):
    rows, width = x.shape
    own = w_out.shape[0]
    return pl.pallas_call(
        encode_kernel,
        in_specs=[SM, SM, HB, HB, HB, HB],
        out_specs=[VM, VM, VM],
        out_shape=[
            jax.ShapeDtypeStruct((rows // 2, width), BF16),
            jax.ShapeDtypeStruct((rows // 2, width), F32),
            jax.ShapeDtypeStruct((rows // 2, width), BF16),
        ],
        scratch_shapes=[
            pltpu.VMEM(gain.shape, F32),
            pltpu.VMEM(x.shape, BF16),
            pltpu.VMEM(w_qkv_t.shape, BF16),
            pltpu.VMEM(w_out.shape, BF16),
            pltpu.VMEM((rows, own), BF16),
            pltpu.SemaphoreType.DMA((6,)),
        ],
        compiler_params=params(12),
        cost_estimate=cost(2 * rows * width * 4 * own, 8 * width * own, rows * rows * own // VHD),
        name="encode",
    )(core, live_tiles, in_hbm(gain), in_hbm(x), in_hbm(w_qkv_t), in_hbm(w_out))


def mid_kernel(x_ref, first_ref, second_ref, gain_ref, _, resid_ref, normed_ref):
    resid = x_ref[...].astype(F32) + (first_ref[...].astype(F32) + second_ref[...].astype(F32))
    resid_ref[...] = resid
    normed_ref[...] = layer_norm(resid, gain_ref[...].reshape(1, -1)).astype(BF16)


def mid(x, first, second, gain, after):
    half, width = first.shape
    return pl.pallas_call(
        mid_kernel,
        in_specs=[VM, VM, VM, VM, AN],
        out_specs=[VM, VM],
        out_shape=[
            jax.ShapeDtypeStruct((half, width), F32),
            jax.ShapeDtypeStruct((half, width), BF16),
        ],
        compiler_params=params(8),
        cost_estimate=cost(10 * half * width, 14 * half * width),
        name="mid",
    )(x, first, second, gain, after)


def fetch_kernel(chip_ref, w1_hbm, w2_hbm, wkv_hbm, _, w1_ref, w2_ref, wkv_ref, sems):
    columns = wkv_ref.shape[2]
    mine = pl.ds(pl.multiple_of(chip_ref[0] * columns, HD), columns)
    loads = [
        pltpu.make_async_copy(w1_hbm, w1_ref, sems.at[0]),
        pltpu.make_async_copy(w2_hbm, w2_ref, sems.at[1]),
        pltpu.make_async_copy(wkv_hbm.at[:, :, mine], wkv_ref, sems.at[2]),
    ]
    for load in loads:
        load.start()
    for load in loads:
        load.wait()


def fetch(chip, w1, w2, w_kv, columns, after):
    shapes = [w1.shape, w2.shape, (w_kv.shape[0], w_kv.shape[1], columns)]
    return pl.pallas_call(
        fetch_kernel,
        in_specs=[SM, HB, HB, HB, AN],
        out_specs=[VM, VM, VM],
        out_shape=[jax.ShapeDtypeStruct(shape, BF16) for shape in shapes],
        scratch_shapes=[pltpu.SemaphoreType.DMA((3,))],
        compiler_params=params(16),
        cost_estimate=cost(0, 20 * w1.size),
        name="fetch",
    )(chip, in_hbm(w1), in_hbm(w2), in_hbm(w_kv), after)


def mlp_kernel(own_ref, other_ref, w1_ref, w2_ref, send_ref, keep_ref):
    half = own_ref.shape[0]
    normed = jnp.concatenate([own_ref[...], other_ref[...]], axis=0)
    hidden = jnp.dot(normed, w1_ref[...], preferred_element_type=F32)
    inner = (0.5 * hidden * (1.0 + lax.erf(hidden * math.sqrt(0.5)))).astype(BF16)
    result = jnp.dot(inner, w2_ref[...], preferred_element_type=F32)
    keep_ref[...] = result[:half]
    send_ref[...] = result[half:].astype(BF16)


def mlp(own, other, w1, w2):
    half, width = own.shape
    return pl.pallas_call(
        mlp_kernel,
        in_specs=[VM, VM, VM, VM],
        out_specs=[VM, VM],
        out_shape=[
            jax.ShapeDtypeStruct((half, width), BF16),
            jax.ShapeDtypeStruct((half, width), F32),
        ],
        compiler_params=params(14),
        cost_estimate=cost(8 * half * w1.size, 4 * w1.size, 2 * half * w1.shape[1]),
        name="mlp",
    )(own, other, w1, w2)


def kv_kernel(start, core_ref, live_ref, keys_ref, gain_ref, _, own_ref, send_ref):
    half = keys_ref.shape[1]
    block = own_ref.shape[1] // 2
    core = core_ref[0]
    slot = lax.broadcasted_iota(jnp.int32, (half, 1), 0) + core * (KI // 2) + start
    live = slot < live_ref[0] * TILE_TOK
    gain = gain_ref[...].reshape(1, -1)

    def write(ref, which):
        for head in range(block // HD):
            at = pl.ds(pl.multiple_of(which * block + head * HD, HD), HD)
            keys = rms_norm(keys_ref[0, :, at], gain)
            ref[:, head * HD : (head + 1) * HD] = keys.astype(BF16)
            values = keys_ref[1, :, at]
            ref[:, block + head * HD : block + (head + 1) * HD] = jnp.where(
                live, values, DEAD
            ).astype(BF16)

    write(send_ref, 1 - core)
    write(own_ref, core)


def finish_kv(start, core, live_tiles, key_value, gain, after):
    _, half, columns = key_value.shape
    return pl.pallas_call(
        functools.partial(kv_kernel, start),
        in_specs=[SM, SM, VM, VM, AN],
        out_specs=[VM, VM],
        out_shape=[jax.ShapeDtypeStruct((half, columns), BF16)] * 2,
        compiler_params=params(8),
        cost_estimate=cost(10 * key_value.size, 6 * key_value.size),
        name="finish_kv",
    )(core, live_tiles, key_value, gain, after)


def query_kernel(text_ref, gain_ref, out_ref):
    kv_local, blocks, rows, _ = out_ref.shape
    group = rows // QB
    gain = gain_ref[...].reshape(1, -1)
    for head in range(kv_local):
        for block in range(blocks):
            for member in range(group):
                at = (head * group + member) * HD
                part = text_ref[block * QB : (block + 1) * QB, at : at + HD].astype(F32)
                out_ref[head, block, member * QB : (member + 1) * QB, :] = (
                    rms_norm(part, gain) / math.sqrt(HD)
                ).astype(BF16)


def norm_queries(text, gain, kv_local):
    rows, columns = text.shape
    group = columns // HD // kv_local
    return pl.pallas_call(
        query_kernel,
        in_specs=[VM, VM],
        out_specs=VM,
        out_shape=jax.ShapeDtypeStruct((kv_local, rows // QB, group * QB, HD), BF16),
        compiler_params=params(8),
        cost_estimate=cost(8 * rows * columns, 4 * rows * columns),
        name="norm_queries",
    )(text, gain)


def cross_kernel(slots, first, last, mask_ref, seq_ref, q_ref, *refs):
    flat = sum(count for _, count in slots)
    kv_refs, refs = list(refs[:flat]), refs[flat:]
    refs = refs if first else refs[1:]
    out_ref, acc, vals = refs if last else (None, *refs)
    kv_local, blocks, rows, _ = q_ref.shape
    group = rows // QB
    images = mask_ref.shape[1]
    if first:
        acc[...] = jnp.zeros_like(acc)

    def one_image(image, chunks):
        for head in range(kv_local):
            at = 0
            for kv in chunks:
                values = kv[:, (kv_local + head) * HD : (kv_local + head + 1) * HD]
                live = values < DEAD * 0.5
                span = slice(at, at + values.shape[0])
                vals[head, span, :HD] = jnp.where(live, values, jnp.zeros_like(values))
                vals[head, span, HD:] = jnp.where(live, 1.0, 0.0).astype(BF16)
                at += values.shape[0]
        for block in range(blocks):

            @pl.when(mask_ref[block, image] > 0)
            def _(block=block):
                for head in range(kv_local):
                    keys = [kv[:, head * HD : (head + 1) * HD] for kv in chunks]
                    keys = keys[0] if len(keys) == 1 else jnp.concatenate(keys, axis=0)
                    for member in range(group):
                        at = slice(member * QB, (member + 1) * QB)
                        sims = lax.dot_general(
                            q_ref[head, block, at, :], keys, NT, preferred_element_type=F32
                        )
                        expo = jnp.exp(sims).astype(BF16)
                        acc[head, block, at, :] += jnp.dot(
                            expo, vals[head], preferred_element_type=F32
                        )

    if slots[0][0] is None:

        @pl.loop(0, images)
        def _(image):
            one_image(image, [kv_refs[0].at[image]])
    else:
        for bits, count in slots:
            one_image(seq_ref[0] ^ bits, [kv_refs.pop(0) for _ in range(count)])

    if not last:
        return
    for block in range(blocks):
        seen = lax.fori_loop(
            0, images, lambda i, s, block=block: s + mask_ref[block, i], jnp.int32(0)
        )
        for head in range(kv_local):
            for member in range(group):
                at = slice(member * QB, (member + 1) * QB)
                total = acc[head, block, at, :HD]
                denom = acc[head, block, at, HD:]
                column = (head * group + member) * HD
                out_ref[block * QB : (block + 1) * QB, column : column + HD] = jnp.where(
                    seen > 0, total / jnp.where(seen > 0, denom, 1.0), 0.0
                ).astype(BF16)


def cross(mask, seq, queries, slots, acc=None, last=True):
    kv_local, blocks, rows, _ = queries.shape
    flat = [chunk for _, chunks in slots for chunk in chunks]
    keys = sum(chunk.shape[-2] for chunk in slots[0][1])
    columns = kv_local * (rows // QB) * HD
    work = blocks * rows * sum(kv.size for kv in flat) // (2 * HD)
    sums = (kv_local, blocks, rows, 2 * HD)
    given = [] if acc is None else [acc]
    shapes = [jax.ShapeDtypeStruct((blocks * QB, columns), BF16)] * last
    shapes.append(jax.ShapeDtypeStruct(sums, F32))
    result = pl.pallas_call(
        functools.partial(
            cross_kernel, [(bits, len(chunks)) for bits, chunks in slots], acc is None, last
        ),
        in_specs=[SM, SM, VM] + [VM] * len(flat + given),
        out_specs=[VM] * len(shapes),
        out_shape=shapes,
        scratch_shapes=[pltpu.VMEM((kv_local, keys, 2 * HD), BF16)],
        input_output_aliases={3 + len(flat): len(shapes) - 1} if given else {},
        compiler_params=params(14),
        cost_estimate=cost(4 * work * HD, 4 * queries.size, work),
        name="cross",
    )(mask, seq, queries, *flat, *given)
    return result[0]


def swap_line(bits, value):
    return lax.ppermute(value, "seq", [(s, s ^ bits) for s in range(8)])


def tie(values, *after):
    return lax.optimization_barrier((tuple(values), after))[0]


def gather_line(blocks):
    images = []
    for block in blocks:
        images.append({0: block, 4: swap_line(4, block), 2: swap_line(2, block)})
    crossed = []

    def swap_x(value):
        if len(crossed) > 1:
            value = tie((value,), crossed[-2])[0]
        crossed.append(swap_line(1, value))
        return crossed[-1]

    for got in images:
        got[1] = swap_x(got[0])
    for got in images:
        got[3] = swap_x(got[2])
        got[6] = swap_line(2, tie((got[4],), got[2])[0])
        got[5] = swap_x(got[4])
    for number, got in enumerate(images):
        if number == len(images) - 1 and number > 0:
            got[7] = swap_line(2, got[5])
        else:
            got[7] = swap_x(got[6])
    return images


def per_device(
    vis_in,
    live_tiles,
    ln1_gain,
    w_qkv,
    w_out,
    ln2_gain,
    w_fc1,
    w_fc2,
    w_kv,
    k_gain,
    q_gain,
    text_queries,
    block_mask,
):
    head_count = lax.axis_size("head")
    head_index = lax.axis_index("head")
    core = head_index % 2
    core_arg = core.astype(jnp.int32).reshape(1)
    kv_local = KVH // head_count
    swap_core = functools.partial(
        lax.ppermute, axis_name="head", perm=[(i, i ^ 1) for i in range(head_count)]
    )

    def swap_chip(value, bit):
        return lax.ppermute(value, "head", [(i, i ^ bit) for i in range(head_count)])

    def sum_chips(value):
        bit = 2
        other = swap_chip(value, bit)
        while 2 * bit < head_count:
            bit *= 2
            value = (value.astype(F32) + other.astype(F32)).astype(BF16)
            other = swap_chip(value, bit)
        return value, other

    x = vis_in.reshape(vis_in.shape[0] * vis_in.shape[1], vis_in.shape[2])
    rows, width = x.shape
    half = rows // 2
    line = lax.axis_size("seq") == 8
    cuts = [0, half * FIRST // 128, half] if line else [0, half]
    chunks = [slice(at, end) for at, end in zip(cuts, cuts[1:])]
    chip_columns = 2 * kv_local * HD

    queries = norm_queries(text_queries, q_gain, kv_local)
    send, kept, own_x = encode(
        core_arg, live_tiles, x, ln1_gain, jnp.swapaxes(w_qkv, 1, 2), w_out
    )
    received = swap_core(send)
    chip_arg = (head_index // 2).astype(jnp.int32).reshape(1)
    first = (kept + received.astype(F32)).astype(BF16)
    w1, w2, w_chip = fetch(chip_arg, w_fc1, w_fc2, w_kv, chip_columns, first)
    first, second = sum_chips(first)
    resid, normed = mid(own_x, first, second, ln2_gain, w_chip)
    other = swap_core(normed)
    sums = []
    for at in chunks:
        send, keep = mlp(normed[at], other[at], w1, w2)
        sums.append((keep + swap_core(send).astype(F32)).astype(BF16))
    sums = [sum_chips(value) for value in sums]
    blocks = []
    for at, (first, second) in zip(chunks, sums):
        second = tie((second,), blocks[-1] if blocks else sums[-1][0])[0]
        vision = (resid[at] + (first.astype(F32) + second.astype(F32))).astype(BF16)
        key_value = jnp.einsum("rc,cjd->jrd", vision, w_chip, preferred_element_type=F32)
        own, send = finish_kv(at.start, core_arg, live_tiles, key_value, k_gain, queries)
        blocks.append(jnp.concatenate([own, swap_core(send)], axis=0))

    seq = lax.axis_index("seq").astype(jnp.int32).reshape(1)
    if not line:
        stacked = lax.all_gather(jnp.concatenate(blocks, axis=0), "seq", axis=0)
        return cross(block_mask, seq, queries, [(None, [stacked])])
    gathered = gather_line(blocks)
    acc = None
    for number, part in enumerate(PARTS):
        slots = [(bits, [images[bits] for images in gathered]) for bits in part]
        acc = cross(block_mask, seq, queries, slots, acc, number == len(PARTS) - 1)
    return acc


def solution(mesh):
    placed = (
        P("seq", None, None),
        P("seq"),
        P(),
        P(None, None, "head"),
        P("head", None),
        P(),
        P(None, "head"),
        P("head", None),
        P(),
        P(),
        P(),
        P("seq", "head"),
        P("seq", None),
    )
    return jax.shard_map(
        per_device, mesh=mesh, in_specs=placed, out_specs=P("seq", "head"), check_vma=False
    )
```

time: 97.2 us -> 69.7 us (0.72)
  the two profiles are of different devices: /device:TPU:18 before, /device:TPU:0 now
where the time goes in v2:
time: 69.7 us; the launch traced here: 70.3 us
  Pallas kernels  25.4 us (36%)
  waiting for transfers between devices  22.4 us (32%)
  starting transfers between devices  20.2 us (29%)
  matrix products  1.07 us (2%)
  between operations  0.93 us (1%)
    ppermute x14, starting transfers between devices, swap_line(): return lax.ppermute(value, 'seq', [(s, s ^ bits) for s in range(8)])  13.1 us
    pallas_call x5, Pallas kernels, cross(): pl.pallas_call(functools.partial(cross_kernel, [(bits, len(chunks)) for b...  12 us
    ppermute x14, waiting for transfers between devices, swap_line(): return lax.ppermute(value, 'seq', [(s, s ^ bits) for s in range(8)])  8.58 us
    ppermute x3, waiting for transfers between devices, swap_chip(): lax.ppermute(value, 'head', [(i, i ^ bit) for i in range(head_count)])  8.56 us
    ppermute x3, starting transfers between devices, swap_chip(): lax.ppermute(value, 'head', [(i, i ^ bit) for i in range(head_count)])  5.76 us
    pallas_call x1, Pallas kernels, encode(): pl.pallas_call(encode_kernel, in_specs=[SM, SM, HB, HB, HB, HB], out_spec...  5.63 us
    pallas_call x1, Pallas kernels, fetch(): pl.pallas_call(fetch_kernel, in_specs=[SM, HB, HB, HB, AN], out_specs=[VM...  3.71 us
    ppermute x2, waiting for transfers between devices, per_device(): blocks.append(jnp.concatenate([own, swap_core(send)], axis=0))  2.45 us
  transfers between devices with their start and end apart: 23, of which 11 were waited for; matrix products, arithmetic and copies ran while one was open for 2% of the time, Pallas kernels for 21%

profile of v2, /device:TPU:0, one launch (start us, length us, event | category | flops | bytes accessed | tf_op | source)
XLA Modules:
  0.0 70.3 jit_solution(1146942021096123028)
XLA Ops:
  0.7 5.6 %encode.1 = (bf16[128,1280]{1,0:T(8,128)(2,1)S(1)}, f32[128,1280]{1,0:T(8,128)S(1)}, bf16[128,1280]{1,0:T(8,128)(2,1)S(1)}) custom-call(s32[1]{0:T(128)} %bitcast.1.core_ref, s32[1]{0:T(128)S(6)} %copy.34.live_ref, f32[1280]{0:T(1024)} %gain_hbm.1, bf16[256,1280]{1,0:T(8,128)(2,1)} %bitcast.16, bf16[3,320,1280]{2,1,0:T(8,128)(2,1)} %bitcast.15, ...), custom_call_target="tpu_custom_call" | custom-call | flops 838860800 | bytes 3276800 | tf_op jit(solution)/shard_map/encode/pallas_call | solution.py:118
  6.8 1.3 %collective-permute-done = bf16[128,1280]{1,0:T(8,128)(2,1)S(1)} collective-permute-done((bf16[128,1280]{1,0:T(8,128)(2,1)S(1)}, bf16[128,1280]{1,0:T(8,128)(2,1)S(1)}, u32[]{:S(2)}, u32[]{:S(2)}) %collective-permute-start) | collective-permute-done | bytes 327712 | tf_op jit(solution)/shard_map/ppermute | solution.py:452
  8.1 3.0 %collective-permute-start.1 = (bf16[128,1280]{1,0:T(8,128)(2,1)S(1)}, bf16[128,1280]{1,0:T(8,128)(2,1)S(1)}, u32[]{:S(2)}, u32[]{:S(2)}) collective-permute-start(bf16[128,1280]{1,0:T(8,128)(2,1)S(1)} %add_convert_fusion._.first_ref), channel_id=1, source_target_pairs={{0,2},{1,3},{2,0},{3,1},{4,6},{5,7},{6,4},{7,5},{8,10},{9,11},{10,... | collective-permute-start | bytes 983048 | tf_op jit(solution)/shard_map/ppermute | solution.py:429
  11.1 3.7 %fetch.1 = (bf16[1280,1280]{1,0:T(8,128)(2,1)S(1)}, bf16[1280,1280]{1,0:T(8,128)(2,1)S(1)}, bf16[1280,2,512]{2,1,0:T(2,128)(2,1)S(1)}) custom-call(s32[1]{0:T(128)} %bitcast.2.chip_ref, bf16[1280,1280]{1,0:T(8,128)(2,1)} %w1_hbm.1, bf16[1280,1280]{1,0:T(8,128)(2,1)} %w2_hbm.1, bf16[1280,2,1024]{2,1,0:T(2,128)(2,1)} %wkv_hbm.1, ...), custom_call_target="tpu_custom_call" | custom-call | bytes 32768000 | tf_op jit(solution)/shard_map/fetch/pallas_call | solution.py:179
  14.8 4.3 %collective-permute-done.1.second_ref = bf16[128,1280]{1,0:T(8,128)(2,1)S(1)} collective-permute-done((bf16[128,1280]{1,0:T(8,128)(2,1)S(1)}, bf16[128,1280]{1,0:T(8,128)(2,1)S(1)}, u32[]{:S(2)}, u32[]{:S(2)}) %collective-permute-start.1) | collective-permute-done | bytes 327712 | tf_op jit(solution)/shard_map/ppermute | solution.py:429
  19.5 1.6 %collective-permute-done.2 = bf16[128,1280]{1,0:T(8,128)(2,1)S(1)} collective-permute-done((bf16[128,1280]{1,0:T(8,128)(2,1)S(1)}, bf16[128,1280]{1,0:T(8,128)(2,1)S(1)}, u32[]{:S(2)}, u32[]{:S(2)}) %collective-permute-start.2) | collective-permute-done | bytes 327712 | tf_op jit(solution)/shard_map/ppermute | solution.py:458
  21.2 1.2 %mlp.2 = (bf16[64,1280]{1,0:T(8,128)(2,1)S(1)}, f32[64,1280]{1,0:T(8,128)S(1)}) custom-call(bf16[64,1280]{1,0:T(8,128)(2,1)S(1)} %get-tuple-element.60.own_ref, bf16[64,1280]{1,0:T(8,128)(2,1)S(1)} %get-tuple-element.58.other_ref, bf16[1280,1280]{1,0:T(8,128)(2,1)S(1)} %get-tuple-element.37.w1_ref, bf16[1280,1280]{1,0:T(8,128)(2,1)S(1)} %get-tuple-element.38.w2_ref), custom_call_target="tpu_custom_call" | custom-call | flops 838860800 | bytes 6553600 | tf_op jit(solution)/shard_map/mlp/pallas_call | solution.py:203
  23.7 1.2 %mlp.3 = (bf16[64,1280]{1,0:T(8,128)(2,1)S(1)}, f32[64,1280]{1,0:T(8,128)S(1)}) custom-call(bf16[64,1280]{1,0:T(8,128)(2,1)S(1)} %get-tuple-element.59.own_ref, bf16[64,1280]{1,0:T(8,128)(2,1)S(1)} %get-tuple-element.57.other_ref, bf16[1280,1280]{1,0:T(8,128)(2,1)S(1)} %get-tuple-element.37.w1_ref, bf16[1280,1280]{1,0:T(8,128)(2,1)S(1)} %get-tuple-element.38.w2_ref), custom_call_target="tpu_custom_call" | custom-call | flops 838860800 | bytes 6553600 | tf_op jit(solution)/shard_map/mlp/pallas_call | solution.py:203
  25.3 1.8 %collective-permute-start.4 = (bf16[64,1280]{1,0:T(8,128)(2,1)S(1)}, bf16[64,1280]{1,0:T(8,128)(2,1)S(1)}, u32[]{:S(2)}, u32[]{:S(2)}) collective-permute-start(bf16[64,1280]{1,0:T(8,128)(2,1)S(1)} %add_convert_fusion.4), channel_id=1, source_target_pairs={{0,2},{1,3},{2,0},{3,1},{4,6},{5,7},{6,4},{7,5},{8,10},{9,11},{10,... | collective-permute-start | bytes 491528 | tf_op jit(solution)/shard_map/ppermute | solution.py:429
  28.2 4.3 %collective-permute-done.4 = bf16[64,1280]{1,0:T(8,128)(2,1)S(1)} collective-permute-done((bf16[64,1280]{1,0:T(8,128)(2,1)S(1)}, bf16[64,1280]{1,0:T(8,128)(2,1)S(1)}, u32[]{:S(2)}, u32[]{:S(2)}) %collective-permute-start.4) | collective-permute-done | bytes 163872 | tf_op jit(solution)/shard_map/ppermute | solution.py:429
  33.3 1.2 %collective-permute-done.6 = bf16[64,512]{1,0:T(8,128)(2,1)S(1)} collective-permute-done((bf16[64,512]{1,0:T(8,128)(2,1)S(1)}, bf16[64,512]{1,0:T(8,128)(2,1)S(1)}, u32[]{:S(2)}, u32[]{:S(2)}) %collective-permute-start.6) | collective-permute-done | bytes 65568 | tf_op jit(solution)/shard_map/ppermute | solution.py:470
  34.5 1.7 %collective-permute-start.13 = (bf16[128,512]{1,0:T(8,128)(2,1)S(1)}, bf16[128,512]{1,0:T(8,128)(2,1)S(1)}, u32[]{:S(2)}, u32[]{:S(2)}) collective-permute-start(bf16[128,512]{1,0:T(8,128)(2,1)S(1)} %constant_dynamic-update-slice_fusion.refs_0_), channel_id=1, source_target_pairs={{0,4},{4,0},{8,12},{12,8},{16,20},{20,16},{24,28},{28,24},{1,5},{5... | collective-permute-start | bytes 393224 | tf_op jit(solution)/shard_map/ppermute | solution.py:371
  36.2 1.6 %collective-permute-start.8 = (bf16[128,512]{1,0:T(8,128)(2,1)S(1)}, bf16[128,512]{1,0:T(8,128)(2,1)S(1)}, u32[]{:S(2)}, u32[]{:S(2)}) collective-permute-start(bf16[128,512]{1,0:T(8,128)(2,1)S(1)} %constant_dynamic-update-slice_fusion.refs_0_), channel_id=1, source_target_pairs={{0,8},{4,12},{8,0},{12,4},{16,24},{20,28},{24,16},{28,20},{1,9},{5... | collective-permute-start | bytes 393224 | tf_op jit(solution)/shard_map/ppermute | solution.py:371
  37.8 2.6 %collective-permute-start.7 = (bf16[128,512]{1,0:T(8,128)(2,1)S(1)}, bf16[128,512]{1,0:T(8,128)(2,1)S(1)}, u32[]{:S(2)}, u32[]{:S(2)}) collective-permute-start(bf16[128,512]{1,0:T(8,128)(2,1)S(1)} %constant_dynamic-update-slice_fusion.refs_0_), channel_id=1, source_target_pairs={{0,16},{4,20},{8,24},{12,28},{16,0},{20,4},{24,8},{28,12},{1,17},{... | collective-permute-start | bytes 393224 | tf_op jit(solution)/shard_map/ppermute | solution.py:371
  41.2 1.2 %collective-permute-done.11 = bf16[64,512]{1,0:T(8,128)(2,1)S(1)} collective-permute-done((bf16[64,512]{1,0:T(8,128)(2,1)S(1)}, bf16[64,512]{1,0:T(8,128)(2,1)S(1)}, u32[]{:S(2)}, u32[]{:S(2)}) %collective-permute-start.11) | collective-permute-done | bytes 65568 | tf_op jit(solution)/shard_map/ppermute | solution.py:470
  43.5 1.7 %collective-permute-start.14 = (bf16[128,512]{1,0:T(8,128)(2,1)S(1)}, bf16[128,512]{1,0:T(8,128)(2,1)S(1)}, u32[]{:S(2)}, u32[]{:S(2)}) collective-permute-start(bf16[128,512]{1,0:T(8,128)(2,1)S(1)} %collective-permute-done.8.refs_0_), channel_id=1, source_target_pairs={{0,4},{4,0},{8,12},{12,8},{16,20},{20,16},{24,28},{28,24},{1,5},{5... | collective-permute-start | bytes 393224 | tf_op jit(solution)/shard_map/ppermute | solution.py:371
  45.7 3.1 %collective-permute-done.18.refs_3_ = bf16[128,512]{1,0:T(8,128)(2,1)S(1)} collective-permute-done((bf16[128,512]{1,0:T(8,128)(2,1)S(1)}, bf16[128,512]{1,0:T(8,128)(2,1)S(1)}, u32[]{:S(2)}, u32[]{:S(2)}) %collective-permute-start.18) | collective-permute-done | bytes 131104 | tf_op jit(solution)/shard_map/ppermute | solution.py:371
  49.3 1.6 %collective-permute-done.12.refs_1_ = bf16[128,512]{1,0:T(8,128)(2,1)S(1)} collective-permute-done((bf16[128,512]{1,0:T(8,128)(2,1)S(1)}, bf16[128,512]{1,0:T(8,128)(2,1)S(1)}, u32[]{:S(2)}, u32[]{:S(2)}) %collective-permute-start.12) | collective-permute-done | bytes 131104 | tf_op jit(solution)/shard_map/ppermute | solution.py:371
  52.1 2.7 %collective-permute-done.19.refs_0_ = bf16[128,512]{1,0:T(8,128)(2,1)S(1)} collective-permute-done((bf16[128,512]{1,0:T(8,128)(2,1)S(1)}, bf16[128,512]{1,0:T(8,128)(2,1)S(1)}, u32[]{:S(2)}, u32[]{:S(2)}) %collective-permute-start.19) | collective-permute-done | bytes 131104 | tf_op jit(solution)/shard_map/ppermute | solution.py:371
  56.2 1.3 %collective-permute-start.22 = (bf16[128,512]{1,0:T(8,128)(2,1)S(1)}, bf16[128,512]{1,0:T(8,128)(2,1)S(1)}, u32[]{:S(2)}, u32[]{:S(2)}) collective-permute-start(bf16[128,512]{1,0:T(8,128)(2,1)S(1)} %collective-permute-done.17.refs_1_), channel_id=1, source_target_pairs={{0,8},{4,12},{8,0},{12,4},{16,24},{20,28},{24,16},{28,20},{1,9},{5... | collective-permute-start | bytes 393224 | tf_op jit(solution)/shard_map/ppermute | solution.py:371
  57.4 3.4 %cross.6.refs_4_ = f32[2,2,1024,256]{3,2,1,0:T(8,128)S(1)} custom-call(s32[2,8]{1,0:T(2,128)S(1)} %copy-done.1, s32[1]{0:T(128)} %bitcast.seq_ref, bf16[2,2,1024,128]{3,2,1,0:T(8,128)(2,1)S(1)} %norm_queries.1._.q_ref, bf16[128,512]{1,0:T(8,128)(2,1)S(1)} %collective-permute-done.8.refs_0_, ...), custom_call_target="tpu_custom_call", output_to_operand_aliasing={{}: (7, {})} | custom-call | flops 1073741824 | bytes 2097152 | tf_op jit(solution)/shard_map/cross/pallas_call | solution.py:354
  61.4 1.2 %collective-permute-start.21 = (bf16[128,512]{1,0:T(8,128)(2,1)S(1)}, bf16[128,512]{1,0:T(8,128)(2,1)S(1)}, u32[]{:S(2)}, u32[]{:S(2)}) collective-permute-start(bf16[128,512]{1,0:T(8,128)(2,1)S(1)} %collective-permute-done.20.refs_1_), channel_id=1, source_target_pairs={{0,8},{4,12},{8,0},{12,4},{16,24},{20,28},{24,16},{28,20},{1,9},{5... | collective-permute-start | bytes 393224 | tf_op jit(solution)/shard_map/ppermute | solution.py:371
  62.5 3.2 %cross.7.refs_4_ = f32[2,2,1024,256]{3,2,1,0:T(8,128)S(1)} custom-call(s32[2,8]{1,0:T(2,128)S(1)} %copy-done.1, s32[1]{0:T(128)} %bitcast.seq_ref, bf16[2,2,1024,128]{3,2,1,0:T(8,128)(2,1)S(1)} %norm_queries.1._.q_ref, bf16[128,512]{1,0:T(8,128)(2,1)S(1)} %collective-permute-done.7.refs_0_, ...), custom_call_target="tpu_custom_call", output_to_operand_aliasing={{}: (7, {})} | custom-call | flops 1073741824 | bytes 2097152 | tf_op jit(solution)/shard_map/cross/pallas_call | solution.py:354
  66.5 3.7 %cross.9 = (bf16[256,2048]{1,0:T(8,128)(2,1)}, f32[2,2,1024,256]{3,2,1,0:T(8,128)S(1)}) custom-call(s32[2,8]{1,0:T(2,128)S(1)} %copy-done.1, s32[1]{0:T(128)} %bitcast.seq_ref, bf16[2,2,1024,128]{3,2,1,0:T(8,128)(2,1)S(1)} %norm_queries.1._.q_ref, bf16[128,512]{1,0:T(8,128)(2,1)S(1)} %collective-permute-done.16.refs_0_, ...), custom_call_target="tpu_custom_call", output_to_operand_aliasing={{1}: (5, {})} | custom-call | flops 536870912 | bytes 2097152 | tf_op jit(solution)/shard_map/cross/pallas_call | solution.py:354
  (56 shorter events, 11.3 us)
Async XLA Ops:
  6.3 1.8 %collective-permute-start = (bf16[128,1280]{1,0:T(8,128)(2,1)S(1)}, bf16[128,1280]{1,0:T(8,128)(2,1)S(1)}, u32[]{:S(2)}, u32[]{:S(2)}) collective-permute-start(bf16[128,1280]{1,0:T(8,128)(2,1)S(1)} %get-tuple-element.32), channel_id=1, source_target_pairs={{0,1},{1,0},{2,3},{3,2},{4,5},{5,4},{6,7},{7,6},{8,9},{9,8},{10,11... | collective-permute-start | bytes 983048 | tf_op jit(solution)/shard_map/ppermute | solution.py:452
  8.1 11.0 %collective-permute-start.1 = (bf16[128,1280]{1,0:T(8,128)(2,1)S(1)}, bf16[128,1280]{1,0:T(8,128)(2,1)S(1)}, u32[]{:S(2)}, u32[]{:S(2)}) collective-permute-start(bf16[128,1280]{1,0:T(8,128)(2,1)S(1)} %add_convert_fusion._.first_ref), channel_id=1, source_target_pairs={{0,2},{1,3},{2,0},{3,1},{4,6},{5,7},{6,4},{7,5},{8,10},{9,11},{10,... | collective-permute-start | bytes 983048 | tf_op jit(solution)/shard_map/ppermute | solution.py:429
  19.4 1.7 %collective-permute-start.2 = (bf16[128,1280]{1,0:T(8,128)(2,1)S(1)}, bf16[128,1280]{1,0:T(8,128)(2,1)S(1)}, u32[]{:S(2)}, u32[]{:S(2)}) collective-permute-start(bf16[128,1280]{1,0:T(8,128)(2,1)S(1)} %get-tuple-element.36), channel_id=1, source_target_pairs={{0,1},{1,0},{2,3},{3,2},{4,5},{5,4},{6,7},{7,6},{8,9},{9,8},{10,11... | collective-permute-start | bytes 983048 | tf_op jit(solution)/shard_map/ppermute | solution.py:458
  22.4 3.0 %collective-permute-start.3 = (bf16[64,1280]{1,0:T(8,128)(2,1)S(1)}, bf16[64,1280]{1,0:T(8,128)(2,1)S(1)}, u32[]{:S(2)}, u32[]{:S(2)}) collective-permute-start(bf16[64,1280]{1,0:T(8,128)(2,1)S(1)} %get-tuple-element.40), channel_id=1, source_target_pairs={{0,1},{1,0},{2,3},{3,2},{4,5},{5,4},{6,7},{7,6},{8,9},{9,8},{10,11... | collective-permute-start | bytes 491528 | tf_op jit(solution)/shard_map/ppermute | solution.py:462
  24.9 2.3 %collective-permute-start.5 = (bf16[64,1280]{1,0:T(8,128)(2,1)S(1)}, bf16[64,1280]{1,0:T(8,128)(2,1)S(1)}, u32[]{:S(2)}, u32[]{:S(2)}) collective-permute-start(bf16[64,1280]{1,0:T(8,128)(2,1)S(1)} %get-tuple-element.42), channel_id=1, source_target_pairs={{0,1},{1,0},{2,3},{3,2},{4,5},{5,4},{6,7},{7,6},{8,9},{9,8},{10,11... | collective-permute-start | bytes 491528 | tf_op jit(solution)/shard_map/ppermute | solution.py:462
  25.3 7.1 %collective-permute-start.4 = (bf16[64,1280]{1,0:T(8,128)(2,1)S(1)}, bf16[64,1280]{1,0:T(8,128)(2,1)S(1)}, u32[]{:S(2)}, u32[]{:S(2)}) collective-permute-start(bf16[64,1280]{1,0:T(8,128)(2,1)S(1)} %add_convert_fusion.4), channel_id=1, source_target_pairs={{0,2},{1,3},{2,0},{3,1},{4,6},{5,7},{6,4},{7,5},{8,10},{9,11},{10,... | collective-permute-start | bytes 491528 | tf_op jit(solution)/shard_map/ppermute | solution.py:429
  27.2 13.2 %collective-permute-start.10 = (bf16[64,1280]{1,0:T(8,128)(2,1)S(1)}, bf16[64,1280]{1,0:T(8,128)(2,1)S(1)}, u32[]{:S(2)}, u32[]{:S(2)}) collective-permute-start(bf16[64,1280]{1,0:T(8,128)(2,1)S(1)} %add_convert_fusion.3), channel_id=1, source_target_pairs={{0,2},{1,3},{2,0},{3,1},{4,6},{5,7},{6,4},{7,5},{8,10},{9,11},{10,... | collective-permute-start | bytes 491528 | tf_op jit(solution)/shard_map/ppermute | solution.py:429
  33.0 22.3 %copy-start.1 = (s32[2,8]{1,0:T(2,128)S(1)}, s32[2,8]{1,0:T(2,128)}, u32[]{:S(2)}) copy-start(s32[2,8]{1,0:T(2,128)} %mask_ref.9) | copy-start | bytes 196
  33.2 1.3 %collective-permute-start.6 = (bf16[64,512]{1,0:T(8,128)(2,1)S(1)}, bf16[64,512]{1,0:T(8,128)(2,1)S(1)}, u32[]{:S(2)}, u32[]{:S(2)}) collective-permute-start(bf16[64,512]{1,0:T(8,128)(2,1)S(1)} %get-tuple-element.45), channel_id=1, source_target_pairs={{0,1},{1,0},{2,3},{3,2},{4,5},{5,4},{6,7},{7,6},{8,9},{9,8},{10,11... | collective-permute-start | bytes 196616 | tf_op jit(solution)/shard_map/ppermute | solution.py:470
  34.5 8.9 %collective-permute-start.13 = (bf16[128,512]{1,0:T(8,128)(2,1)S(1)}, bf16[128,512]{1,0:T(8,128)(2,1)S(1)}, u32[]{:S(2)}, u32[]{:S(2)}) collective-permute-start(bf16[128,512]{1,0:T(8,128)(2,1)S(1)} %constant_dynamic-update-slice_fusion.refs_0_), channel_id=1, source_target_pairs={{0,4},{4,0},{8,12},{12,8},{16,20},{20,16},{24,28},{28,24},{1,5},{5... | collective-permute-start | bytes 393224 | tf_op jit(solution)/shard_map/ppermute | solution.py:371
  36.2 7.3 %collective-permute-start.8 = (bf16[128,512]{1,0:T(8,128)(2,1)S(1)}, bf16[128,512]{1,0:T(8,128)(2,1)S(1)}, u32[]{:S(2)}, u32[]{:S(2)}) collective-permute-start(bf16[128,512]{1,0:T(8,128)(2,1)S(1)} %constant_dynamic-update-slice_fusion.refs_0_), channel_id=1, source_target_pairs={{0,8},{4,12},{8,0},{12,4},{16,24},{20,28},{24,16},{28,20},{1,9},{5... | collective-permute-start | bytes 393224 | tf_op jit(solution)/shard_map/ppermute | solution.py:371
  37.8 7.9 %collective-permute-start.7 = (bf16[128,512]{1,0:T(8,128)(2,1)S(1)}, bf16[128,512]{1,0:T(8,128)(2,1)S(1)}, u32[]{:S(2)}, u32[]{:S(2)}) collective-permute-start(bf16[128,512]{1,0:T(8,128)(2,1)S(1)} %constant_dynamic-update-slice_fusion.refs_0_), channel_id=1, source_target_pairs={{0,16},{4,20},{8,24},{12,28},{16,0},{20,4},{24,8},{28,12},{1,17},{... | collective-permute-start | bytes 393224 | tf_op jit(solution)/shard_map/ppermute | solution.py:371
  41.1 1.3 %collective-permute-start.11 = (bf16[64,512]{1,0:T(8,128)(2,1)S(1)}, bf16[64,512]{1,0:T(8,128)(2,1)S(1)}, u32[]{:S(2)}, u32[]{:S(2)}) collective-permute-start(bf16[64,512]{1,0:T(8,128)(2,1)S(1)} %get-tuple-element.49), channel_id=1, source_target_pairs={{0,1},{1,0},{2,3},{3,2},{4,5},{5,4},{6,7},{7,6},{8,9},{9,8},{10,11... | collective-permute-start | bytes 196616 | tf_op jit(solution)/shard_map/ppermute | solution.py:470
  42.4 6.3 %collective-permute-start.18 = (bf16[128,512]{1,0:T(8,128)(2,1)S(1)}, bf16[128,512]{1,0:T(8,128)(2,1)S(1)}, u32[]{:S(2)}, u32[]{:S(2)}) collective-permute-start(bf16[128,512]{1,0:T(8,128)(2,1)S(1)} %constant_dynamic-update-slice_fusion.2.refs_1_), channel_id=1, source_target_pairs={{0,4},{4,0},{8,12},{12,8},{16,20},{20,16},{24,28},{28,24},{1,5},{5... | collective-permute-start | bytes 393224 | tf_op jit(solution)/shard_map/ppermute | solution.py:371
  42.9 7.9 %collective-permute-start.12 = (bf16[128,512]{1,0:T(8,128)(2,1)S(1)}, bf16[128,512]{1,0:T(8,128)(2,1)S(1)}, u32[]{:S(2)}, u32[]{:S(2)}) collective-permute-start(bf16[128,512]{1,0:T(8,128)(2,1)S(1)} %constant_dynamic-update-slice_fusion.2.refs_1_), channel_id=1, source_target_pairs={{0,8},{4,12},{8,0},{12,4},{16,24},{20,28},{24,16},{28,20},{1,9},{5... | collective-permute-start | bytes 393224 | tf_op jit(solution)/shard_map/ppermute | solution.py:371
  43.4 8.7 %collective-permute-start.17 = (bf16[128,512]{1,0:T(8,128)(2,1)S(1)}, bf16[128,512]{1,0:T(8,128)(2,1)S(1)}, u32[]{:S(2)}, u32[]{:S(2)}) collective-permute-start(bf16[128,512]{1,0:T(8,128)(2,1)S(1)} %constant_dynamic-update-slice_fusion.2.refs_1_), channel_id=1, source_target_pairs={{0,16},{4,20},{8,24},{12,28},{16,0},{20,4},{24,8},{28,12},{1,17},{... | collective-permute-start | bytes 393224 | tf_op jit(solution)/shard_map/ppermute | solution.py:371
  43.5 8.0 %collective-permute-start.14 = (bf16[128,512]{1,0:T(8,128)(2,1)S(1)}, bf16[128,512]{1,0:T(8,128)(2,1)S(1)}, u32[]{:S(2)}, u32[]{:S(2)}) collective-permute-start(bf16[128,512]{1,0:T(8,128)(2,1)S(1)} %collective-permute-done.8.refs_0_), channel_id=1, source_target_pairs={{0,4},{4,0},{8,12},{12,8},{16,20},{20,16},{24,28},{28,24},{1,5},{5... | collective-permute-start | bytes 393224 | tf_op jit(solution)/shard_map/ppermute | solution.py:371
  48.8 6.1 %collective-permute-start.19 = (bf16[128,512]{1,0:T(8,128)(2,1)S(1)}, bf16[128,512]{1,0:T(8,128)(2,1)S(1)}, u32[]{:S(2)}, u32[]{:S(2)}) collective-permute-start(bf16[128,512]{1,0:T(8,128)(2,1)S(1)} %collective-permute-done.7.refs_0_), channel_id=1, source_target_pairs={{0,4},{4,0},{8,12},{12,8},{16,20},{20,16},{24,28},{28,24},{1,5},{5... | collective-permute-start | bytes 393224 | tf_op jit(solution)/shard_map/ppermute | solution.py:371
  49.3 11.6 %collective-permute-start.9 = (bf16[128,512]{1,0:T(8,128)(2,1)S(1)}, bf16[128,512]{1,0:T(8,128)(2,1)S(1)}, u32[]{:S(2)}, u32[]{:S(2)}) collective-permute-start(bf16[128,512]{1,0:T(8,128)(2,1)S(1)} %collective-permute-done.7.refs_0_), channel_id=1, source_target_pairs={{0,8},{4,12},{8,0},{12,4},{16,24},{20,28},{24,16},{28,20},{1,9},{5... | collective-permute-start | bytes 393224 | tf_op jit(solution)/shard_map/ppermute | solution.py:371
  51.6 9.3 %collective-permute-start.15 = (bf16[128,512]{1,0:T(8,128)(2,1)S(1)}, bf16[128,512]{1,0:T(8,128)(2,1)S(1)}, u32[]{:S(2)}, u32[]{:S(2)}) collective-permute-start(bf16[128,512]{1,0:T(8,128)(2,1)S(1)} %collective-permute-done.12.refs_1_), channel_id=1, source_target_pairs={{0,4},{4,0},{8,12},{12,8},{16,20},{20,16},{24,28},{28,24},{1,5},{5... | collective-permute-start | bytes 393224 | tf_op jit(solution)/shard_map/ppermute | solution.py:371
  54.8 6.5 %collective-permute-start.20 = (bf16[128,512]{1,0:T(8,128)(2,1)S(1)}, bf16[128,512]{1,0:T(8,128)(2,1)S(1)}, u32[]{:S(2)}, u32[]{:S(2)}) collective-permute-start(bf16[128,512]{1,0:T(8,128)(2,1)S(1)} %collective-permute-done.17.refs_1_), channel_id=1, source_target_pairs={{0,4},{4,0},{8,12},{12,8},{16,20},{20,16},{24,28},{28,24},{1,5},{5... | collective-permute-start | bytes 393224 | tf_op jit(solution)/shard_map/ppermute | solution.py:371
  56.2 9.6 %collective-permute-start.22 = (bf16[128,512]{1,0:T(8,128)(2,1)S(1)}, bf16[128,512]{1,0:T(8,128)(2,1)S(1)}, u32[]{:S(2)}, u32[]{:S(2)}) collective-permute-start(bf16[128,512]{1,0:T(8,128)(2,1)S(1)} %collective-permute-done.17.refs_1_), channel_id=1, source_target_pairs={{0,8},{4,12},{8,0},{12,4},{16,24},{20,28},{24,16},{28,20},{1,9},{5... | collective-permute-start | bytes 393224 | tf_op jit(solution)/shard_map/ppermute | solution.py:371
  60.9 5.6 %collective-permute-start.16 = (bf16[128,512]{1,0:T(8,128)(2,1)S(1)}, bf16[128,512]{1,0:T(8,128)(2,1)S(1)}, u32[]{:S(2)}, u32[]{:S(2)}) collective-permute-start(bf16[128,512]{1,0:T(8,128)(2,1)S(1)} %collective-permute-done.9.refs_2_), channel_id=1, source_target_pairs={{0,4},{4,0},{8,12},{12,8},{16,20},{20,16},{24,28},{28,24},{1,5},{5... | collective-permute-start | bytes 393224 | tf_op jit(solution)/shard_map/ppermute | solution.py:371
  61.4 5.2 %collective-permute-start.21 = (bf16[128,512]{1,0:T(8,128)(2,1)S(1)}, bf16[128,512]{1,0:T(8,128)(2,1)S(1)}, u32[]{:S(2)}, u32[]{:S(2)}) collective-permute-start(bf16[128,512]{1,0:T(8,128)(2,1)S(1)} %collective-permute-done.20.refs_1_), channel_id=1, source_target_pairs={{0,8},{4,12},{8,0},{12,4},{16,24},{20,28},{24,16},{28,20},{1,9},{5... | collective-permute-start | bytes 393224 | tf_op jit(solution)/shard_map/ppermute | solution.py:371
  (4 other events, 19.0 us)

commit v3 on v2

v3 whole, which is shorter than its diff:
```python
import functools
import math

import jax
import jax.numpy as jnp
from jax import lax
from jax.experimental import pallas as pl
from jax.experimental.pallas import tpu as pltpu
from jax.sharding import PartitionSpec as P

KVH = 8
HD = 128
TILE_TOK = 64
QB = 128
VHD = 80
KI = 256
DEAD = 1e30
FIRST = 64
EARLY = [[0], [2, 1]]
LATE = [[4, 3], [5, 6], [7]]
F32 = jnp.float32
BF16 = jnp.bfloat16

NT = (((1,), (1,)), ((), ()))
VM = pl.BlockSpec(memory_space=pltpu.VMEM)
SM = pl.BlockSpec(memory_space=pltpu.SMEM)
HB = pl.BlockSpec(memory_space=pltpu.HBM)
AN = pl.BlockSpec(memory_space=pl.ANY)


def params(mib):
    return pltpu.CompilerParams(vmem_limit_bytes=mib * 1024 * 1024)


def in_hbm(value):
    return pltpu.with_memory_space_constraint(value, pltpu.HBM)


def cost(flops, size, transcendentals=0):
    return pl.CostEstimate(flops=flops, bytes_accessed=size, transcendentals=transcendentals)


def layer_norm(values, gain):
    center = values - jnp.mean(values, axis=-1, keepdims=True)
    spread = jnp.mean(center * center, axis=-1, keepdims=True)
    return center * (1.0 / jnp.sqrt(spread + 1e-05)) * gain


def rms_norm(values, gain):
    square = jnp.mean(values * values, axis=-1, keepdims=True)
    return values * (1.0 / jnp.sqrt(square + 1e-05)) * gain


def encode_kernel(
    core_ref,
    live_ref,
    gain_hbm,
    x_hbm,
    wqkv_hbm,
    wout_hbm,
    send_ref,
    keep_ref,
    own_ref,
    gain_ref,
    x_ref,
    wqkv_ref,
    wout_ref,
    mixed_ref,
    sems,
):
    loads = [pltpu.make_async_copy(x_hbm, x_ref, sems.at[0])]
    loads += [
        pltpu.make_async_copy(wqkv_hbm.at[j], wqkv_ref.at[j], sems.at[1 + j]) for j in range(3)
    ]
    loads.append(pltpu.make_async_copy(wout_hbm, wout_ref, sems.at[4]))
    loads.append(pltpu.make_async_copy(gain_hbm, gain_ref, sems.at[5]))
    for load in loads:
        load.start()
    rows, width = mixed_ref.shape
    half = rows // 2
    core = core_ref[0]
    own_rows = pl.ds(pl.multiple_of(core * half, half), half)
    other_rows = pl.ds(pl.multiple_of((1 - core) * half, half), half)

    loads[0].wait()
    loads[5].wait()
    own_ref[...] = x_ref[own_rows, :]
    normed = layer_norm(x_ref[...].astype(F32), gain_ref[...].reshape(1, -1)).astype(BF16)
    for load in loads[1:4]:
        load.wait()
    weights = wqkv_ref[...].reshape(3 * width, x_ref.shape[1])
    qkv = lax.dot_general(normed, weights, NT, preferred_element_type=F32).astype(BF16)
    q, k, v = [qkv[:, j * width : (j + 1) * width] for j in range(3)]
    lane = lax.broadcasted_iota(jnp.int32, (1, width), 1)
    slot = lax.broadcasted_iota(jnp.int32, (1, rows), 1)
    live = jnp.where(slot < live_ref[0] * TILE_TOK, 1.0, 0.0).astype(F32)
    zero = jnp.zeros_like(q)
    mixed = jnp.zeros((rows, width), F32)
    for head in range(width // VHD):
        own = (lane >= head * VHD) & (lane < (head + 1) * VHD)
        scores = lax.dot_general(jnp.where(own, q, zero), k, NT, preferred_element_type=F32)
        expo = jnp.exp(scores * (1.0 / math.sqrt(VHD))) * live
        probs = (expo * (1.0 / jnp.sum(expo, axis=-1, keepdims=True))).astype(BF16)
        mixed = mixed + jnp.dot(probs, jnp.where(own, v, zero), preferred_element_type=F32)
    mixed_ref[...] = mixed.astype(BF16)
    loads[4].wait()
    send_ref[...] = jnp.dot(
        mixed_ref[other_rows, :], wout_ref[...], preferred_element_type=F32
    ).astype(BF16)
    keep_ref[...] = jnp.dot(mixed_ref[own_rows, :], wout_ref[...], preferred_element_type=F32)


def encode(core, live_tiles, x, gain, w_qkv_t, w_out):
    rows, width = x.shape
    own = w_out.shape[0]
    return pl.pallas_call(
        encode_kernel,
        in_specs=[SM, SM, HB, HB, HB, HB],
        out_specs=[VM, VM, VM],
        out_shape=[
            jax.ShapeDtypeStruct((rows // 2, width), BF16),
            jax.ShapeDtypeStruct((rows // 2, width), F32),
            jax.ShapeDtypeStruct((rows // 2, width), BF16),
        ],
        scratch_shapes=[
            pltpu.VMEM(gain.shape, F32),
            pltpu.VMEM(x.shape, BF16),
            pltpu.VMEM(w_qkv_t.shape, BF16),
            pltpu.VMEM(w_out.shape, BF16),
            pltpu.VMEM((rows, own), BF16),
            pltpu.SemaphoreType.DMA((6,)),
        ],
        compiler_params=params(12),
        cost_estimate=cost(2 * rows * width * 4 * own, 8 * width * own, rows * rows * own // VHD),
        name="encode",
    )(core, live_tiles, in_hbm(gain), in_hbm(x), in_hbm(w_qkv_t), in_hbm(w_out))


def mid_kernel(x_ref, first_ref, second_ref, gain_ref, _, __, resid_ref, normed_ref):
    resid = x_ref[...].astype(F32) + (first_ref[...].astype(F32) + second_ref[...].astype(F32))
    resid_ref[...] = resid
    normed_ref[...] = layer_norm(resid, gain_ref[...].reshape(1, -1)).astype(BF16)


def mid(x, first, second, gain, *after):
    half, width = first.shape
    return pl.pallas_call(
        mid_kernel,
        in_specs=[VM, VM, VM, VM, AN, AN],
        out_specs=[VM, VM],
        out_shape=[
            jax.ShapeDtypeStruct((half, width), F32),
            jax.ShapeDtypeStruct((half, width), BF16),
        ],
        compiler_params=params(8),
        cost_estimate=cost(10 * half * width, 14 * half * width),
        name="mid",
    )(x, first, second, gain, *after)


def fetch_kernel(chip_ref, w1_hbm, w2_hbm, wkv_hbm, _, w1_ref, w2_ref, wkv_ref, sems):
    columns = wkv_ref.shape[2]
    mine = pl.ds(pl.multiple_of(chip_ref[0] * columns, HD), columns)
    loads = [
        pltpu.make_async_copy(w1_hbm, w1_ref, sems.at[0]),
        pltpu.make_async_copy(w2_hbm, w2_ref, sems.at[1]),
        pltpu.make_async_copy(wkv_hbm.at[:, :, mine], wkv_ref, sems.at[2]),
    ]
    for load in loads:
        load.start()
    for load in loads:
        load.wait()


def fetch(chip, w1, w2, w_kv, columns, after):
    shapes = [w1.shape, w2.shape, (w_kv.shape[0], w_kv.shape[1], columns)]
    return pl.pallas_call(
        fetch_kernel,
        in_specs=[SM, HB, HB, HB, AN],
        out_specs=[VM, VM, VM],
        out_shape=[jax.ShapeDtypeStruct(shape, BF16) for shape in shapes],
        scratch_shapes=[pltpu.SemaphoreType.DMA((3,))],
        compiler_params=params(16),
        cost_estimate=cost(0, 20 * w1.size),
        name="fetch",
    )(chip, in_hbm(w1), in_hbm(w2), in_hbm(w_kv), after)


def mlp_kernel(normed_ref, w1_ref, w2_ref, out_ref):
    hidden = jnp.dot(normed_ref[...], w1_ref[...], preferred_element_type=F32)
    inner = (0.5 * hidden * (1.0 + lax.erf(hidden * math.sqrt(0.5)))).astype(BF16)
    result = jnp.dot(inner, w2_ref[...], preferred_element_type=F32)
    out_ref[...] = result.astype(out_ref.dtype)


def mlp(normed, w1, w2, kept_as):
    return pl.pallas_call(
        mlp_kernel,
        in_specs=[VM, VM, VM],
        out_specs=VM,
        out_shape=jax.ShapeDtypeStruct(normed.shape, kept_as),
        compiler_params=params(14),
        cost_estimate=cost(4 * normed.size * w1.shape[1], 4 * w1.size, 2 * normed.size),
        name="mlp",
    )(normed, w1, w2)


def kv_kernel(start, core_ref, live_ref, keys_ref, gain_ref, own_ref, send_ref):
    half = keys_ref.shape[1]
    block = own_ref.shape[1] // 2
    core = core_ref[0]
    slot = lax.broadcasted_iota(jnp.int32, (half, 1), 0) + core * (KI // 2) + start
    live = slot < live_ref[0] * TILE_TOK
    gain = gain_ref[...].reshape(1, -1)

    def write(ref, which):
        for head in range(block // HD):
            at = pl.ds(pl.multiple_of(which * block + head * HD, HD), HD)
            keys = rms_norm(keys_ref[0, :, at], gain)
            ref[:, head * HD : (head + 1) * HD] = keys.astype(BF16)
            values = keys_ref[1, :, at]
            ref[:, block + head * HD : block + (head + 1) * HD] = jnp.where(
                live, values, DEAD
            ).astype(BF16)

    write(send_ref, 1 - core)
    write(own_ref, core)


def finish_kv(start, core, live_tiles, key_value, gain):
    _, half, columns = key_value.shape
    return pl.pallas_call(
        functools.partial(kv_kernel, start),
        in_specs=[SM, SM, VM, VM],
        out_specs=[VM, VM],
        out_shape=[jax.ShapeDtypeStruct((half, columns), BF16)] * 2,
        compiler_params=params(8),
        cost_estimate=cost(10 * key_value.size, 6 * key_value.size),
        name="finish_kv",
    )(core, live_tiles, key_value, gain)


def query_kernel(line, mask_ref, seq_ref, text_ref, gain_ref, out_ref, flags_ref):
    kv_local, blocks, rows, _ = out_ref.shape
    group = rows // QB
    images = mask_ref.shape[0] // blocks
    lane = lax.broadcasted_iota(jnp.int32, (1, flags_ref.shape[1]), 1)
    for block in range(blocks):
        row = jnp.zeros_like(lane)
        seen = jnp.int32(0)
        for slot in range(images):
            image = seq_ref[0] ^ slot if line else slot
            flag = mask_ref[block * images + image]
            row = jnp.where(lane == slot, flag, row)
            seen = seen + flag
        flags_ref[block : block + 1, :] = row
        flags_ref[blocks + block : blocks + block + 1, :] = jnp.zeros_like(lane) + seen
    gain = gain_ref[...].reshape(1, -1)
    for head in range(kv_local):
        for block in range(blocks):
            for member in range(group):
                at = (head * group + member) * HD
                part = text_ref[block * QB : (block + 1) * QB, at : at + HD].astype(F32)
                out_ref[head, block, member * QB : (member + 1) * QB, :] = (
                    rms_norm(part, gain) * (1.0 / math.sqrt(HD))
                ).astype(BF16)


def norm_queries(line, mask, seq, text, gain, kv_local):
    rows, columns = text.shape
    group = columns // HD // kv_local
    blocks, images = mask.shape
    lanes = -(-images // 128) * 128
    return pl.pallas_call(
        functools.partial(query_kernel, line),
        in_specs=[SM, SM, VM, VM],
        out_specs=[VM, VM],
        out_shape=[
            jax.ShapeDtypeStruct((kv_local, rows // QB, group * QB, HD), BF16),
            jax.ShapeDtypeStruct((2 * blocks, lanes), jnp.int32),
        ],
        compiler_params=params(8),
        cost_estimate=cost(8 * rows * columns, 4 * rows * columns),
        name="norm_queries",
    )(mask.reshape(-1), seq, text, gain)


def cross_kernel(slots, images, first, last, flags_ref, q_ref, *refs):
    flat = sum(count for _, count in slots)
    kv_refs, refs = list(refs[:flat]), refs[flat:]
    refs = refs if first else refs[1:]
    kv_local, blocks, rows, _ = q_ref.shape
    group = rows // QB
    if last:
        out_hbm, acc, vals, out_ref, sems = refs
    else:
        acc, vals = refs

    def wanted(block, image):
        if isinstance(image, int):
            return flags_ref[block : block + 1, image : image + 1][0, 0] > 0
        row = flags_ref[block : block + 1, :]
        lane = lax.broadcasted_iota(jnp.int32, row.shape, 1)
        return jnp.max(jnp.where(lane == image, row, 0)) > 0

    def attend(block, head, member, chunks):
        at = slice(member * QB, (member + 1) * QB)
        keys = [kv[:, head * HD : (head + 1) * HD] for kv in chunks]
        keys = keys[0] if len(keys) == 1 else jnp.concatenate(keys, axis=0)
        sims = lax.dot_general(q_ref[head, block, at, :], keys, NT, preferred_element_type=F32)
        return jnp.dot(jnp.exp(sims).astype(BF16), vals[head], preferred_element_type=F32)

    def one_image(image, chunks, fresh):
        some = functools.reduce(jnp.logical_or, [wanted(block, image) for block in range(blocks)])

        @pl.when(some)
        def _():
            for head in range(kv_local):
                at = 0
                for kv in chunks:
                    values = kv[:, (kv_local + head) * HD : (kv_local + head + 1) * HD]
                    live = values < DEAD * 0.5
                    span = slice(at, at + values.shape[0])
                    vals[head, span, :HD] = jnp.where(live, values, jnp.zeros_like(values))
                    vals[head, span, HD:] = jnp.where(live, 1.0, 0.0).astype(BF16)
                    at += values.shape[0]

        for block in range(blocks):

            @pl.when(wanted(block, image))
            def _(block=block):
                for head in range(kv_local):
                    for member in range(group):
                        at = slice(member * QB, (member + 1) * QB)
                        more = attend(block, head, member, chunks)
                        acc[head, block, at, :] = more if fresh else acc[head, block, at, :] + more

            if fresh:

                @pl.when(jnp.logical_not(wanted(block, image)))
                def _(block=block):
                    acc[:, block] = jnp.zeros((kv_local, rows, 2 * HD), F32)

    if slots[0][0] is None:
        acc[...] = jnp.zeros_like(acc)

        @pl.loop(0, images)
        def _(image):
            one_image(image, [kv_refs[0].at[image]], False)
    else:
        for number, (bits, count) in enumerate(slots):
            one_image(bits, [kv_refs.pop(0) for _ in range(count)], first and number == 0)

    if not last:
        return
    span = group * HD
    copies = {}
    for block in range(blocks):
        seen = flags_ref[blocks + block : blocks + block + 1, :1][0, 0]
        for head in range(kv_local):
            rows_at = slice(block * QB, (block + 1) * QB)
            columns = slice(head * span, (head + 1) * span)

            @pl.when(seen > 0)
            def _(head=head, block=block, rows_at=rows_at):
                for member in range(group):
                    at = slice(member * QB, (member + 1) * QB)
                    column = (head * group + member) * HD
                    out_ref[rows_at, column : column + HD] = (
                        acc[head, block, at, :HD] / acc[head, block, at, HD:]
                    ).astype(BF16)

            @pl.when(seen == 0)
            def _(rows_at=rows_at, columns=columns):
                out_ref[rows_at, columns] = jnp.zeros((QB, span), BF16)

            copies[block, head] = pltpu.make_async_copy(
                out_ref.at[rows_at, columns], out_hbm.at[rows_at, columns], sems.at[block, head]
            )
            copies[block, head].start()
    for copy in copies.values():
        copy.wait()


def cross(images, flags, queries, slots, acc=None, last=True):
    kv_local, blocks, rows, _ = queries.shape
    flat = [chunk for _, chunks in slots for chunk in chunks]
    keys = sum(chunk.shape[-2] for chunk in slots[0][1])
    out = jax.ShapeDtypeStruct((blocks * QB, kv_local * (rows // QB) * HD), BF16)
    work = blocks * rows * sum(kv.size for kv in flat) // (2 * HD)
    sums = (kv_local, blocks, rows, 2 * HD)
    given = [] if acc is None else [acc]
    scratch = [pltpu.VMEM((kv_local, keys, 2 * HD), BF16)]
    if last:
        scratch += [pltpu.VMEM(out.shape, BF16), pltpu.SemaphoreType.DMA((blocks, kv_local))]
    result = pl.pallas_call(
        functools.partial(
            cross_kernel,
            [(bits, len(chunks)) for bits, chunks in slots],
            images,
            acc is None,
            last,
        ),
        in_specs=[VM, VM] + [VM] * len(flat + given),
        out_specs=[HB, VM] if last else [VM],
        out_shape=[out] * last + [jax.ShapeDtypeStruct(sums, F32)],
        scratch_shapes=scratch,
        input_output_aliases={2 + len(flat): int(last)} if given else {},
        compiler_params=params(14),
        cost_estimate=cost(4 * work * HD, 4 * queries.size, work),
        name="cross",
    )(flags, queries, *flat, *given)
    return result[0]


def swap_line(bits, value):
    return lax.ppermute(value, "seq", [(s, s ^ bits) for s in range(8)])


def tie(values, *after):
    return lax.optimization_barrier((tuple(values), after))[0]


def gather_line(blocks, attend):
    images = []
    for block in blocks:
        images.append({0: block, 4: swap_line(4, block), 2: swap_line(2, block)})
    crossed = []

    def swap_x(value):
        if len(crossed) > 1:
            value = tie((value,), crossed[-2])[0]
        crossed.append(swap_line(1, value))
        return crossed[-1]

    def slots(*several):
        return [(bits, [got[bits] for got in images]) for bits in several]

    for got in images:
        got[1] = swap_x(got[0])
    acc = None
    for got, several in zip(images, EARLY):
        acc = attend(slots(*several), acc, False)
        far, near, acc = tie((got[4], got[2], acc))
        got[3] = swap_x(near)
        got[6] = swap_line(2, far)
        got[5] = swap_x(far)
    for number, got in enumerate(images):
        if number == len(images) - 1 and number > 0:
            got[7] = swap_line(2, got[5])
        else:
            got[7] = swap_x(got[6])
    for several in LATE:
        acc = attend(slots(*several), acc, several == LATE[-1])
    return acc


def per_device(
    vis_in,
    live_tiles,
    ln1_gain,
    w_qkv,
    w_out,
    ln2_gain,
    w_fc1,
    w_fc2,
    w_kv,
    k_gain,
    q_gain,
    text_queries,
    block_mask,
):
    head_count = lax.axis_size("head")
    head_index = lax.axis_index("head")
    core = head_index % 2
    core_arg = core.astype(jnp.int32).reshape(1)
    kv_local = KVH // head_count
    swap_core = functools.partial(
        lax.ppermute, axis_name="head", perm=[(i, i ^ 1) for i in range(head_count)]
    )

    def swap_chip(value, bit):
        return lax.ppermute(value, "head", [(i, i ^ bit) for i in range(head_count)])

    def sum_chips(value):
        bit = 2
        other = swap_chip(value, bit)
        while 2 * bit < head_count:
            bit *= 2
            value = (value.astype(F32) + other.astype(F32)).astype(BF16)
            other = swap_chip(value, bit)
        return value, other

    x = vis_in.reshape(vis_in.shape[0] * vis_in.shape[1], vis_in.shape[2])
    rows, width = x.shape
    half = rows // 2
    line = lax.axis_size("seq") == 8
    cuts = [0, half * FIRST // 128, half] if line else [0, half]
    chunks = [slice(at, end) for at, end in zip(cuts, cuts[1:])]
    chip_columns = 2 * kv_local * HD

    seq = lax.axis_index("seq").astype(jnp.int32).reshape(1)
    images = block_mask.shape[1]
    queries, flags = norm_queries(line, block_mask, seq, text_queries, q_gain, kv_local)
    send, kept, own_x = encode(
        core_arg, live_tiles, x, ln1_gain, jnp.swapaxes(w_qkv, 1, 2), w_out
    )
    received = swap_core(send)
    chip_arg = (head_index // 2).astype(jnp.int32).reshape(1)
    first = (kept + received.astype(F32)).astype(BF16)
    w1, w2, w_chip = fetch(chip_arg, w_fc1, w_fc2, w_kv, chip_columns, first)
    first, second = sum_chips(first)
    resid, normed = mid(own_x, first, second, ln2_gain, w_chip, queries)
    other = swap_core(normed)
    keep = mlp(normed, w1, w2, F32)
    received = swap_core(mlp(other, w1, w2, BF16))
    sums = [(keep[at] + received[at].astype(F32)).astype(BF16) for at in chunks]
    sums = [sum_chips(value) for value in sums]
    blocks = []
    for at, (first, second) in zip(chunks, sums):
        second = tie((second,), blocks[-1] if blocks else sums[-1][0])[0]
        vision = (resid[at] + (first.astype(F32) + second.astype(F32))).astype(BF16)
        key_value = jnp.einsum("rc,cjd->jrd", vision, w_chip, preferred_element_type=F32)
        own, send = finish_kv(at.start, core_arg, live_tiles, key_value, k_gain)
        blocks.append(jnp.concatenate([own, swap_core(send)], axis=0))

    if not line:
        stacked = lax.all_gather(jnp.concatenate(blocks, axis=0), "seq", axis=0)
        return cross(images, flags, queries, [(None, [stacked])])
    return gather_line(blocks, functools.partial(cross, images, flags, queries))


def solution(mesh):
    placed = (
        P("seq", None, None),
        P("seq"),
        P(),
        P(None, None, "head"),
        P("head", None),
        P(),
        P(None, "head"),
        P("head", None),
        P(),
        P(),
        P(),
        P("seq", "head"),
        P("seq", None),
    )
    return jax.shard_map(
        per_device, mesh=mesh, in_specs=placed, out_specs=P("seq", "head"), check_vma=False
    )
```

time: 69.7 us -> 66.3 us (0.951)
  Pallas kernels: 25.4 us -> 20.8 us
  waiting for transfers between devices: 22.4 us -> 23.9 us
  starting transfers between devices: 20.2 us -> 19.4 us
    pallas_call x5, Pallas kernels: 12 us -> 7.37 us  [cross(): pl.pallas_call(functools.partial(cross_kernel, [(bits, len(chunks)) for b...]
    ppermute x14, waiting for transfers between devices: 8.58 us -> 10.7 us  [swap_line(): return lax.ppermute(value, 'seq', [(s, s ^ bits) for s in range(8)])]
    ppermute x3, waiting for transfers between devices: 8.56 us -> 7.56 us  [swap_chip(): lax.ppermute(value, 'head', [(i, i ^ bit) for i in range(head_count)])]
    ppermute x3, starting transfers between devices: 5.76 us -> 5.05 us  [swap_chip(): lax.ppermute(value, 'head', [(i, i ^ bit) for i in range(head_count)])]
  transfers between devices with their start and end apart: 23 -> 22, of which waited for: 11 -> 12; matrix products, arithmetic and copies ran while one was open for 2% -> 2% of each run, Pallas kernels for 21% -> 19%
where the time goes in v3:
time: 66.3 us; the launch traced here: 66.6 us
  waiting for transfers between devices  23.9 us (36%)
  Pallas kernels  20.8 us (31%)
  starting transfers between devices  19.4 us (29%)
  between operations  1.13 us (2%)
  matrix products  1.07 us (2%)
    ppermute x14, starting transfers between devices, swap_line(): return lax.ppermute(value, 'seq', [(s, s ^ bits) for s in range(8)])  13.5 us
    ppermute x14, waiting for transfers between devices, swap_line(): return lax.ppermute(value, 'seq', [(s, s ^ bits) for s in range(8)])  10.7 us
    ppermute x3, waiting for transfers between devices, swap_chip(): lax.ppermute(value, 'head', [(i, i ^ bit) for i in range(head_count)])  7.56 us
    pallas_call x5, Pallas kernels, cross(): pl.pallas_call(functools.partial(cross_kernel, [(bits, len(chunks)) for b...  7.37 us
    pallas_call x1, Pallas kernels, encode(): pl.pallas_call(encode_kernel, in_specs=[SM, SM, HB, HB, HB, HB], out_spec...  5.15 us
    ppermute x3, starting transfers between devices, swap_chip(): lax.ppermute(value, 'head', [(i, i ^ bit) for i in range(head_count)])  5.05 us
    pallas_call x1, Pallas kernels, fetch(): pl.pallas_call(fetch_kernel, in_specs=[SM, HB, HB, HB, AN], out_specs=[VM...  3.71 us
    ppermute x2, waiting for transfers between devices, per_device(): blocks.append(jnp.concatenate([own, swap_core(send)], axis=0))  2.45 us
  transfers between devices with their start and end apart: 22, of which 12 were waited for; matrix products, arithmetic and copies ran while one was open for 2% of the time, Pallas kernels for 19%

profile of v3, /device:TPU:0, one launch (start us, length us, event | category | flops | bytes accessed | tf_op | source)
XLA Modules:
  0.0 66.6 jit_solution(1535085326899239618)
XLA Ops:
  0.8 5.1 %encode.1 = (bf16[128,1280]{1,0:T(8,128)(2,1)S(1)}, f32[128,1280]{1,0:T(8,128)S(1)}, bf16[128,1280]{1,0:T(8,128)(2,1)S(1)}) custom-call(s32[1]{0:T(128)} %bitcast.1.core_ref, s32[1]{0:T(128)S(6)} %copy.34.live_ref, f32[1280]{0:T(1024)} %gain_hbm.1, bf16[256,1280]{1,0:T(8,128)(2,1)} %bitcast.16, bf16[3,320,1280]{2,1,0:T(8,128)(2,1)} %bitcast.15, ...), custom_call_target="tpu_custom_call" | custom-call | flops 838860800 | bytes 3276800 | tf_op jit(solution)/shard_map/encode/pallas_call | solution.py:116
  6.4 1.3 %collective-permute-done = bf16[128,1280]{1,0:T(8,128)(2,1)S(1)} collective-permute-done((bf16[128,1280]{1,0:T(8,128)(2,1)S(1)}, bf16[128,1280]{1,0:T(8,128)(2,1)S(1)}, u32[]{:S(2)}, u32[]{:S(2)}) %collective-permute-start) | collective-permute-done | bytes 327712 | tf_op jit(solution)/shard_map/ppermute | solution.py:508
  7.7 3.0 %collective-permute-start.1 = (bf16[128,1280]{1,0:T(8,128)(2,1)S(1)}, bf16[128,1280]{1,0:T(8,128)(2,1)S(1)}, u32[]{:S(2)}, u32[]{:S(2)}) collective-permute-start(bf16[128,1280]{1,0:T(8,128)(2,1)S(1)} %add_convert_fusion._.first_ref), channel_id=1, source_target_pairs={{0,2},{1,3},{2,0},{3,1},{4,6},{5,7},{6,4},{7,5},{8,10},{9,11},{10,... | collective-permute-start | bytes 983048 | tf_op jit(solution)/shard_map/ppermute | solution.py:483
  10.8 1.6 %norm_queries.1 = (bf16[2,2,1024,128]{3,2,1,0:T(8,128)(2,1)S(1)}, s32[4,128]{1,0:T(4,128)S(1)}) custom-call(s32[16]{0:T(128)S(1)} %reshape.15.mask_ref, s32[1]{0:T(128)} %bitcast.seq_ref, bf16[256,2048]{1,0:T(8,128)(2,1)S(1)} %copy-done, f32[128]{0:T(128)S(1)} %copy-done.3), custom_call_target="tpu_custom_call" | custom-call | flops 4194304 | bytes 2097152 | tf_op jit(solution)/shard_map/norm_queries/pallas_call | solution.py:274
  12.5 3.7 %fetch.1 = (bf16[1280,1280]{1,0:T(8,128)(2,1)S(1)}, bf16[1280,1280]{1,0:T(8,128)(2,1)S(1)}, bf16[1280,2,512]{2,1,0:T(2,128)(2,1)S(1)}) custom-call(s32[1]{0:T(128)} %bitcast.2.chip_ref, bf16[1280,1280]{1,0:T(8,128)(2,1)} %w1_hbm.1, bf16[1280,1280]{1,0:T(8,128)(2,1)} %w2_hbm.1, bf16[1280,2,1024]{2,1,0:T(2,128)(2,1)} %wkv_hbm.1, ...), custom_call_target="tpu_custom_call" | custom-call | bytes 32768000 | tf_op jit(solution)/shard_map/fetch/pallas_call | solution.py:177
  16.2 2.5 %collective-permute-done.1.second_ref = bf16[128,1280]{1,0:T(8,128)(2,1)S(1)} collective-permute-done((bf16[128,1280]{1,0:T(8,128)(2,1)S(1)}, bf16[128,1280]{1,0:T(8,128)(2,1)S(1)}, u32[]{:S(2)}, u32[]{:S(2)}) %collective-permute-start.1) | collective-permute-done | bytes 327712 | tf_op jit(solution)/shard_map/ppermute | solution.py:483
  19.1 1.6 %collective-permute-done.2.normed_ref = bf16[128,1280]{1,0:T(8,128)(2,1)S(1)} collective-permute-done((bf16[128,1280]{1,0:T(8,128)(2,1)S(1)}, bf16[128,1280]{1,0:T(8,128)(2,1)S(1)}, u32[]{:S(2)}, u32[]{:S(2)}) %collective-permute-start.2) | collective-permute-done | bytes 327712 | tf_op jit(solution)/shard_map/ppermute | solution.py:514
  23.7 1.8 %collective-permute-start.4 = (bf16[64,1280]{1,0:T(8,128)(2,1)S(1)}, bf16[64,1280]{1,0:T(8,128)(2,1)S(1)}, u32[]{:S(2)}, u32[]{:S(2)}) collective-permute-start(bf16[64,1280]{1,0:T(8,128)(2,1)S(1)} %get-tuple-element.62), channel_id=1, source_target_pairs={{0,2},{1,3},{2,0},{3,1},{4,6},{5,7},{6,4},{7,5},{8,10},{9,11},{10,... | collective-permute-start | bytes 491528 | tf_op jit(solution)/shard_map/ppermute | solution.py:483
  25.8 5.0 %collective-permute-done.4 = bf16[64,1280]{1,0:T(8,128)(2,1)S(1)} collective-permute-done((bf16[64,1280]{1,0:T(8,128)(2,1)S(1)}, bf16[64,1280]{1,0:T(8,128)(2,1)S(1)}, u32[]{:S(2)}, u32[]{:S(2)}) %collective-permute-start.4) | collective-permute-done | bytes 163872 | tf_op jit(solution)/shard_map/ppermute | solution.py:483
  32.8 1.7 %collective-permute-start.13 = (bf16[128,512]{1,0:T(8,128)(2,1)S(1)}, bf16[128,512]{1,0:T(8,128)(2,1)S(1)}, u32[]{:S(2)}, u32[]{:S(2)}) collective-permute-start(bf16[128,512]{1,0:T(8,128)(2,1)S(1)} %constant_dynamic-update-slice_fusion.refs_0_), channel_id=1, source_target_pairs={{0,4},{4,0},{8,12},{12,8},{16,20},{20,16},{24,28},{28,24},{1,5},{5... | collective-permute-start | bytes 393224 | tf_op jit(solution)/shard_map/ppermute | solution.py:417
  34.5 1.6 %collective-permute-start.7 = (bf16[128,512]{1,0:T(8,128)(2,1)S(1)}, bf16[128,512]{1,0:T(8,128)(2,1)S(1)}, u32[]{:S(2)}, u32[]{:S(2)}) collective-permute-start(bf16[128,512]{1,0:T(8,128)(2,1)S(1)} %constant_dynamic-update-slice_fusion.refs_0_), channel_id=1, source_target_pairs={{0,8},{4,12},{8,0},{12,4},{16,24},{20,28},{24,16},{28,20},{1,9},{5... | collective-permute-start | bytes 393224 | tf_op jit(solution)/shard_map/ppermute | solution.py:417
  36.1 2.6 %collective-permute-start.6 = (bf16[128,512]{1,0:T(8,128)(2,1)S(1)}, bf16[128,512]{1,0:T(8,128)(2,1)S(1)}, u32[]{:S(2)}, u32[]{:S(2)}) collective-permute-start(bf16[128,512]{1,0:T(8,128)(2,1)S(1)} %constant_dynamic-update-slice_fusion.refs_0_), channel_id=1, source_target_pairs={{0,16},{4,20},{8,24},{12,28},{16,0},{20,4},{24,8},{28,12},{1,17},{... | collective-permute-start | bytes 393224 | tf_op jit(solution)/shard_map/ppermute | solution.py:417
  39.5 1.2 %collective-permute-done.9 = bf16[64,512]{1,0:T(8,128)(2,1)S(1)} collective-permute-done((bf16[64,512]{1,0:T(8,128)(2,1)S(1)}, bf16[64,512]{1,0:T(8,128)(2,1)S(1)}, u32[]{:S(2)}, u32[]{:S(2)}) %collective-permute-start.9) | collective-permute-done | bytes 65568 | tf_op jit(solution)/shard_map/ppermute | solution.py:525
  44.2 1.2 %collective-permute-start.15 = (bf16[128,512]{1,0:T(8,128)(2,1)S(1)}, bf16[128,512]{1,0:T(8,128)(2,1)S(1)}, u32[]{:S(2)}, u32[]{:S(2)}) collective-permute-start(bf16[128,512]{1,0:T(8,128)(2,1)S(1)} %collective-permute-done.7.refs_0_), channel_id=1, source_target_pairs={{0,4},{4,0},{8,12},{12,8},{16,20},{20,16},{24,28},{28,24},{1,5},{5... | collective-permute-start | bytes 393224 | tf_op jit(solution)/shard_map/ppermute | solution.py:417
  45.4 1.7 %collective-permute-done.14.refs_3_ = bf16[128,512]{1,0:T(8,128)(2,1)S(1)} collective-permute-done((bf16[128,512]{1,0:T(8,128)(2,1)S(1)}, bf16[128,512]{1,0:T(8,128)(2,1)S(1)}, u32[]{:S(2)}, u32[]{:S(2)}) %collective-permute-start.14) | collective-permute-done | bytes 131104 | tf_op jit(solution)/shard_map/ppermute | solution.py:417
  48.7 1.7 %cross.6.refs_4_ = f32[2,2,1024,256]{3,2,1,0:T(8,128)S(1)} custom-call(s32[4,128]{1,0:T(4,128)S(1)} %get-tuple-element.33.flags_ref, bf16[2,2,1024,128]{3,2,1,0:T(8,128)(2,1)S(1)} %get-tuple-element.34.__.q_ref, bf16[128,512]{1,0:T(8,128)(2,1)S(1)} %collective-permute-done.7.refs_0_, ...), custom_call_target="tpu_custom_call", output_to_operand_aliasing={{}: (6, {})} | custom-call | flops 1073741824 | bytes 2097152 | tf_op jit(solution)/shard_map/cross/pallas_call | solution.py:396
  50.4 1.4 %collective-permute-done.11.refs_1_ = bf16[128,512]{1,0:T(8,128)(2,1)S(1)} collective-permute-done((bf16[128,512]{1,0:T(8,128)(2,1)S(1)}, bf16[128,512]{1,0:T(8,128)(2,1)S(1)}, u32[]{:S(2)}, u32[]{:S(2)}) %collective-permute-start.11) | collective-permute-done | bytes 131104 | tf_op jit(solution)/shard_map/ppermute | solution.py:417
  52.6 1.2 %collective-permute-start.19 = (bf16[128,512]{1,0:T(8,128)(2,1)S(1)}, bf16[128,512]{1,0:T(8,128)(2,1)S(1)}, u32[]{:S(2)}, u32[]{:S(2)}) collective-permute-start(bf16[128,512]{1,0:T(8,128)(2,1)S(1)} %collective-permute-done.11.refs_1_), channel_id=1, source_target_pairs={{0,4},{4,0},{8,12},{12,8},{16,20},{20,16},{24,28},{28,24},{1,5},{5... | collective-permute-start | bytes 393224 | tf_op jit(solution)/shard_map/ppermute | solution.py:417
  53.9 3.7 %collective-permute-done.16.refs_3_ = bf16[128,512]{1,0:T(8,128)(2,1)S(1)} collective-permute-done((bf16[128,512]{1,0:T(8,128)(2,1)S(1)}, bf16[128,512]{1,0:T(8,128)(2,1)S(1)}, u32[]{:S(2)}, u32[]{:S(2)}) %collective-permute-start.16) | collective-permute-done | bytes 131104 | tf_op jit(solution)/shard_map/ppermute | solution.py:417
  58.1 2.0 %collective-permute-done.19.refs_1_ = bf16[128,512]{1,0:T(8,128)(2,1)S(1)} collective-permute-done((bf16[128,512]{1,0:T(8,128)(2,1)S(1)}, bf16[128,512]{1,0:T(8,128)(2,1)S(1)}, u32[]{:S(2)}, u32[]{:S(2)}) %collective-permute-start.19) | collective-permute-done | bytes 131104 | tf_op jit(solution)/shard_map/ppermute | solution.py:417
  60.1 1.5 %cross.7.refs_4_ = f32[2,2,1024,256]{3,2,1,0:T(8,128)S(1)} custom-call(s32[4,128]{1,0:T(4,128)S(1)} %get-tuple-element.33.flags_ref, bf16[2,2,1024,128]{3,2,1,0:T(8,128)(2,1)S(1)} %get-tuple-element.34.__.q_ref, bf16[128,512]{1,0:T(8,128)(2,1)S(1)} %collective-permute-done.6.refs_0_, ...), custom_call_target="tpu_custom_call", output_to_operand_aliasing={{}: (6, {})} | custom-call | flops 1073741824 | bytes 2097152 | tf_op jit(solution)/shard_map/cross/pallas_call | solution.py:396
  61.6 1.5 %cross.8.refs_2_ = f32[2,2,1024,256]{3,2,1,0:T(8,128)S(1)} custom-call(s32[4,128]{1,0:T(4,128)S(1)} %get-tuple-element.33.flags_ref, bf16[2,2,1024,128]{3,2,1,0:T(8,128)(2,1)S(1)} %get-tuple-element.34.__.q_ref, bf16[128,512]{1,0:T(8,128)(2,1)S(1)} %collective-permute-done.18.refs_0_, ...), custom_call_target="tpu_custom_call", output_to_operand_aliasing={{}: (6, {})} | custom-call | flops 1073741824 | bytes 2097152 | tf_op jit(solution)/shard_map/cross/pallas_call | solution.py:396
  63.2 1.9 %collective-permute-done.20.refs_1_ = bf16[128,512]{1,0:T(8,128)(2,1)S(1)} collective-permute-done((bf16[128,512]{1,0:T(8,128)(2,1)S(1)}, bf16[128,512]{1,0:T(8,128)(2,1)S(1)}, u32[]{:S(2)}, u32[]{:S(2)}) %collective-permute-start.20) | collective-permute-done | bytes 131104 | tf_op jit(solution)/shard_map/ppermute | solution.py:417
  65.0 1.4 %cross.9 = (bf16[256,2048]{1,0:T(8,128)(2,1)}, f32[2,2,1024,256]{3,2,1,0:T(8,128)S(1)}) custom-call(s32[4,128]{1,0:T(4,128)S(1)} %get-tuple-element.33.flags_ref, bf16[2,2,1024,128]{3,2,1,0:T(8,128)(2,1)S(1)} %get-tuple-element.34.__.q_ref, bf16[128,512]{1,0:T(8,128)(2,1)S(1)} %collective-permute-done.17.refs_0_, ...), custom_call_target="tpu_custom_call", output_to_operand_aliasing={{1}: (4, {})} | custom-call | flops 536870912 | bytes 2097152 | tf_op jit(solution)/shard_map/cross/pallas_call | solution.py:396
  (52 shorter events, 13.4 us)
Async XLA Ops:
  0.0 10.8 %copy-start = (bf16[256,2048]{1,0:T(8,128)(2,1)S(1)}, bf16[256,2048]{1,0:T(8,128)(2,1)}, u32[]{:S(2)}) copy-start(bf16[256,2048]{1,0:T(8,128)(2,1)} %text_ref.1) | copy-start | bytes 3145732
  0.0 10.8 %copy-start.3 = (f32[128]{0:T(128)S(1)}, f32[128]{0:T(128)}, u32[]{:S(2)}) copy-start(f32[128]{0:T(128)} %gain_ref.4) | copy-start | bytes 1540
  5.9 1.8 %collective-permute-start = (bf16[128,1280]{1,0:T(8,128)(2,1)S(1)}, bf16[128,1280]{1,0:T(8,128)(2,1)S(1)}, u32[]{:S(2)}, u32[]{:S(2)}) collective-permute-start(bf16[128,1280]{1,0:T(8,128)(2,1)S(1)} %get-tuple-element.36), channel_id=1, source_target_pairs={{0,1},{1,0},{2,3},{3,2},{4,5},{5,4},{6,7},{7,6},{8,9},{9,8},{10,11... | collective-permute-start | bytes 983048 | tf_op jit(solution)/shard_map/ppermute | solution.py:508
  7.7 11.0 %collective-permute-start.1 = (bf16[128,1280]{1,0:T(8,128)(2,1)S(1)}, bf16[128,1280]{1,0:T(8,128)(2,1)S(1)}, u32[]{:S(2)}, u32[]{:S(2)}) collective-permute-start(bf16[128,1280]{1,0:T(8,128)(2,1)S(1)} %add_convert_fusion._.first_ref), channel_id=1, source_target_pairs={{0,2},{1,3},{2,0},{3,1},{4,6},{5,7},{6,4},{7,5},{8,10},{9,11},{10,... | collective-permute-start | bytes 983048 | tf_op jit(solution)/shard_map/ppermute | solution.py:483
  19.0 1.7 %collective-permute-start.2 = (bf16[128,1280]{1,0:T(8,128)(2,1)S(1)}, bf16[128,1280]{1,0:T(8,128)(2,1)S(1)}, u32[]{:S(2)}, u32[]{:S(2)}) collective-permute-start(bf16[128,1280]{1,0:T(8,128)(2,1)S(1)} %get-tuple-element.40.normed_ref), channel_id=1, source_target_pairs={{0,1},{1,0},{2,3},{3,2},{4,5},{5,4},{6,7},{7,6},{8,9},{9,8},{10,11... | collective-permute-start | bytes 983048 | tf_op jit(solution)/shard_map/ppermute | solution.py:514
  21.9 1.7 %collective-permute-start.3 = (bf16[128,1280]{1,0:T(8,128)(2,1)S(1)}, bf16[128,1280]{1,0:T(8,128)(2,1)S(1)}, u32[]{:S(2)}, u32[]{:S(2)}) collective-permute-start(bf16[128,1280]{1,0:T(8,128)(2,1)S(1)} %mlp.3), channel_id=1, source_target_pairs={{0,1},{1,0},{2,3},{3,2},{4,5},{5,4},{6,7},{7,6},{8,9},{9,8},{10,11... | collective-permute-start | bytes 983048 | tf_op jit(solution)/shard_map/ppermute | solution.py:516
  23.7 7.1 %collective-permute-start.4 = (bf16[64,1280]{1,0:T(8,128)(2,1)S(1)}, bf16[64,1280]{1,0:T(8,128)(2,1)S(1)}, u32[]{:S(2)}, u32[]{:S(2)}) collective-permute-start(bf16[64,1280]{1,0:T(8,128)(2,1)S(1)} %get-tuple-element.62), channel_id=1, source_target_pairs={{0,2},{1,3},{2,0},{3,1},{4,6},{5,7},{6,4},{7,5},{8,10},{9,11},{10,... | collective-permute-start | bytes 491528 | tf_op jit(solution)/shard_map/ppermute | solution.py:483
  25.5 13.2 %collective-permute-start.8 = (bf16[64,1280]{1,0:T(8,128)(2,1)S(1)}, bf16[64,1280]{1,0:T(8,128)(2,1)S(1)}, u32[]{:S(2)}, u32[]{:S(2)}) collective-permute-start(bf16[64,1280]{1,0:T(8,128)(2,1)S(1)} %get-tuple-element.61), channel_id=1, source_target_pairs={{0,2},{1,3},{2,0},{3,1},{4,6},{5,7},{6,4},{7,5},{8,10},{9,11},{10,... | collective-permute-start | bytes 491528 | tf_op jit(solution)/shard_map/ppermute | solution.py:483
  31.5 1.3 %collective-permute-start.5 = (bf16[64,512]{1,0:T(8,128)(2,1)S(1)}, bf16[64,512]{1,0:T(8,128)(2,1)S(1)}, u32[]{:S(2)}, u32[]{:S(2)}) collective-permute-start(bf16[64,512]{1,0:T(8,128)(2,1)S(1)} %get-tuple-element.45), channel_id=1, source_target_pairs={{0,1},{1,0},{2,3},{3,2},{4,5},{5,4},{6,7},{7,6},{8,9},{9,8},{10,11... | collective-permute-start | bytes 196616 | tf_op jit(solution)/shard_map/ppermute | solution.py:525
  32.8 11.3 %collective-permute-start.13 = (bf16[128,512]{1,0:T(8,128)(2,1)S(1)}, bf16[128,512]{1,0:T(8,128)(2,1)S(1)}, u32[]{:S(2)}, u32[]{:S(2)}) collective-permute-start(bf16[128,512]{1,0:T(8,128)(2,1)S(1)} %constant_dynamic-update-slice_fusion.refs_0_), channel_id=1, source_target_pairs={{0,4},{4,0},{8,12},{12,8},{16,20},{20,16},{24,28},{28,24},{1,5},{5... | collective-permute-start | bytes 393224 | tf_op jit(solution)/shard_map/ppermute | solution.py:417
  34.5 8.4 %collective-permute-start.7 = (bf16[128,512]{1,0:T(8,128)(2,1)S(1)}, bf16[128,512]{1,0:T(8,128)(2,1)S(1)}, u32[]{:S(2)}, u32[]{:S(2)}) collective-permute-start(bf16[128,512]{1,0:T(8,128)(2,1)S(1)} %constant_dynamic-update-slice_fusion.refs_0_), channel_id=1, source_target_pairs={{0,8},{4,12},{8,0},{12,4},{16,24},{20,28},{24,16},{28,20},{1,9},{5... | collective-permute-start | bytes 393224 | tf_op jit(solution)/shard_map/ppermute | solution.py:417
  36.1 8.1 %collective-permute-start.6 = (bf16[128,512]{1,0:T(8,128)(2,1)S(1)}, bf16[128,512]{1,0:T(8,128)(2,1)S(1)}, u32[]{:S(2)}, u32[]{:S(2)}) collective-permute-start(bf16[128,512]{1,0:T(8,128)(2,1)S(1)} %constant_dynamic-update-slice_fusion.refs_0_), channel_id=1, source_target_pairs={{0,16},{4,20},{8,24},{12,28},{16,0},{20,4},{24,8},{28,12},{1,17},{... | collective-permute-start | bytes 393224 | tf_op jit(solution)/shard_map/ppermute | solution.py:417
  39.4 1.3 %collective-permute-start.9 = (bf16[64,512]{1,0:T(8,128)(2,1)S(1)}, bf16[64,512]{1,0:T(8,128)(2,1)S(1)}, u32[]{:S(2)}, u32[]{:S(2)}) collective-permute-start(bf16[64,512]{1,0:T(8,128)(2,1)S(1)} %get-tuple-element.48), channel_id=1, source_target_pairs={{0,1},{1,0},{2,3},{3,2},{4,5},{5,4},{6,7},{7,6},{8,9},{9,8},{10,11... | collective-permute-start | bytes 196616 | tf_op jit(solution)/shard_map/ppermute | solution.py:525
  40.7 6.3 %collective-permute-start.14 = (bf16[128,512]{1,0:T(8,128)(2,1)S(1)}, bf16[128,512]{1,0:T(8,128)(2,1)S(1)}, u32[]{:S(2)}, u32[]{:S(2)}) collective-permute-start(bf16[128,512]{1,0:T(8,128)(2,1)S(1)} %constant_dynamic-update-slice_fusion.2.refs_1_), channel_id=1, source_target_pairs={{0,4},{4,0},{8,12},{12,8},{16,20},{20,16},{24,28},{28,24},{1,5},{5... | collective-permute-start | bytes 393224 | tf_op jit(solution)/shard_map/ppermute | solution.py:417
  41.3 7.4 %collective-permute-start.12 = (bf16[128,512]{1,0:T(8,128)(2,1)S(1)}, bf16[128,512]{1,0:T(8,128)(2,1)S(1)}, u32[]{:S(2)}, u32[]{:S(2)}) collective-permute-start(bf16[128,512]{1,0:T(8,128)(2,1)S(1)} %constant_dynamic-update-slice_fusion.2.refs_1_), channel_id=1, source_target_pairs={{0,8},{4,12},{8,0},{12,4},{16,24},{20,28},{24,16},{28,20},{1,9},{5... | collective-permute-start | bytes 393224 | tf_op jit(solution)/shard_map/ppermute | solution.py:417
  42.9 8.9 %collective-permute-start.11 = (bf16[128,512]{1,0:T(8,128)(2,1)S(1)}, bf16[128,512]{1,0:T(8,128)(2,1)S(1)}, u32[]{:S(2)}, u32[]{:S(2)}) collective-permute-start(bf16[128,512]{1,0:T(8,128)(2,1)S(1)} %constant_dynamic-update-slice_fusion.2.refs_1_), channel_id=1, source_target_pairs={{0,16},{4,20},{8,24},{12,28},{16,0},{20,4},{24,8},{28,12},{1,17},{... | collective-permute-start | bytes 393224 | tf_op jit(solution)/shard_map/ppermute | solution.py:417
  44.2 7.7 %collective-permute-start.15 = (bf16[128,512]{1,0:T(8,128)(2,1)S(1)}, bf16[128,512]{1,0:T(8,128)(2,1)S(1)}, u32[]{:S(2)}, u32[]{:S(2)}) collective-permute-start(bf16[128,512]{1,0:T(8,128)(2,1)S(1)} %collective-permute-done.7.refs_0_), channel_id=1, source_target_pairs={{0,4},{4,0},{8,12},{12,8},{16,20},{20,16},{24,28},{28,24},{1,5},{5... | collective-permute-start | bytes 393224 | tf_op jit(solution)/shard_map/ppermute | solution.py:417
  47.1 5.5 %collective-permute-start.18 = (bf16[128,512]{1,0:T(8,128)(2,1)S(1)}, bf16[128,512]{1,0:T(8,128)(2,1)S(1)}, u32[]{:S(2)}, u32[]{:S(2)}) collective-permute-start(bf16[128,512]{1,0:T(8,128)(2,1)S(1)} %collective-permute-done.6.refs_0_), channel_id=1, source_target_pairs={{0,4},{4,0},{8,12},{12,8},{16,20},{20,16},{24,28},{28,24},{1,5},{5... | collective-permute-start | bytes 393224 | tf_op jit(solution)/shard_map/ppermute | solution.py:417
  47.6 6.3 %collective-permute-start.10 = (bf16[128,512]{1,0:T(8,128)(2,1)S(1)}, bf16[128,512]{1,0:T(8,128)(2,1)S(1)}, u32[]{:S(2)}, u32[]{:S(2)}) collective-permute-start(bf16[128,512]{1,0:T(8,128)(2,1)S(1)} %collective-permute-done.6.refs_0_), channel_id=1, source_target_pairs={{0,8},{4,12},{8,0},{12,4},{16,24},{20,28},{24,16},{28,20},{1,9},{5... | collective-permute-start | bytes 393224 | tf_op jit(solution)/shard_map/ppermute | solution.py:417
  51.8 5.8 %collective-permute-start.16 = (bf16[128,512]{1,0:T(8,128)(2,1)S(1)}, bf16[128,512]{1,0:T(8,128)(2,1)S(1)}, u32[]{:S(2)}, u32[]{:S(2)}) collective-permute-start(bf16[128,512]{1,0:T(8,128)(2,1)S(1)} %collective-permute-done.12.refs_1_), channel_id=1, source_target_pairs={{0,4},{4,0},{8,12},{12,8},{16,20},{20,16},{24,28},{28,24},{1,5},{5... | collective-permute-start | bytes 393224 | tf_op jit(solution)/shard_map/ppermute | solution.py:417
  52.6 7.5 %collective-permute-start.19 = (bf16[128,512]{1,0:T(8,128)(2,1)S(1)}, bf16[128,512]{1,0:T(8,128)(2,1)S(1)}, u32[]{:S(2)}, u32[]{:S(2)}) collective-permute-start(bf16[128,512]{1,0:T(8,128)(2,1)S(1)} %collective-permute-done.11.refs_1_), channel_id=1, source_target_pairs={{0,4},{4,0},{8,12},{12,8},{16,20},{20,16},{24,28},{28,24},{1,5},{5... | collective-permute-start | bytes 393224 | tf_op jit(solution)/shard_map/ppermute | solution.py:417
  53.9 7.8 %collective-permute-start.21 = (bf16[128,512]{1,0:T(8,128)(2,1)S(1)}, bf16[128,512]{1,0:T(8,128)(2,1)S(1)}, u32[]{:S(2)}, u32[]{:S(2)}) collective-permute-start(bf16[128,512]{1,0:T(8,128)(2,1)S(1)} %collective-permute-done.11.refs_1_), channel_id=1, source_target_pairs={{0,8},{4,12},{8,0},{12,4},{16,24},{20,28},{24,16},{28,20},{1,9},{5... | collective-permute-start | bytes 393224 | tf_op jit(solution)/shard_map/ppermute | solution.py:417
  57.6 5.6 %collective-permute-start.17 = (bf16[128,512]{1,0:T(8,128)(2,1)S(1)}, bf16[128,512]{1,0:T(8,128)(2,1)S(1)}, u32[]{:S(2)}, u32[]{:S(2)}) collective-permute-start(bf16[128,512]{1,0:T(8,128)(2,1)S(1)} %collective-permute-done.10.refs_2_), channel_id=1, source_target_pairs={{0,4},{4,0},{8,12},{12,8},{16,20},{20,16},{24,28},{28,24},{1,5},{5... | collective-permute-start | bytes 393224 | tf_op jit(solution)/shard_map/ppermute | solution.py:417
  60.1 5.0 %collective-permute-start.20 = (bf16[128,512]{1,0:T(8,128)(2,1)S(1)}, bf16[128,512]{1,0:T(8,128)(2,1)S(1)}, u32[]{:S(2)}, u32[]{:S(2)}) collective-permute-start(bf16[128,512]{1,0:T(8,128)(2,1)S(1)} %collective-permute-done.19.refs_1_), channel_id=1, source_target_pairs={{0,8},{4,12},{8,0},{12,4},{16,24},{20,28},{24,16},{28,20},{1,9},{5... | collective-permute-start | bytes 393224 | tf_op jit(solution)/shard_map/ppermute | solution.py:417
  (3 other events, 25.0 us)

commit v4 on v3

--- a/solution.py
+++ b/solution.py
@@ -240,7 +240,7 @@
     )(core, live_tiles, key_value, gain)
 
 
-def query_kernel(line, mask_ref, seq_ref, text_ref, gain_ref, out_ref, flags_ref):
+def query_kernel(line, mask_ref, seq_ref, core_ref, text_ref, gain_ref, out_ref, flags_ref):
     kv_local, blocks, rows, _ = out_ref.shape
     group = rows // QB
     images = mask_ref.shape[0] // blocks
@@ -249,7 +249,10 @@
         row = jnp.zeros_like(lane)
         seen = jnp.int32(0)
         for slot in range(images):
-            image = seq_ref[0] ^ slot if line else slot
+            image = slot
+            if line:
+                turned = (slot & 4) | (slot & 1) << 1 | (slot & 2) >> 1
+                image = seq_ref[0] ^ jnp.where(core_ref[0] == 0, slot, turned)
             flag = mask_ref[block * images + image]
             row = jnp.where(lane == slot, flag, row)
             seen = seen + flag
@@ -266,14 +269,14 @@
                 ).astype(BF16)
 
 
-def norm_queries(line, mask, seq, text, gain, kv_local):
+def norm_queries(line, mask, seq, core, text, gain, kv_local):
     rows, columns = text.shape
     group = columns // HD // kv_local
     blocks, images = mask.shape
     lanes = -(-images // 128) * 128
     return pl.pallas_call(
         functools.partial(query_kernel, line),
-        in_specs=[SM, SM, VM, VM],
+        in_specs=[SM, SM, SM, VM, VM],
         out_specs=[VM, VM],
         out_shape=[
             jax.ShapeDtypeStruct((kv_local, rows // QB, group * QB, HD), BF16),
@@ -282,7 +285,7 @@
         compiler_params=params(8),
         cost_estimate=cost(8 * rows * columns, 4 * rows * columns),
         name="norm_queries",
-    )(mask.reshape(-1), seq, text, gain)
+    )(mask.reshape(-1), seq, core, text, gain)
 
 
 def cross_kernel(slots, images, first, last, flags_ref, q_ref, *refs):
@@ -413,8 +416,14 @@
     return result[0]
 
 
-def swap_line(bits, value):
-    return lax.ppermute(value, "seq", [(s, s ^ bits) for s in range(8)])
+def swap_line(value, even, odd):
+    heads = lax.axis_size("head")
+    pairs = []
+    for seq in range(lax.axis_size("seq")):
+        for head in range(heads):
+            other = seq ^ (odd if head % 2 else even)
+            pairs.append((seq * heads + head, other * heads + head))
+    return lax.ppermute(value, ("seq", "head"), pairs)
 
 
 def tie(values, *after):
@@ -422,36 +431,34 @@
 
 
 def gather_line(blocks, attend):
-    images = []
-    for block in blocks:
-        images.append({0: block, 4: swap_line(4, block), 2: swap_line(2, block)})
     crossed = []
 
-    def swap_x(value):
+    def one(value):
         if len(crossed) > 1:
             value = tie((value,), crossed[-2])[0]
-        crossed.append(swap_line(1, value))
+        crossed.append(swap_line(value, 1, 2))
         return crossed[-1]
+
+    def two(value):
+        return swap_line(value, 2, 1)
 
     def slots(*several):
         return [(bits, [got[bits] for got in images]) for bits in several]
 
+    images = [{0: block, 4: swap_line(block, 4, 4)} for block in blocks]
     for got in images:
-        got[1] = swap_x(got[0])
+        got[1] = one(got[0])
+    for got in images:
+        got[2] = two(got[0])
+    for got in images:
+        got[6] = two(got[4])
+        got[5] = one(got[4])
+        got[3] = one(got[2])
+    images[0][7] = one(images[0][6])
+    images[1][7] = two(images[1][5])
     acc = None
-    for got, several in zip(images, EARLY):
-        acc = attend(slots(*several), acc, False)
-        far, near, acc = tie((got[4], got[2], acc))
-        got[3] = swap_x(near)
-        got[6] = swap_line(2, far)
-        got[5] = swap_x(far)
-    for number, got in enumerate(images):
-        if number == len(images) - 1 and number > 0:
-            got[7] = swap_line(2, got[5])
-        else:
-            got[7] = swap_x(got[6])
-    for several in LATE:
-        acc = attend(slots(*several), acc, several == LATE[-1])
+    for several in ((0,), (2, 1), (4, 3), (5, 6), (7,)):
+        acc = attend(slots(*several), acc, several == (7,))
     return acc
 
 
@@ -501,7 +508,7 @@
 
     seq = lax.axis_index("seq").astype(jnp.int32).reshape(1)
     images = block_mask.shape[1]
-    queries, flags = norm_queries(line, block_mask, seq, text_queries, q_gain, kv_local)
+    queries, flags = norm_queries(line, block_mask, seq, core_arg, text_queries, q_gain, kv_local)
     send, kept, own_x = encode(
         core_arg, live_tiles, x, ln1_gain, jnp.swapaxes(w_qkv, 1, 2), w_out
     )

time: 66.3 us -> 66.6 us (level); the launches traced: 66.6 us -> 65.3 us
  Pallas kernels: 20.8 us -> 18.4 us
  waiting for transfers between devices: 23.9 us -> 24.7 us
    pallas_call x5, Pallas kernels: 7.37 us -> 4.89 us  [cross(): pl.pallas_call(functools.partial(cross_kernel, [(bits, len(chunks)) for b...]
    ppermute x14, waiting for transfers between devices: 10.7 us -> 11.5 us  [swap_line(): return lax.ppermute(value, ('seq', 'head'), pairs)]
  transfers between devices with their start and end apart: 22 -> 22, of which waited for: 12 -> 14; matrix products, arithmetic and copies ran while one was open for 2% -> 2% of each run, Pallas kernels for 19% -> 16%
where the time goes in v4:
time: 66.6 us; the launch traced here: 65.3 us
  waiting for transfers between devices  24.7 us (37%)
  starting transfers between devices  19.9 us (30%)
  Pallas kernels  18.4 us (28%)
  between operations  1.12 us (2%)
  matrix products  1.07 us (2%)
    ppermute x14, starting transfers between devices, swap_line(): return lax.ppermute(value, ('seq', 'head'), pairs)  13.9 us
    ppermute x14, waiting for transfers between devices, swap_line(): return lax.ppermute(value, ('seq', 'head'), pairs)  11.5 us
    ppermute x3, waiting for transfers between devices, swap_chip(): lax.ppermute(value, 'head', [(i, i ^ bit) for i in range(head_count)])  7.56 us
    pallas_call x1, Pallas kernels, encode(): pl.pallas_call(encode_kernel, in_specs=[SM, SM, HB, HB, HB, HB], out_spec...  5.15 us
    ppermute x3, starting transfers between devices, swap_chip(): lax.ppermute(value, 'head', [(i, i ^ bit) for i in range(head_count)])  5.05 us
    pallas_call x5, Pallas kernels, cross(): pl.pallas_call(functools.partial(cross_kernel, [(bits, len(chunks)) for b...  4.89 us
    pallas_call x1, Pallas kernels, fetch(): pl.pallas_call(fetch_kernel, in_specs=[SM, HB, HB, HB, AN], out_specs=[VM...  3.71 us
    ppermute x2, waiting for transfers between devices, per_device(): blocks.append(jnp.concatenate([own, swap_core(send)], axis=0))  2.45 us
  transfers between devices with their start and end apart: 22, of which 14 were waited for; matrix products, arithmetic and copies ran while one was open for 2% of the time, Pallas kernels for 16%

profile of v4, /device:TPU:0, one launch (start us, length us, event | category | flops | bytes accessed | tf_op | source)
XLA Modules:
  0.0 65.3 jit_solution(4741181459997329831)
XLA Ops:
  0.8 5.1 %encode.1 = (bf16[128,1280]{1,0:T(8,128)(2,1)S(1)}, f32[128,1280]{1,0:T(8,128)S(1)}, bf16[128,1280]{1,0:T(8,128)(2,1)S(1)}) custom-call(s32[1]{0:T(128)} %bitcast.1.core_ref, s32[1]{0:T(128)S(6)} %copy.34.live_ref, f32[1280]{0:T(1024)} %gain_hbm.1, bf16[256,1280]{1,0:T(8,128)(2,1)} %bitcast.16, bf16[3,320,1280]{2,1,0:T(8,128)(2,1)} %bitcast.15, ...), custom_call_target="tpu_custom_call" | custom-call | flops 838860800 | bytes 3276800 | tf_op jit(solution)/shard_map/encode/pallas_call | solution.py:116
  6.4 1.3 %collective-permute-done = bf16[128,1280]{1,0:T(8,128)(2,1)S(1)} collective-permute-done((bf16[128,1280]{1,0:T(8,128)(2,1)S(1)}, bf16[128,1280]{1,0:T(8,128)(2,1)S(1)}, u32[]{:S(2)}, u32[]{:S(2)}) %collective-permute-start) | collective-permute-done | bytes 327712 | tf_op jit(solution)/shard_map/ppermute | solution.py:515
  7.7 3.0 %collective-permute-start.1 = (bf16[128,1280]{1,0:T(8,128)(2,1)S(1)}, bf16[128,1280]{1,0:T(8,128)(2,1)S(1)}, u32[]{:S(2)}, u32[]{:S(2)}) collective-permute-start(bf16[128,1280]{1,0:T(8,128)(2,1)S(1)} %add_convert_fusion._.first_ref), channel_id=1, source_target_pairs={{0,2},{1,3},{2,0},{3,1},{4,6},{5,7},{6,4},{7,5},{8,10},{9,11},{10,... | collective-permute-start | bytes 983048 | tf_op jit(solution)/shard_map/ppermute | solution.py:490
  10.8 1.6 %norm_queries.1 = (bf16[2,2,1024,128]{3,2,1,0:T(8,128)(2,1)S(1)}, s32[4,128]{1,0:T(4,128)S(1)}) custom-call(s32[16]{0:T(128)S(1)} %reshape.15.mask_ref, s32[1]{0:T(128)} %bitcast.seq_ref, s32[1]{0:T(128)} %bitcast.1.core_ref, bf16[256,2048]{1,0:T(8,128)(2,1)S(1)} %copy-done, f32[128]{0:T(128)S(1)} %copy-done.3), custom_call_target="tpu_custom_call" | custom-call | flops 4194304 | bytes 2097152 | tf_op jit(solution)/shard_map/norm_queries/pallas_call | solution.py:277
  12.5 3.7 %fetch.1 = (bf16[1280,1280]{1,0:T(8,128)(2,1)S(1)}, bf16[1280,1280]{1,0:T(8,128)(2,1)S(1)}, bf16[1280,2,512]{2,1,0:T(2,128)(2,1)S(1)}) custom-call(s32[1]{0:T(128)} %bitcast.2.chip_ref, bf16[1280,1280]{1,0:T(8,128)(2,1)} %w1_hbm.1, bf16[1280,1280]{1,0:T(8,128)(2,1)} %w2_hbm.1, bf16[1280,2,1024]{2,1,0:T(2,128)(2,1)} %wkv_hbm.1, ...), custom_call_target="tpu_custom_call" | custom-call | bytes 32768000 | tf_op jit(solution)/shard_map/fetch/pallas_call | solution.py:177
  16.2 2.5 %collective-permute-done.1.second_ref = bf16[128,1280]{1,0:T(8,128)(2,1)S(1)} collective-permute-done((bf16[128,1280]{1,0:T(8,128)(2,1)S(1)}, bf16[128,1280]{1,0:T(8,128)(2,1)S(1)}, u32[]{:S(2)}, u32[]{:S(2)}) %collective-permute-start.1) | collective-permute-done | bytes 327712 | tf_op jit(solution)/shard_map/ppermute | solution.py:490
  19.1 1.6 %collective-permute-done.2.normed_ref = bf16[128,1280]{1,0:T(8,128)(2,1)S(1)} collective-permute-done((bf16[128,1280]{1,0:T(8,128)(2,1)S(1)}, bf16[128,1280]{1,0:T(8,128)(2,1)S(1)}, u32[]{:S(2)}, u32[]{:S(2)}) %collective-permute-start.2) | collective-permute-done | bytes 327712 | tf_op jit(solution)/shard_map/ppermute | solution.py:521
  20.7 1.2 %mlp.3 = bf16[128,1280]{1,0:T(8,128)(2,1)S(1)} custom-call(bf16[128,1280]{1,0:T(8,128)(2,1)S(1)} %collective-permute-done.2.normed_ref, bf16[1280,1280]{1,0:T(8,128)(2,1)S(1)} %get-tuple-element.35.w1_ref, bf16[1280,1280]{1,0:T(8,128)(2,1)S(1)} %get-tuple-element.36.w2_ref), custom_call_target="tpu_custom_call" | custom-call | flops 838860800 | bytes 6553600 | tf_op jit(solution)/shard_map/mlp/pallas_call | solution.py:197
  23.7 1.8 %collective-permute-start.4 = (bf16[64,1280]{1,0:T(8,128)(2,1)S(1)}, bf16[64,1280]{1,0:T(8,128)(2,1)S(1)}, u32[]{:S(2)}, u32[]{:S(2)}) collective-permute-start(bf16[64,1280]{1,0:T(8,128)(2,1)S(1)} %get-tuple-element.50), channel_id=1, source_target_pairs={{0,2},{1,3},{2,0},{3,1},{4,6},{5,7},{6,4},{7,5},{8,10},{9,11},{10,... | collective-permute-start | bytes 491528 | tf_op jit(solution)/shard_map/ppermute | solution.py:490
  25.8 5.0 %collective-permute-done.4 = bf16[64,1280]{1,0:T(8,128)(2,1)S(1)} collective-permute-done((bf16[64,1280]{1,0:T(8,128)(2,1)S(1)}, bf16[64,1280]{1,0:T(8,128)(2,1)S(1)}, u32[]{:S(2)}, u32[]{:S(2)}) %collective-permute-start.4) | collective-permute-done | bytes 163872 | tf_op jit(solution)/shard_map/ppermute | solution.py:490
  31.6 1.2 %collective-permute-done.5 = bf16[64,512]{1,0:T(8,128)(2,1)S(1)} collective-permute-done((bf16[64,512]{1,0:T(8,128)(2,1)S(1)}, bf16[64,512]{1,0:T(8,128)(2,1)S(1)}, u32[]{:S(2)}, u32[]{:S(2)}) %collective-permute-start.5) | collective-permute-done | bytes 65568 | tf_op jit(solution)/shard_map/ppermute | solution.py:532
  32.8 1.8 %collective-permute-start.17 = (bf16[128,512]{1,0:T(8,128)(2,1)S(1)}, bf16[128,512]{1,0:T(8,128)(2,1)S(1)}, u32[]{:S(2)}, u32[]{:S(2)}) collective-permute-start(bf16[128,512]{1,0:T(8,128)(2,1)S(1)} %constant_dynamic-update-slice_fusion.refs_0_), channel_id=1, source_target_pairs={{0,8},{1,5},{2,10},{3,7},{4,12},{5,1},{6,14},{7,3},{8,0},{9,13},{1... | collective-permute-start | bytes 393224 | tf_op jit(solution)/shard_map/ppermute | solution.py:426
  34.6 1.5 %collective-permute-start.11 = (bf16[128,512]{1,0:T(8,128)(2,1)S(1)}, bf16[128,512]{1,0:T(8,128)(2,1)S(1)}, u32[]{:S(2)}, u32[]{:S(2)}) collective-permute-start(bf16[128,512]{1,0:T(8,128)(2,1)S(1)} %constant_dynamic-update-slice_fusion.refs_0_), channel_id=1, source_target_pairs={{0,4},{1,9},{2,6},{3,11},{4,0},{5,13},{6,2},{7,15},{8,12},{9,1},{1... | collective-permute-start | bytes 393224 | tf_op jit(solution)/shard_map/ppermute | solution.py:426
  36.1 2.6 %collective-permute-start.6 = (bf16[128,512]{1,0:T(8,128)(2,1)S(1)}, bf16[128,512]{1,0:T(8,128)(2,1)S(1)}, u32[]{:S(2)}, u32[]{:S(2)}) collective-permute-start(bf16[128,512]{1,0:T(8,128)(2,1)S(1)} %constant_dynamic-update-slice_fusion.refs_0_), channel_id=1, source_target_pairs={{0,16},{1,17},{2,18},{3,19},{4,20},{5,21},{6,22},{7,23},{8,24},{9,... | collective-permute-start | bytes 393224 | tf_op jit(solution)/shard_map/ppermute | solution.py:426
  39.5 1.2 %collective-permute-done.9 = bf16[64,512]{1,0:T(8,128)(2,1)S(1)} collective-permute-done((bf16[64,512]{1,0:T(8,128)(2,1)S(1)}, bf16[64,512]{1,0:T(8,128)(2,1)S(1)}, u32[]{:S(2)}, u32[]{:S(2)}) %collective-permute-start.9) | collective-permute-done | bytes 65568 | tf_op jit(solution)/shard_map/ppermute | solution.py:532
  42.2 2.7 %collective-permute-done.6.refs_0_ = bf16[128,512]{1,0:T(8,128)(2,1)S(1)} collective-permute-done((bf16[128,512]{1,0:T(8,128)(2,1)S(1)}, bf16[128,512]{1,0:T(8,128)(2,1)S(1)}, u32[]{:S(2)}, u32[]{:S(2)}) %collective-permute-start.6) | collective-permute-done | bytes 131104 | tf_op jit(solution)/shard_map/ppermute | solution.py:426
  45.1 1.3 %collective-permute-done.18.refs_3_ = bf16[128,512]{1,0:T(8,128)(2,1)S(1)} collective-permute-done((bf16[128,512]{1,0:T(8,128)(2,1)S(1)}, bf16[128,512]{1,0:T(8,128)(2,1)S(1)}, u32[]{:S(2)}, u32[]{:S(2)}) %collective-permute-start.18) | collective-permute-done | bytes 131104 | tf_op jit(solution)/shard_map/ppermute | solution.py:426
  47.7 2.9 %collective-permute-done.10.refs_1_ = bf16[128,512]{1,0:T(8,128)(2,1)S(1)} collective-permute-done((bf16[128,512]{1,0:T(8,128)(2,1)S(1)}, bf16[128,512]{1,0:T(8,128)(2,1)S(1)}, u32[]{:S(2)}, u32[]{:S(2)}) %collective-permute-start.10) | collective-permute-done | bytes 131104 | tf_op jit(solution)/shard_map/ppermute | solution.py:426
  50.6 1.4 %collective-permute-start.13 = (bf16[128,512]{1,0:T(8,128)(2,1)S(1)}, bf16[128,512]{1,0:T(8,128)(2,1)S(1)}, u32[]{:S(2)}, u32[]{:S(2)}) collective-permute-start(bf16[128,512]{1,0:T(8,128)(2,1)S(1)} %collective-permute-done.10.refs_1_), channel_id=1, source_target_pairs={{0,4},{1,9},{2,6},{3,11},{4,0},{5,13},{6,2},{7,15},{8,12},{9,1},{1... | collective-permute-start | bytes 393224 | tf_op jit(solution)/shard_map/ppermute | solution.py:426
  53.5 1.7 %cross.6.refs_4_ = f32[2,2,1024,256]{3,2,1,0:T(8,128)S(1)} custom-call(s32[4,128]{1,0:T(4,128)S(1)} %get-tuple-element.27.flags_ref, bf16[2,2,1024,128]{3,2,1,0:T(8,128)(2,1)S(1)} %get-tuple-element.28.__.q_ref, bf16[128,512]{1,0:T(8,128)(2,1)S(1)} %collective-permute-done.17.refs_0_, ...), custom_call_target="tpu_custom_call", output_to_operand_aliasing={{}: (6, {})} | custom-call | flops 1073741824 | bytes 2097152 | tf_op jit(solution)/shard_map/cross/pallas_call | solution.py:399
  55.6 2.6 %collective-permute-start.14 = (bf16[128,512]{1,0:T(8,128)(2,1)S(1)}, bf16[128,512]{1,0:T(8,128)(2,1)S(1)}, u32[]{:S(2)}, u32[]{:S(2)}) collective-permute-start(bf16[128,512]{1,0:T(8,128)(2,1)S(1)} %collective-permute-done.7.refs_2_), channel_id=1, source_target_pairs={{0,4},{1,9},{2,6},{3,11},{4,0},{5,13},{6,2},{7,15},{8,12},{9,1},{1... | collective-permute-start | bytes 393224 | tf_op jit(solution)/shard_map/ppermute | solution.py:426
  59.7 1.5 %collective-permute-done.14.refs_0_ = bf16[128,512]{1,0:T(8,128)(2,1)S(1)} collective-permute-done((bf16[128,512]{1,0:T(8,128)(2,1)S(1)}, bf16[128,512]{1,0:T(8,128)(2,1)S(1)}, u32[]{:S(2)}, u32[]{:S(2)}) %collective-permute-start.14) | collective-permute-done | bytes 131104 | tf_op jit(solution)/shard_map/ppermute | solution.py:426
  61.2 2.6 %collective-permute-done.15.refs_1_ = bf16[128,512]{1,0:T(8,128)(2,1)S(1)} collective-permute-done((bf16[128,512]{1,0:T(8,128)(2,1)S(1)}, bf16[128,512]{1,0:T(8,128)(2,1)S(1)}, u32[]{:S(2)}, u32[]{:S(2)}) %collective-permute-start.15) | collective-permute-done | bytes 131104 | tf_op jit(solution)/shard_map/ppermute | solution.py:426
  63.8 1.4 %cross.9 = (bf16[256,2048]{1,0:T(8,128)(2,1)}, f32[2,2,1024,256]{3,2,1,0:T(8,128)S(1)}) custom-call(s32[4,128]{1,0:T(4,128)S(1)} %get-tuple-element.27.flags_ref, bf16[2,2,1024,128]{3,2,1,0:T(8,128)(2,1)S(1)} %get-tuple-element.28.__.q_ref, bf16[128,512]{1,0:T(8,128)(2,1)S(1)} %collective-permute-done.14.refs_0_, ...), custom_call_target="tpu_custom_call", output_to_operand_aliasing={{1}: (4, {})} | custom-call | flops 536870912 | bytes 2097152 | tf_op jit(solution)/shard_map/cross/pallas_call | solution.py:399
  (52 shorter events, 10.7 us)
Async XLA Ops:
  0.0 10.8 %copy-start = (bf16[256,2048]{1,0:T(8,128)(2,1)S(1)}, bf16[256,2048]{1,0:T(8,128)(2,1)}, u32[]{:S(2)}) copy-start(bf16[256,2048]{1,0:T(8,128)(2,1)} %text_ref.1) | copy-start | bytes 3145732
  0.0 10.8 %copy-start.3 = (f32[128]{0:T(128)S(1)}, f32[128]{0:T(128)}, u32[]{:S(2)}) copy-start(f32[128]{0:T(128)} %gain_ref.4) | copy-start | bytes 1540
  5.9 1.8 %collective-permute-start = (bf16[128,1280]{1,0:T(8,128)(2,1)S(1)}, bf16[128,1280]{1,0:T(8,128)(2,1)S(1)}, u32[]{:S(2)}, u32[]{:S(2)}) collective-permute-start(bf16[128,1280]{1,0:T(8,128)(2,1)S(1)} %get-tuple-element.30), channel_id=1, source_target_pairs={{0,1},{1,0},{2,3},{3,2},{4,5},{5,4},{6,7},{7,6},{8,9},{9,8},{10,11... | collective-permute-start | bytes 983048 | tf_op jit(solution)/shard_map/ppermute | solution.py:515
  7.7 11.0 %collective-permute-start.1 = (bf16[128,1280]{1,0:T(8,128)(2,1)S(1)}, bf16[128,1280]{1,0:T(8,128)(2,1)S(1)}, u32[]{:S(2)}, u32[]{:S(2)}) collective-permute-start(bf16[128,1280]{1,0:T(8,128)(2,1)S(1)} %add_convert_fusion._.first_ref), channel_id=1, source_target_pairs={{0,2},{1,3},{2,0},{3,1},{4,6},{5,7},{6,4},{7,5},{8,10},{9,11},{10,... | collective-permute-start | bytes 983048 | tf_op jit(solution)/shard_map/ppermute | solution.py:490
  19.0 1.7 %collective-permute-start.2 = (bf16[128,1280]{1,0:T(8,128)(2,1)S(1)}, bf16[128,1280]{1,0:T(8,128)(2,1)S(1)}, u32[]{:S(2)}, u32[]{:S(2)}) collective-permute-start(bf16[128,1280]{1,0:T(8,128)(2,1)S(1)} %get-tuple-element.34.normed_ref), channel_id=1, source_target_pairs={{0,1},{1,0},{2,3},{3,2},{4,5},{5,4},{6,7},{7,6},{8,9},{9,8},{10,11... | collective-permute-start | bytes 983048 | tf_op jit(solution)/shard_map/ppermute | solution.py:521
  21.9 1.7 %collective-permute-start.3 = (bf16[128,1280]{1,0:T(8,128)(2,1)S(1)}, bf16[128,1280]{1,0:T(8,128)(2,1)S(1)}, u32[]{:S(2)}, u32[]{:S(2)}) collective-permute-start(bf16[128,1280]{1,0:T(8,128)(2,1)S(1)} %mlp.3), channel_id=1, source_target_pairs={{0,1},{1,0},{2,3},{3,2},{4,5},{5,4},{6,7},{7,6},{8,9},{9,8},{10,11... | collective-permute-start | bytes 983048 | tf_op jit(solution)/shard_map/ppermute | solution.py:523
  23.7 7.1 %collective-permute-start.4 = (bf16[64,1280]{1,0:T(8,128)(2,1)S(1)}, bf16[64,1280]{1,0:T(8,128)(2,1)S(1)}, u32[]{:S(2)}, u32[]{:S(2)}) collective-permute-start(bf16[64,1280]{1,0:T(8,128)(2,1)S(1)} %get-tuple-element.50), channel_id=1, source_target_pairs={{0,2},{1,3},{2,0},{3,1},{4,6},{5,7},{6,4},{7,5},{8,10},{9,11},{10,... | collective-permute-start | bytes 491528 | tf_op jit(solution)/shard_map/ppermute | solution.py:490
  25.5 13.2 %collective-permute-start.8 = (bf16[64,1280]{1,0:T(8,128)(2,1)S(1)}, bf16[64,1280]{1,0:T(8,128)(2,1)S(1)}, u32[]{:S(2)}, u32[]{:S(2)}) collective-permute-start(bf16[64,1280]{1,0:T(8,128)(2,1)S(1)} %get-tuple-element.49), channel_id=1, source_target_pairs={{0,2},{1,3},{2,0},{3,1},{4,6},{5,7},{6,4},{7,5},{8,10},{9,11},{10,... | collective-permute-start | bytes 491528 | tf_op jit(solution)/shard_map/ppermute | solution.py:490
  31.5 1.3 %collective-permute-start.5 = (bf16[64,512]{1,0:T(8,128)(2,1)S(1)}, bf16[64,512]{1,0:T(8,128)(2,1)S(1)}, u32[]{:S(2)}, u32[]{:S(2)}) collective-permute-start(bf16[64,512]{1,0:T(8,128)(2,1)S(1)} %get-tuple-element.39), channel_id=1, source_target_pairs={{0,1},{1,0},{2,3},{3,2},{4,5},{5,4},{6,7},{7,6},{8,9},{9,8},{10,11... | collective-permute-start | bytes 196616 | tf_op jit(solution)/shard_map/ppermute | solution.py:532
  32.8 12.3 %collective-permute-start.17 = (bf16[128,512]{1,0:T(8,128)(2,1)S(1)}, bf16[128,512]{1,0:T(8,128)(2,1)S(1)}, u32[]{:S(2)}, u32[]{:S(2)}) collective-permute-start(bf16[128,512]{1,0:T(8,128)(2,1)S(1)} %constant_dynamic-update-slice_fusion.refs_0_), channel_id=1, source_target_pairs={{0,8},{1,5},{2,10},{3,7},{4,12},{5,1},{6,14},{7,3},{8,0},{9,13},{1... | collective-permute-start | bytes 393224 | tf_op jit(solution)/shard_map/ppermute | solution.py:426
  34.6 7.1 %collective-permute-start.11 = (bf16[128,512]{1,0:T(8,128)(2,1)S(1)}, bf16[128,512]{1,0:T(8,128)(2,1)S(1)}, u32[]{:S(2)}, u32[]{:S(2)}) collective-permute-start(bf16[128,512]{1,0:T(8,128)(2,1)S(1)} %constant_dynamic-update-slice_fusion.refs_0_), channel_id=1, source_target_pairs={{0,4},{1,9},{2,6},{3,11},{4,0},{5,13},{6,2},{7,15},{8,12},{9,1},{1... | collective-permute-start | bytes 393224 | tf_op jit(solution)/shard_map/ppermute | solution.py:426
  36.1 8.8 %collective-permute-start.6 = (bf16[128,512]{1,0:T(8,128)(2,1)S(1)}, bf16[128,512]{1,0:T(8,128)(2,1)S(1)}, u32[]{:S(2)}, u32[]{:S(2)}) collective-permute-start(bf16[128,512]{1,0:T(8,128)(2,1)S(1)} %constant_dynamic-update-slice_fusion.refs_0_), channel_id=1, source_target_pairs={{0,16},{1,17},{2,18},{3,19},{4,20},{5,21},{6,22},{7,23},{8,24},{9,... | collective-permute-start | bytes 393224 | tf_op jit(solution)/shard_map/ppermute | solution.py:426
  39.4 1.3 %collective-permute-start.9 = (bf16[64,512]{1,0:T(8,128)(2,1)S(1)}, bf16[64,512]{1,0:T(8,128)(2,1)S(1)}, u32[]{:S(2)}, u32[]{:S(2)}) collective-permute-start(bf16[64,512]{1,0:T(8,128)(2,1)S(1)} %get-tuple-element.42), channel_id=1, source_target_pairs={{0,1},{1,0},{2,3},{3,2},{4,5},{5,4},{6,7},{7,6},{8,9},{9,8},{10,11... | collective-permute-start | bytes 196616 | tf_op jit(solution)/shard_map/ppermute | solution.py:532
  40.7 5.7 %collective-permute-start.18 = (bf16[128,512]{1,0:T(8,128)(2,1)S(1)}, bf16[128,512]{1,0:T(8,128)(2,1)S(1)}, u32[]{:S(2)}, u32[]{:S(2)}) collective-permute-start(bf16[128,512]{1,0:T(8,128)(2,1)S(1)} %constant_dynamic-update-slice_fusion.2.refs_1_), channel_id=1, source_target_pairs={{0,4},{1,9},{2,6},{3,11},{4,0},{5,13},{6,2},{7,15},{8,12},{9,1},{1... | collective-permute-start | bytes 393224 | tf_op jit(solution)/shard_map/ppermute | solution.py:426
  41.3 10.8 %collective-permute-start.20 = (bf16[128,512]{1,0:T(8,128)(2,1)S(1)}, bf16[128,512]{1,0:T(8,128)(2,1)S(1)}, u32[]{:S(2)}, u32[]{:S(2)}) collective-permute-start(bf16[128,512]{1,0:T(8,128)(2,1)S(1)} %constant_dynamic-update-slice_fusion.2.refs_1_), channel_id=1, source_target_pairs={{0,8},{1,5},{2,10},{3,7},{4,12},{5,1},{6,14},{7,3},{8,0},{9,13},{1... | collective-permute-start | bytes 393224 | tf_op jit(solution)/shard_map/ppermute | solution.py:426
  41.7 8.9 %collective-permute-start.10 = (bf16[128,512]{1,0:T(8,128)(2,1)S(1)}, bf16[128,512]{1,0:T(8,128)(2,1)S(1)}, u32[]{:S(2)}, u32[]{:S(2)}) collective-permute-start(bf16[128,512]{1,0:T(8,128)(2,1)S(1)} %constant_dynamic-update-slice_fusion.2.refs_1_), channel_id=1, source_target_pairs={{0,16},{1,17},{2,18},{3,19},{4,20},{5,21},{6,22},{7,23},{8,24},{9,... | collective-permute-start | bytes 393224 | tf_op jit(solution)/shard_map/ppermute | solution.py:426
  44.9 5.7 %collective-permute-start.12 = (bf16[128,512]{1,0:T(8,128)(2,1)S(1)}, bf16[128,512]{1,0:T(8,128)(2,1)S(1)}, u32[]{:S(2)}, u32[]{:S(2)}) collective-permute-start(bf16[128,512]{1,0:T(8,128)(2,1)S(1)} %collective-permute-done.6.refs_0_), channel_id=1, source_target_pairs={{0,4},{1,9},{2,6},{3,11},{4,0},{5,13},{6,2},{7,15},{8,12},{9,1},{1... | collective-permute-start | bytes 393224 | tf_op jit(solution)/shard_map/ppermute | solution.py:426
  46.5 5.6 %collective-permute-start.19 = (bf16[128,512]{1,0:T(8,128)(2,1)S(1)}, bf16[128,512]{1,0:T(8,128)(2,1)S(1)}, u32[]{:S(2)}, u32[]{:S(2)}) collective-permute-start(bf16[128,512]{1,0:T(8,128)(2,1)S(1)} %collective-permute-done.17.refs_0_), channel_id=1, source_target_pairs={{0,4},{1,9},{2,6},{3,11},{4,0},{5,13},{6,2},{7,15},{8,12},{9,1},{1... | collective-permute-start | bytes 393224 | tf_op jit(solution)/shard_map/ppermute | solution.py:426
  47.0 8.2 %collective-permute-start.7 = (bf16[128,512]{1,0:T(8,128)(2,1)S(1)}, bf16[128,512]{1,0:T(8,128)(2,1)S(1)}, u32[]{:S(2)}, u32[]{:S(2)}) collective-permute-start(bf16[128,512]{1,0:T(8,128)(2,1)S(1)} %collective-permute-done.6.refs_0_), channel_id=1, source_target_pairs={{0,8},{1,5},{2,10},{3,7},{4,12},{5,1},{6,14},{7,3},{8,0},{9,13},{1... | collective-permute-start | bytes 393224 | tf_op jit(solution)/shard_map/ppermute | solution.py:426
  50.6 5.0 %collective-permute-start.13 = (bf16[128,512]{1,0:T(8,128)(2,1)S(1)}, bf16[128,512]{1,0:T(8,128)(2,1)S(1)}, u32[]{:S(2)}, u32[]{:S(2)}) collective-permute-start(bf16[128,512]{1,0:T(8,128)(2,1)S(1)} %collective-permute-done.10.refs_1_), channel_id=1, source_target_pairs={{0,4},{1,9},{2,6},{3,11},{4,0},{5,13},{6,2},{7,15},{8,12},{9,1},{1... | collective-permute-start | bytes 393224 | tf_op jit(solution)/shard_map/ppermute | solution.py:426
  52.1 6.3 %collective-permute-start.21 = (bf16[128,512]{1,0:T(8,128)(2,1)S(1)}, bf16[128,512]{1,0:T(8,128)(2,1)S(1)}, u32[]{:S(2)}, u32[]{:S(2)}) collective-permute-start(bf16[128,512]{1,0:T(8,128)(2,1)S(1)} %collective-permute-done.20.refs_1_), channel_id=1, source_target_pairs={{0,4},{1,9},{2,6},{3,11},{4,0},{5,13},{6,2},{7,15},{8,12},{9,1},{1... | collective-permute-start | bytes 393224 | tf_op jit(solution)/shard_map/ppermute | solution.py:426
  53.4 5.6 %collective-permute-start.16 = (bf16[128,512]{1,0:T(8,128)(2,1)S(1)}, bf16[128,512]{1,0:T(8,128)(2,1)S(1)}, u32[]{:S(2)}, u32[]{:S(2)}) collective-permute-start(bf16[128,512]{1,0:T(8,128)(2,1)S(1)} %collective-permute-done.10.refs_1_), channel_id=1, source_target_pairs={{0,8},{1,5},{2,10},{3,7},{4,12},{5,1},{6,14},{7,3},{8,0},{9,13},{1... | collective-permute-start | bytes 393224 | tf_op jit(solution)/shard_map/ppermute | solution.py:426
  55.6 5.6 %collective-permute-start.14 = (bf16[128,512]{1,0:T(8,128)(2,1)S(1)}, bf16[128,512]{1,0:T(8,128)(2,1)S(1)}, u32[]{:S(2)}, u32[]{:S(2)}) collective-permute-start(bf16[128,512]{1,0:T(8,128)(2,1)S(1)} %collective-permute-done.7.refs_2_), channel_id=1, source_target_pairs={{0,4},{1,9},{2,6},{3,11},{4,0},{5,13},{6,2},{7,15},{8,12},{9,1},{1... | collective-permute-start | bytes 393224 | tf_op jit(solution)/shard_map/ppermute | solution.py:426
  58.2 5.6 %collective-permute-start.15 = (bf16[128,512]{1,0:T(8,128)(2,1)S(1)}, bf16[128,512]{1,0:T(8,128)(2,1)S(1)}, u32[]{:S(2)}, u32[]{:S(2)}) collective-permute-start(bf16[128,512]{1,0:T(8,128)(2,1)S(1)} %collective-permute-done.13.refs_1_), channel_id=1, source_target_pairs={{0,8},{1,5},{2,10},{3,7},{4,12},{5,1},{6,14},{7,3},{8,0},{9,13},{1... | collective-permute-start | bytes 393224 | tf_op jit(solution)/shard_map/ppermute | solution.py:426
  (3 other events, 25.0 us)

commit v5 on v4

--- a/solution.py
+++ b/solution.py
@@ -369,9 +369,11 @@
                 for member in range(group):
                     at = slice(member * QB, (member + 1) * QB)
                     column = (head * group + member) * HD
-                    out_ref[rows_at, column : column + HD] = (
-                        acc[head, block, at, :HD] / acc[head, block, at, HD:]
-                    ).astype(BF16)
+                    total = acc[head, block, at, :HD]
+                    denom = acc[head, block, at, HD:]
+                    inverse = pl.reciprocal(denom, approx=True)
+                    inverse = inverse * (2.0 - denom * inverse)
+                    out_ref[rows_at, column : column + HD] = (total * inverse).astype(BF16)
 
             @pl.when(seen == 0)
             def _(rows_at=rows_at, columns=columns):
@@ -454,10 +456,11 @@
         got[6] = two(got[4])
         got[5] = one(got[4])
         got[3] = one(got[2])
+    acc = attend(slots(0, 2, 1), None, False)
+    images[1][5], acc = tie((images[1][5], acc))
     images[0][7] = one(images[0][6])
     images[1][7] = two(images[1][5])
-    acc = None
-    for several in ((0,), (2, 1), (4, 3), (5, 6), (7,)):
+    for several in ((4, 3, 5, 6), (7,)):
         acc = attend(slots(*several), acc, several == (7,))
     return acc
 

time: 66.6 us -> 65 us (0.976); the launches traced: 65.3 us -> 64.9 us
  waiting for transfers between devices: 24.7 us -> 21.8 us
  Pallas kernels: 18.4 us -> 20.3 us
    ppermute x14, waiting for transfers between devices: 11.5 us -> 8.65 us  [swap_line(): return lax.ppermute(value, ('seq', 'head'), pairs)]
    pallas_call x5 -> x3, Pallas kernels: 4.89 us -> 6.78 us  [cross(): pl.pallas_call(functools.partial(cross_kernel, [(bits, len(chunks)) for b...]
  transfers between devices with their start and end apart: 22 -> 22, of which waited for: 14 -> 11; matrix products, arithmetic and copies ran while one was open for 2% -> 2% of each run, Pallas kernels for 16% -> 19%
where the time goes in v5:
time: 65 us; the launch traced here: 64.9 us
  waiting for transfers between devices  21.8 us (34%)
  starting transfers between devices  20.4 us (31%)
  Pallas kernels  20.3 us (31%)
  matrix products  1.07 us (2%)
  between operations  1.05 us (2%)
    ppermute x14, starting transfers between devices, swap_line(): return lax.ppermute(value, ('seq', 'head'), pairs)  14.4 us
    ppermute x14, waiting for transfers between devices, swap_line(): return lax.ppermute(value, ('seq', 'head'), pairs)  8.65 us
    ppermute x3, waiting for transfers between devices, swap_chip(): lax.ppermute(value, 'head', [(i, i ^ bit) for i in range(head_count)])  7.56 us
    pallas_call x3, Pallas kernels, cross(): pl.pallas_call(functools.partial(cross_kernel, [(bits, len(chunks)) for b...  6.78 us
    pallas_call x1, Pallas kernels, encode(): pl.pallas_call(encode_kernel, in_specs=[SM, SM, HB, HB, HB, HB], out_spec...  5.21 us
    ppermute x3, starting transfers between devices, swap_chip(): lax.ppermute(value, 'head', [(i, i ^ bit) for i in range(head_count)])  5.04 us
    pallas_call x1, Pallas kernels, fetch(): pl.pallas_call(fetch_kernel, in_specs=[SM, HB, HB, HB, AN], out_specs=[VM...  3.71 us
    ppermute x2, waiting for transfers between devices, per_device(): blocks.append(jnp.concatenate([own, swap_core(send)], axis=0))  2.45 us
  transfers between devices with their start and end apart: 22, of which 11 were waited for; matrix products, arithmetic and copies ran while one was open for 2% of the time, Pallas kernels for 19%

profile of v5, /device:TPU:0, one launch (start us, length us, event | category | flops | bytes accessed | tf_op | source)
XLA Modules:
  0.0 64.9 jit_solution(10978048073842695424)
XLA Ops:
  0.7 5.2 %encode.1 = (bf16[128,1280]{1,0:T(8,128)(2,1)S(1)}, f32[128,1280]{1,0:T(8,128)S(1)}, bf16[128,1280]{1,0:T(8,128)(2,1)S(1)}) custom-call(s32[1]{0:T(128)} %bitcast.1.core_ref, s32[1]{0:T(128)S(6)} %copy.30.live_ref, f32[1280]{0:T(1024)} %gain_hbm.1, bf16[256,1280]{1,0:T(8,128)(2,1)} %bitcast.16, bf16[3,320,1280]{2,1,0:T(8,128)(2,1)} %bitcast.15, ...), custom_call_target="tpu_custom_call" | custom-call | flops 838860800 | bytes 3276800 | tf_op jit(solution)/shard_map/encode/pallas_call | solution.py:116
  6.4 1.3 %collective-permute-done = bf16[128,1280]{1,0:T(8,128)(2,1)S(1)} collective-permute-done((bf16[128,1280]{1,0:T(8,128)(2,1)S(1)}, bf16[128,1280]{1,0:T(8,128)(2,1)S(1)}, u32[]{:S(2)}, u32[]{:S(2)}) %collective-permute-start) | collective-permute-done | bytes 327712 | tf_op jit(solution)/shard_map/ppermute | solution.py:518
  7.7 2.9 %collective-permute-start.1 = (bf16[128,1280]{1,0:T(8,128)(2,1)S(1)}, bf16[128,1280]{1,0:T(8,128)(2,1)S(1)}, u32[]{:S(2)}, u32[]{:S(2)}) collective-permute-start(bf16[128,1280]{1,0:T(8,128)(2,1)S(1)} %add_convert_fusion._.first_ref), channel_id=1, source_target_pairs={{0,2},{1,3},{2,0},{3,1},{4,6},{5,7},{6,4},{7,5},{8,10},{9,11},{10,... | collective-permute-start | bytes 983048 | tf_op jit(solution)/shard_map/ppermute | solution.py:493
  10.8 1.6 %norm_queries.1 = (bf16[2,2,1024,128]{3,2,1,0:T(8,128)(2,1)S(1)}, s32[4,128]{1,0:T(4,128)S(1)}) custom-call(s32[16]{0:T(128)S(1)} %reshape.15.mask_ref, s32[1]{0:T(128)} %bitcast.seq_ref, s32[1]{0:T(128)} %bitcast.1.core_ref, bf16[256,2048]{1,0:T(8,128)(2,1)S(1)} %copy-done, f32[128]{0:T(128)S(1)} %copy-done.3), custom_call_target="tpu_custom_call" | custom-call | flops 4194304 | bytes 2097152 | tf_op jit(solution)/shard_map/norm_queries/pallas_call | solution.py:277
  12.4 3.7 %fetch.1 = (bf16[1280,1280]{1,0:T(8,128)(2,1)S(1)}, bf16[1280,1280]{1,0:T(8,128)(2,1)S(1)}, bf16[1280,2,512]{2,1,0:T(2,128)(2,1)S(1)}) custom-call(s32[1]{0:T(128)} %bitcast.2.chip_ref, bf16[1280,1280]{1,0:T(8,128)(2,1)} %w1_hbm.1, bf16[1280,1280]{1,0:T(8,128)(2,1)} %w2_hbm.1, bf16[1280,2,1024]{2,1,0:T(2,128)(2,1)} %wkv_hbm.1, ...), custom_call_target="tpu_custom_call" | custom-call | bytes 32768000 | tf_op jit(solution)/shard_map/fetch/pallas_call | solution.py:177
  16.2 2.5 %collective-permute-done.1.second_ref = bf16[128,1280]{1,0:T(8,128)(2,1)S(1)} collective-permute-done((bf16[128,1280]{1,0:T(8,128)(2,1)S(1)}, bf16[128,1280]{1,0:T(8,128)(2,1)S(1)}, u32[]{:S(2)}, u32[]{:S(2)}) %collective-permute-start.1) | collective-permute-done | bytes 327712 | tf_op jit(solution)/shard_map/ppermute | solution.py:493
  19.1 1.6 %collective-permute-done.2.normed_ref = bf16[128,1280]{1,0:T(8,128)(2,1)S(1)} collective-permute-done((bf16[128,1280]{1,0:T(8,128)(2,1)S(1)}, bf16[128,1280]{1,0:T(8,128)(2,1)S(1)}, u32[]{:S(2)}, u32[]{:S(2)}) %collective-permute-start.2) | collective-permute-done | bytes 327712 | tf_op jit(solution)/shard_map/ppermute | solution.py:524
  23.7 1.8 %collective-permute-start.4 = (bf16[64,1280]{1,0:T(8,128)(2,1)S(1)}, bf16[64,1280]{1,0:T(8,128)(2,1)S(1)}, u32[]{:S(2)}, u32[]{:S(2)}) collective-permute-start(bf16[64,1280]{1,0:T(8,128)(2,1)S(1)} %get-tuple-element.54), channel_id=1, source_target_pairs={{0,2},{1,3},{2,0},{3,1},{4,6},{5,7},{6,4},{7,5},{8,10},{9,11},{10,... | collective-permute-start | bytes 491528 | tf_op jit(solution)/shard_map/ppermute | solution.py:493
  25.8 5.0 %collective-permute-done.4 = bf16[64,1280]{1,0:T(8,128)(2,1)S(1)} collective-permute-done((bf16[64,1280]{1,0:T(8,128)(2,1)S(1)}, bf16[64,1280]{1,0:T(8,128)(2,1)S(1)}, u32[]{:S(2)}, u32[]{:S(2)}) %collective-permute-start.4) | collective-permute-done | bytes 163872 | tf_op jit(solution)/shard_map/ppermute | solution.py:493
  31.6 1.2 %collective-permute-done.5 = bf16[64,512]{1,0:T(8,128)(2,1)S(1)} collective-permute-done((bf16[64,512]{1,0:T(8,128)(2,1)S(1)}, bf16[64,512]{1,0:T(8,128)(2,1)S(1)}, u32[]{:S(2)}, u32[]{:S(2)}) %collective-permute-start.5) | collective-permute-done | bytes 65568 | tf_op jit(solution)/shard_map/ppermute | solution.py:535
  32.8 1.8 %collective-permute-start.15 = (bf16[128,512]{1,0:T(8,128)(2,1)S(1)}, bf16[128,512]{1,0:T(8,128)(2,1)S(1)}, u32[]{:S(2)}, u32[]{:S(2)}) collective-permute-start(bf16[128,512]{1,0:T(8,128)(2,1)S(1)} %constant_dynamic-update-slice_fusion.refs_0_), channel_id=1, source_target_pairs={{0,8},{1,5},{2,10},{3,7},{4,12},{5,1},{6,14},{7,3},{8,0},{9,13},{1... | collective-permute-start | bytes 393224 | tf_op jit(solution)/shard_map/ppermute | solution.py:428
  34.6 1.5 %collective-permute-start.11 = (bf16[128,512]{1,0:T(8,128)(2,1)S(1)}, bf16[128,512]{1,0:T(8,128)(2,1)S(1)}, u32[]{:S(2)}, u32[]{:S(2)}) collective-permute-start(bf16[128,512]{1,0:T(8,128)(2,1)S(1)} %constant_dynamic-update-slice_fusion.refs_0_), channel_id=1, source_target_pairs={{0,4},{1,9},{2,6},{3,11},{4,0},{5,13},{6,2},{7,15},{8,12},{9,1},{1... | collective-permute-start | bytes 393224 | tf_op jit(solution)/shard_map/ppermute | solution.py:428
  36.1 2.6 %collective-permute-start.6 = (bf16[128,512]{1,0:T(8,128)(2,1)S(1)}, bf16[128,512]{1,0:T(8,128)(2,1)S(1)}, u32[]{:S(2)}, u32[]{:S(2)}) collective-permute-start(bf16[128,512]{1,0:T(8,128)(2,1)S(1)} %constant_dynamic-update-slice_fusion.refs_0_), channel_id=1, source_target_pairs={{0,16},{1,17},{2,18},{3,19},{4,20},{5,21},{6,22},{7,23},{8,24},{9,... | collective-permute-start | bytes 393224 | tf_op jit(solution)/shard_map/ppermute | solution.py:428
  39.5 1.2 %collective-permute-done.9 = bf16[64,512]{1,0:T(8,128)(2,1)S(1)} collective-permute-done((bf16[64,512]{1,0:T(8,128)(2,1)S(1)}, bf16[64,512]{1,0:T(8,128)(2,1)S(1)}, u32[]{:S(2)}, u32[]{:S(2)}) %collective-permute-start.9) | collective-permute-done | bytes 65568 | tf_op jit(solution)/shard_map/ppermute | solution.py:535
  42.2 2.7 %collective-permute-done.6.refs_0_ = bf16[128,512]{1,0:T(8,128)(2,1)S(1)} collective-permute-done((bf16[128,512]{1,0:T(8,128)(2,1)S(1)}, bf16[128,512]{1,0:T(8,128)(2,1)S(1)}, u32[]{:S(2)}, u32[]{:S(2)}) %collective-permute-start.6) | collective-permute-done | bytes 131104 | tf_op jit(solution)/shard_map/ppermute | solution.py:428
  45.1 1.3 %collective-permute-done.17.refs_5_ = bf16[128,512]{1,0:T(8,128)(2,1)S(1)} collective-permute-done((bf16[128,512]{1,0:T(8,128)(2,1)S(1)}, bf16[128,512]{1,0:T(8,128)(2,1)S(1)}, u32[]{:S(2)}, u32[]{:S(2)}) %collective-permute-start.17) | collective-permute-done | bytes 131104 | tf_op jit(solution)/shard_map/ppermute | solution.py:428
  47.7 2.9 %collective-permute-done.10.refs_1_ = bf16[128,512]{1,0:T(8,128)(2,1)S(1)} collective-permute-done((bf16[128,512]{1,0:T(8,128)(2,1)S(1)}, bf16[128,512]{1,0:T(8,128)(2,1)S(1)}, u32[]{:S(2)}, u32[]{:S(2)}) %collective-permute-start.10) | collective-permute-done | bytes 131104 | tf_op jit(solution)/shard_map/ppermute | solution.py:428
  50.9 1.3 %collective-permute-start.13 = (bf16[128,512]{1,0:T(8,128)(2,1)S(1)}, bf16[128,512]{1,0:T(8,128)(2,1)S(1)}, u32[]{:S(2)}, u32[]{:S(2)}) collective-permute-start(bf16[128,512]{1,0:T(8,128)(2,1)S(1)} %collective-permute-done.10.refs_1_), channel_id=1, source_target_pairs={{0,4},{1,9},{2,6},{3,11},{4,0},{5,13},{6,2},{7,15},{8,12},{9,1},{1... | collective-permute-start | bytes 393224 | tf_op jit(solution)/shard_map/ppermute | solution.py:428
  52.9 1.3 %cross.3.refs_8_ = f32[2,2,1024,256]{3,2,1,0:T(8,128)S(1)} custom-call(s32[4,128]{1,0:T(4,128)S(1)} %get-tuple-element.29.flags_ref, bf16[2,2,1024,128]{3,2,1,0:T(8,128)(2,1)S(1)} %get-tuple-element.30.__.q_ref, bf16[128,512]{1,0:T(8,128)(2,1)S(1)} %constant_dynamic-update-slice_fusion.refs_0_, ...), custom_call_target="tpu_custom_call" | custom-call | flops 1610612736 | bytes 2097152 | tf_op jit(solution)/shard_map/cross/pallas_call | solution.py:401
  54.2 1.6 %collective-permute-done.13.refs_5_ = bf16[128,512]{1,0:T(8,128)(2,1)S(1)} collective-permute-done((bf16[128,512]{1,0:T(8,128)(2,1)S(1)}, bf16[128,512]{1,0:T(8,128)(2,1)S(1)}, u32[]{:S(2)}, u32[]{:S(2)}) %collective-permute-start.13) | collective-permute-done | bytes 131104 | tf_op jit(solution)/shard_map/ppermute | solution.py:428
  55.9 1.3 %collective-permute-start.14 = (bf16[128,512]{1,0:T(8,128)(2,1)S(1)}, bf16[128,512]{1,0:T(8,128)(2,1)S(1)}, u32[]{:S(2)}, u32[]{:S(2)}) collective-permute-start(bf16[128,512]{1,0:T(8,128)(2,1)S(1)} %collective-permute-done.7.refs_6_), channel_id=1, source_target_pairs={{0,4},{1,9},{2,6},{3,11},{4,0},{5,13},{6,2},{7,15},{8,12},{9,1},{1... | collective-permute-start | bytes 393224 | tf_op jit(solution)/shard_map/ppermute | solution.py:428
  57.2 2.0 %collective-permute-start.18 = (bf16[128,512]{1,0:T(8,128)(2,1)S(1)}, bf16[128,512]{1,0:T(8,128)(2,1)S(1)}, u32[]{:S(2)}, u32[]{:S(2)}) collective-permute-start(bf16[128,512]{1,0:T(8,128)(2,1)S(1)} %collective-permute-done.13.refs_5_), channel_id=1, source_target_pairs={{0,8},{1,5},{2,10},{3,7},{4,12},{5,1},{6,14},{7,3},{8,0},{9,13},{1... | collective-permute-start | bytes 393224 | tf_op jit(solution)/shard_map/ppermute | solution.py:428
  59.2 4.0 %cross.4.refs_2_ = f32[2,2,1024,256]{3,2,1,0:T(8,128)S(1)} custom-call(s32[4,128]{1,0:T(4,128)S(1)} %get-tuple-element.29.flags_ref, bf16[2,2,1024,128]{3,2,1,0:T(8,128)(2,1)S(1)} %get-tuple-element.30.__.q_ref, bf16[128,512]{1,0:T(8,128)(2,1)S(1)} %collective-permute-done.6.refs_0_, ...), custom_call_target="tpu_custom_call", output_to_operand_aliasing={{}: (10, {})} | custom-call | flops 2147483648 | bytes 2097152 | tf_op jit(solution)/shard_map/cross/pallas_call | solution.py:401
  63.2 1.5 %cross.5 = (bf16[256,2048]{1,0:T(8,128)(2,1)}, f32[2,2,1024,256]{3,2,1,0:T(8,128)S(1)}) custom-call(s32[4,128]{1,0:T(4,128)S(1)} %get-tuple-element.29.flags_ref, bf16[2,2,1024,128]{3,2,1,0:T(8,128)(2,1)S(1)} %get-tuple-element.30.__.q_ref, bf16[128,512]{1,0:T(8,128)(2,1)S(1)} %collective-permute-done.14.refs_0_, ...), custom_call_target="tpu_custom_call", output_to_operand_aliasing={{1}: (4, {})} | custom-call | flops 536870912 | bytes 2097152 | tf_op jit(solution)/shard_map/cross/pallas_call | solution.py:401
  (50 shorter events, 9.7 us)
Async XLA Ops:
  0.7 10.1 %copy-start = (bf16[256,2048]{1,0:T(8,128)(2,1)S(1)}, bf16[256,2048]{1,0:T(8,128)(2,1)}, u32[]{:S(2)}) copy-start(bf16[256,2048]{1,0:T(8,128)(2,1)} %text_ref.1) | copy-start | bytes 3145732
  0.7 10.1 %copy-start.3 = (f32[128]{0:T(128)S(1)}, f32[128]{0:T(128)}, u32[]{:S(2)}) copy-start(f32[128]{0:T(128)} %gain_ref.4) | copy-start | bytes 1540
  5.9 1.8 %collective-permute-start = (bf16[128,1280]{1,0:T(8,128)(2,1)S(1)}, bf16[128,1280]{1,0:T(8,128)(2,1)S(1)}, u32[]{:S(2)}, u32[]{:S(2)}) collective-permute-start(bf16[128,1280]{1,0:T(8,128)(2,1)S(1)} %get-tuple-element.32), channel_id=1, source_target_pairs={{0,1},{1,0},{2,3},{3,2},{4,5},{5,4},{6,7},{7,6},{8,9},{9,8},{10,11... | collective-permute-start | bytes 983048 | tf_op jit(solution)/shard_map/ppermute | solution.py:518
  7.7 11.0 %collective-permute-start.1 = (bf16[128,1280]{1,0:T(8,128)(2,1)S(1)}, bf16[128,1280]{1,0:T(8,128)(2,1)S(1)}, u32[]{:S(2)}, u32[]{:S(2)}) collective-permute-start(bf16[128,1280]{1,0:T(8,128)(2,1)S(1)} %add_convert_fusion._.first_ref), channel_id=1, source_target_pairs={{0,2},{1,3},{2,0},{3,1},{4,6},{5,7},{6,4},{7,5},{8,10},{9,11},{10,... | collective-permute-start | bytes 983048 | tf_op jit(solution)/shard_map/ppermute | solution.py:493
  19.0 1.7 %collective-permute-start.2 = (bf16[128,1280]{1,0:T(8,128)(2,1)S(1)}, bf16[128,1280]{1,0:T(8,128)(2,1)S(1)}, u32[]{:S(2)}, u32[]{:S(2)}) collective-permute-start(bf16[128,1280]{1,0:T(8,128)(2,1)S(1)} %get-tuple-element.36.normed_ref), channel_id=1, source_target_pairs={{0,1},{1,0},{2,3},{3,2},{4,5},{5,4},{6,7},{7,6},{8,9},{9,8},{10,11... | collective-permute-start | bytes 983048 | tf_op jit(solution)/shard_map/ppermute | solution.py:524
  21.9 1.7 %collective-permute-start.3 = (bf16[128,1280]{1,0:T(8,128)(2,1)S(1)}, bf16[128,1280]{1,0:T(8,128)(2,1)S(1)}, u32[]{:S(2)}, u32[]{:S(2)}) collective-permute-start(bf16[128,1280]{1,0:T(8,128)(2,1)S(1)} %mlp.3), channel_id=1, source_target_pairs={{0,1},{1,0},{2,3},{3,2},{4,5},{5,4},{6,7},{7,6},{8,9},{9,8},{10,11... | collective-permute-start | bytes 983048 | tf_op jit(solution)/shard_map/ppermute | solution.py:526
  23.7 7.1 %collective-permute-start.4 = (bf16[64,1280]{1,0:T(8,128)(2,1)S(1)}, bf16[64,1280]{1,0:T(8,128)(2,1)S(1)}, u32[]{:S(2)}, u32[]{:S(2)}) collective-permute-start(bf16[64,1280]{1,0:T(8,128)(2,1)S(1)} %get-tuple-element.54), channel_id=1, source_target_pairs={{0,2},{1,3},{2,0},{3,1},{4,6},{5,7},{6,4},{7,5},{8,10},{9,11},{10,... | collective-permute-start | bytes 491528 | tf_op jit(solution)/shard_map/ppermute | solution.py:493
  25.5 13.2 %collective-permute-start.8 = (bf16[64,1280]{1,0:T(8,128)(2,1)S(1)}, bf16[64,1280]{1,0:T(8,128)(2,1)S(1)}, u32[]{:S(2)}, u32[]{:S(2)}) collective-permute-start(bf16[64,1280]{1,0:T(8,128)(2,1)S(1)} %get-tuple-element.53), channel_id=1, source_target_pairs={{0,2},{1,3},{2,0},{3,1},{4,6},{5,7},{6,4},{7,5},{8,10},{9,11},{10,... | collective-permute-start | bytes 491528 | tf_op jit(solution)/shard_map/ppermute | solution.py:493
  31.5 1.3 %collective-permute-start.5 = (bf16[64,512]{1,0:T(8,128)(2,1)S(1)}, bf16[64,512]{1,0:T(8,128)(2,1)S(1)}, u32[]{:S(2)}, u32[]{:S(2)}) collective-permute-start(bf16[64,512]{1,0:T(8,128)(2,1)S(1)} %get-tuple-element.41), channel_id=1, source_target_pairs={{0,1},{1,0},{2,3},{3,2},{4,5},{5,4},{6,7},{7,6},{8,9},{9,8},{10,11... | collective-permute-start | bytes 196616 | tf_op jit(solution)/shard_map/ppermute | solution.py:535
  32.8 12.3 %collective-permute-start.15 = (bf16[128,512]{1,0:T(8,128)(2,1)S(1)}, bf16[128,512]{1,0:T(8,128)(2,1)S(1)}, u32[]{:S(2)}, u32[]{:S(2)}) collective-permute-start(bf16[128,512]{1,0:T(8,128)(2,1)S(1)} %constant_dynamic-update-slice_fusion.refs_0_), channel_id=1, source_target_pairs={{0,8},{1,5},{2,10},{3,7},{4,12},{5,1},{6,14},{7,3},{8,0},{9,13},{1... | collective-permute-start | bytes 393224 | tf_op jit(solution)/shard_map/ppermute | solution.py:428
  34.6 7.1 %collective-permute-start.11 = (bf16[128,512]{1,0:T(8,128)(2,1)S(1)}, bf16[128,512]{1,0:T(8,128)(2,1)S(1)}, u32[]{:S(2)}, u32[]{:S(2)}) collective-permute-start(bf16[128,512]{1,0:T(8,128)(2,1)S(1)} %constant_dynamic-update-slice_fusion.refs_0_), channel_id=1, source_target_pairs={{0,4},{1,9},{2,6},{3,11},{4,0},{5,13},{6,2},{7,15},{8,12},{9,1},{1... | collective-permute-start | bytes 393224 | tf_op jit(solution)/shard_map/ppermute | solution.py:428
  36.1 8.8 %collective-permute-start.6 = (bf16[128,512]{1,0:T(8,128)(2,1)S(1)}, bf16[128,512]{1,0:T(8,128)(2,1)S(1)}, u32[]{:S(2)}, u32[]{:S(2)}) collective-permute-start(bf16[128,512]{1,0:T(8,128)(2,1)S(1)} %constant_dynamic-update-slice_fusion.refs_0_), channel_id=1, source_target_pairs={{0,16},{1,17},{2,18},{3,19},{4,20},{5,21},{6,22},{7,23},{8,24},{9,... | collective-permute-start | bytes 393224 | tf_op jit(solution)/shard_map/ppermute | solution.py:428
  39.4 1.3 %collective-permute-start.9 = (bf16[64,512]{1,0:T(8,128)(2,1)S(1)}, bf16[64,512]{1,0:T(8,128)(2,1)S(1)}, u32[]{:S(2)}, u32[]{:S(2)}) collective-permute-start(bf16[64,512]{1,0:T(8,128)(2,1)S(1)} %get-tuple-element.44), channel_id=1, source_target_pairs={{0,1},{1,0},{2,3},{3,2},{4,5},{5,4},{6,7},{7,6},{8,9},{9,8},{10,11... | collective-permute-start | bytes 196616 | tf_op jit(solution)/shard_map/ppermute | solution.py:535
  40.7 5.7 %collective-permute-start.17 = (bf16[128,512]{1,0:T(8,128)(2,1)S(1)}, bf16[128,512]{1,0:T(8,128)(2,1)S(1)}, u32[]{:S(2)}, u32[]{:S(2)}) collective-permute-start(bf16[128,512]{1,0:T(8,128)(2,1)S(1)} %constant_dynamic-update-slice_fusion.2.refs_1_), channel_id=1, source_target_pairs={{0,4},{1,9},{2,6},{3,11},{4,0},{5,13},{6,2},{7,15},{8,12},{9,1},{1... | collective-permute-start | bytes 393224 | tf_op jit(solution)/shard_map/ppermute | solution.py:428
  41.3 10.9 %collective-permute-start.16 = (bf16[128,512]{1,0:T(8,128)(2,1)S(1)}, bf16[128,512]{1,0:T(8,128)(2,1)S(1)}, u32[]{:S(2)}, u32[]{:S(2)}) collective-permute-start(bf16[128,512]{1,0:T(8,128)(2,1)S(1)} %constant_dynamic-update-slice_fusion.2.refs_1_), channel_id=1, source_target_pairs={{0,8},{1,5},{2,10},{3,7},{4,12},{5,1},{6,14},{7,3},{8,0},{9,13},{1... | collective-permute-start | bytes 393224 | tf_op jit(solution)/shard_map/ppermute | solution.py:428
  41.7 8.9 %collective-permute-start.10 = (bf16[128,512]{1,0:T(8,128)(2,1)S(1)}, bf16[128,512]{1,0:T(8,128)(2,1)S(1)}, u32[]{:S(2)}, u32[]{:S(2)}) collective-permute-start(bf16[128,512]{1,0:T(8,128)(2,1)S(1)} %constant_dynamic-update-slice_fusion.2.refs_1_), channel_id=1, source_target_pairs={{0,16},{1,17},{2,18},{3,19},{4,20},{5,21},{6,22},{7,23},{8,24},{9,... | collective-permute-start | bytes 393224 | tf_op jit(solution)/shard_map/ppermute | solution.py:428
  44.9 6.0 %collective-permute-start.12 = (bf16[128,512]{1,0:T(8,128)(2,1)S(1)}, bf16[128,512]{1,0:T(8,128)(2,1)S(1)}, u32[]{:S(2)}, u32[]{:S(2)}) collective-permute-start(bf16[128,512]{1,0:T(8,128)(2,1)S(1)} %collective-permute-done.6.refs_0_), channel_id=1, source_target_pairs={{0,4},{1,9},{2,6},{3,11},{4,0},{5,13},{6,2},{7,15},{8,12},{9,1},{1... | collective-permute-start | bytes 393224 | tf_op jit(solution)/shard_map/ppermute | solution.py:428
  46.5 5.7 %collective-permute-start.19 = (bf16[128,512]{1,0:T(8,128)(2,1)S(1)}, bf16[128,512]{1,0:T(8,128)(2,1)S(1)}, u32[]{:S(2)}, u32[]{:S(2)}) collective-permute-start(bf16[128,512]{1,0:T(8,128)(2,1)S(1)} %collective-permute-done.15.refs_2_), channel_id=1, source_target_pairs={{0,4},{1,9},{2,6},{3,11},{4,0},{5,13},{6,2},{7,15},{8,12},{9,1},{1... | collective-permute-start | bytes 393224 | tf_op jit(solution)/shard_map/ppermute | solution.py:428
  47.0 7.2 %collective-permute-start.7 = (bf16[128,512]{1,0:T(8,128)(2,1)S(1)}, bf16[128,512]{1,0:T(8,128)(2,1)S(1)}, u32[]{:S(2)}, u32[]{:S(2)}) collective-permute-start(bf16[128,512]{1,0:T(8,128)(2,1)S(1)} %collective-permute-done.6.refs_0_), channel_id=1, source_target_pairs={{0,8},{1,5},{2,10},{3,7},{4,12},{5,1},{6,14},{7,3},{8,0},{9,13},{1... | collective-permute-start | bytes 393224 | tf_op jit(solution)/shard_map/ppermute | solution.py:428
  50.6 8.6 %collective-permute-start.21 = (bf16[128,512]{1,0:T(8,128)(2,1)S(1)}, bf16[128,512]{1,0:T(8,128)(2,1)S(1)}, u32[]{:S(2)}, u32[]{:S(2)}) collective-permute-start(bf16[128,512]{1,0:T(8,128)(2,1)S(1)} %collective-permute-done.10.refs_1_), channel_id=1, source_target_pairs={{0,8},{1,5},{2,10},{3,7},{4,12},{5,1},{6,14},{7,3},{8,0},{9,13},{1... | collective-permute-start | bytes 393224 | tf_op jit(solution)/shard_map/ppermute | solution.py:428
  50.9 5.0 %collective-permute-start.13 = (bf16[128,512]{1,0:T(8,128)(2,1)S(1)}, bf16[128,512]{1,0:T(8,128)(2,1)S(1)}, u32[]{:S(2)}, u32[]{:S(2)}) collective-permute-start(bf16[128,512]{1,0:T(8,128)(2,1)S(1)} %collective-permute-done.10.refs_1_), channel_id=1, source_target_pairs={{0,4},{1,9},{2,6},{3,11},{4,0},{5,13},{6,2},{7,15},{8,12},{9,1},{1... | collective-permute-start | bytes 393224 | tf_op jit(solution)/shard_map/ppermute | solution.py:428
  52.2 7.0 %collective-permute-start.20 = (bf16[128,512]{1,0:T(8,128)(2,1)S(1)}, bf16[128,512]{1,0:T(8,128)(2,1)S(1)}, u32[]{:S(2)}, u32[]{:S(2)}) collective-permute-start(bf16[128,512]{1,0:T(8,128)(2,1)S(1)} %collective-permute-done.16.refs_3_), channel_id=1, source_target_pairs={{0,4},{1,9},{2,6},{3,11},{4,0},{5,13},{6,2},{7,15},{8,12},{9,1},{1... | collective-permute-start | bytes 393224 | tf_op jit(solution)/shard_map/ppermute | solution.py:428
  55.9 7.3 %collective-permute-start.14 = (bf16[128,512]{1,0:T(8,128)(2,1)S(1)}, bf16[128,512]{1,0:T(8,128)(2,1)S(1)}, u32[]{:S(2)}, u32[]{:S(2)}) collective-permute-start(bf16[128,512]{1,0:T(8,128)(2,1)S(1)} %collective-permute-done.7.refs_6_), channel_id=1, source_target_pairs={{0,4},{1,9},{2,6},{3,11},{4,0},{5,13},{6,2},{7,15},{8,12},{9,1},{1... | collective-permute-start | bytes 393224 | tf_op jit(solution)/shard_map/ppermute | solution.py:428
  57.2 6.0 %collective-permute-start.18 = (bf16[128,512]{1,0:T(8,128)(2,1)S(1)}, bf16[128,512]{1,0:T(8,128)(2,1)S(1)}, u32[]{:S(2)}, u32[]{:S(2)}) collective-permute-start(bf16[128,512]{1,0:T(8,128)(2,1)S(1)} %collective-permute-done.13.refs_5_), channel_id=1, source_target_pairs={{0,8},{1,5},{2,10},{3,7},{4,12},{5,1},{6,14},{7,3},{8,0},{9,13},{1... | collective-permute-start | bytes 393224 | tf_op jit(solution)/shard_map/ppermute | solution.py:428
  (3 other events, 24.3 us)

commit v6 on v5

--- a/solution.py
+++ b/solution.py
@@ -69,11 +69,9 @@
     sems,
 ):
     loads = [pltpu.make_async_copy(x_hbm, x_ref, sems.at[0])]
-    loads += [
-        pltpu.make_async_copy(wqkv_hbm.at[j], wqkv_ref.at[j], sems.at[1 + j]) for j in range(3)
-    ]
-    loads.append(pltpu.make_async_copy(wout_hbm, wout_ref, sems.at[4]))
-    loads.append(pltpu.make_async_copy(gain_hbm, gain_ref, sems.at[5]))
+    loads.append(pltpu.make_async_copy(wqkv_hbm, wqkv_ref, sems.at[1]))
+    loads.append(pltpu.make_async_copy(wout_hbm, wout_ref, sems.at[2]))
+    loads.append(pltpu.make_async_copy(gain_hbm, gain_ref, sems.at[3]))
     for load in loads:
         load.start()
     rows, width = mixed_ref.shape
@@ -83,11 +81,10 @@
     other_rows = pl.ds(pl.multiple_of((1 - core) * half, half), half)
 
     loads[0].wait()
-    loads[5].wait()
+    loads[3].wait()
     own_ref[...] = x_ref[own_rows, :]
     normed = layer_norm(x_ref[...].astype(F32), gain_ref[...].reshape(1, -1)).astype(BF16)
-    for load in loads[1:4]:
-        load.wait()
+    loads[1].wait()
     weights = wqkv_ref[...].reshape(3 * width, x_ref.shape[1])
     qkv = lax.dot_general(normed, weights, NT, preferred_element_type=F32).astype(BF16)
     q, k, v = [qkv[:, j * width : (j + 1) * width] for j in range(3)]
@@ -103,7 +100,7 @@
         probs = (expo * (1.0 / jnp.sum(expo, axis=-1, keepdims=True))).astype(BF16)
         mixed = mixed + jnp.dot(probs, jnp.where(own, v, zero), preferred_element_type=F32)
     mixed_ref[...] = mixed.astype(BF16)
-    loads[4].wait()
+    loads[2].wait()
     send_ref[...] = jnp.dot(
         mixed_ref[other_rows, :], wout_ref[...], preferred_element_type=F32
     ).astype(BF16)
@@ -128,7 +125,7 @@
             pltpu.VMEM(w_qkv_t.shape, BF16),
             pltpu.VMEM(w_out.shape, BF16),
             pltpu.VMEM((rows, own), BF16),
-            pltpu.SemaphoreType.DMA((6,)),
+            pltpu.SemaphoreType.DMA((4,)),
         ],
         compiler_params=params(12),
         cost_estimate=cost(2 * rows * width * 4 * own, 8 * width * own, rows * rows * own // VHD),
@@ -458,7 +455,7 @@
         got[3] = one(got[2])
     acc = attend(slots(0, 2, 1), None, False)
     images[1][5], acc = tie((images[1][5], acc))
-    images[0][7] = one(images[0][6])
+    images[0][7] = two(images[0][5])
     images[1][7] = two(images[1][5])
     for several in ((4, 3, 5, 6), (7,)):
         acc = attend(slots(*several), acc, several == (7,))

time: 65 us -> 65.6 us (level)
  starting transfers between devices: 20.4 us -> 21.4 us
  waiting for transfers between devices: 21.8 us -> 21.1 us
    ppermute x14, starting transfers between devices: 14.4 us -> 15.4 us  [swap_line(): return lax.ppermute(value, ('seq', 'head'), pairs)]
    ppermute x14, waiting for transfers between devices: 8.65 us -> 7.93 us  [swap_line(): return lax.ppermute(value, ('seq', 'head'), pairs)]
  transfers between devices with their start and end apart: 22 -> 22, of which waited for: 11 -> 11; matrix products, arithmetic and copies ran while one was open for 2% -> 2% of each run, Pallas kernels for 19% -> 18%
where the time goes in v6:
time: 65.6 us; the launch traced here: 65.3 us
  starting transfers between devices  21.4 us (33%)
  waiting for transfers between devices  21.1 us (32%)
  Pallas kernels  20.4 us (31%)
  matrix products  1.07 us (2%)
  between operations  1.04 us (2%)
    ppermute x14, starting transfers between devices, swap_line(): return lax.ppermute(value, ('seq', 'head'), pairs)  15.4 us
    ppermute x14, waiting for transfers between devices, swap_line(): return lax.ppermute(value, ('seq', 'head'), pairs)  7.93 us
    ppermute x3, waiting for transfers between devices, swap_chip(): lax.ppermute(value, 'head', [(i, i ^ bit) for i in range(head_count)])  7.56 us
    pallas_call x3, Pallas kernels, cross(): pl.pallas_call(functools.partial(cross_kernel, [(bits, len(chunks)) for b...  6.92 us
    pallas_call x1, Pallas kernels, encode(): pl.pallas_call(encode_kernel, in_specs=[SM, SM, HB, HB, HB, HB], out_spec...  5.19 us
    ppermute x3, starting transfers between devices, swap_chip(): lax.ppermute(value, 'head', [(i, i ^ bit) for i in range(head_count)])  5.05 us
    pallas_call x1, Pallas kernels, fetch(): pl.pallas_call(fetch_kernel, in_specs=[SM, HB, HB, HB, AN], out_specs=[VM...  3.71 us
    ppermute x2, waiting for transfers between devices, per_device(): blocks.append(jnp.concatenate([own, swap_core(send)], axis=0))  2.45 us
  transfers between devices with their start and end apart: 22, of which 11 were waited for; matrix products, arithmetic and copies ran while one was open for 2% of the time, Pallas kernels for 18%

profile of v6, /device:TPU:0, one launch (start us, length us, event | category | flops | bytes accessed | tf_op | source)
XLA Modules:
  0.0 65.3 jit_solution(8868522018756883844)
XLA Ops:
  0.7 5.2 %encode.1 = (bf16[128,1280]{1,0:T(8,128)(2,1)S(1)}, f32[128,1280]{1,0:T(8,128)S(1)}, bf16[128,1280]{1,0:T(8,128)(2,1)S(1)}) custom-call(s32[1]{0:T(128)} %bitcast.1.core_ref, s32[1]{0:T(128)S(6)} %copy.30.live_ref, f32[1280]{0:T(1024)} %gain_hbm.1, bf16[256,1280]{1,0:T(8,128)(2,1)} %bitcast.16, bf16[3,320,1280]{2,1,0:T(8,128)(2,1)} %bitcast.15, ...), custom_call_target="tpu_custom_call" | custom-call | flops 838860800 | bytes 3276800 | tf_op jit(solution)/shard_map/encode/pallas_call | solution.py:113
  6.4 1.3 %collective-permute-done = bf16[128,1280]{1,0:T(8,128)(2,1)S(1)} collective-permute-done((bf16[128,1280]{1,0:T(8,128)(2,1)S(1)}, bf16[128,1280]{1,0:T(8,128)(2,1)S(1)}, u32[]{:S(2)}, u32[]{:S(2)}) %collective-permute-start) | collective-permute-done | bytes 327712 | tf_op jit(solution)/shard_map/ppermute | solution.py:515
  7.7 3.0 %collective-permute-start.1 = (bf16[128,1280]{1,0:T(8,128)(2,1)S(1)}, bf16[128,1280]{1,0:T(8,128)(2,1)S(1)}, u32[]{:S(2)}, u32[]{:S(2)}) collective-permute-start(bf16[128,1280]{1,0:T(8,128)(2,1)S(1)} %add_convert_fusion._.first_ref), channel_id=1, source_target_pairs={{0,2},{1,3},{2,0},{3,1},{4,6},{5,7},{6,4},{7,5},{8,10},{9,11},{10,... | collective-permute-start | bytes 983048 | tf_op jit(solution)/shard_map/ppermute | solution.py:490
  10.8 1.6 %norm_queries.1 = (bf16[2,2,1024,128]{3,2,1,0:T(8,128)(2,1)S(1)}, s32[4,128]{1,0:T(4,128)S(1)}) custom-call(s32[16]{0:T(128)S(1)} %reshape.15.mask_ref, s32[1]{0:T(128)} %bitcast.seq_ref, s32[1]{0:T(128)} %bitcast.1.core_ref, bf16[256,2048]{1,0:T(8,128)(2,1)S(1)} %copy-done, f32[128]{0:T(128)S(1)} %copy-done.3), custom_call_target="tpu_custom_call" | custom-call | flops 4194304 | bytes 2097152 | tf_op jit(solution)/shard_map/norm_queries/pallas_call | solution.py:274
  12.4 3.7 %fetch.1 = (bf16[1280,1280]{1,0:T(8,128)(2,1)S(1)}, bf16[1280,1280]{1,0:T(8,128)(2,1)S(1)}, bf16[1280,2,512]{2,1,0:T(2,128)(2,1)S(1)}) custom-call(s32[1]{0:T(128)} %bitcast.2.chip_ref, bf16[1280,1280]{1,0:T(8,128)(2,1)} %w1_hbm.1, bf16[1280,1280]{1,0:T(8,128)(2,1)} %w2_hbm.1, bf16[1280,2,1024]{2,1,0:T(2,128)(2,1)} %wkv_hbm.1, ...), custom_call_target="tpu_custom_call" | custom-call | bytes 32768000 | tf_op jit(solution)/shard_map/fetch/pallas_call | solution.py:174
  16.1 2.5 %collective-permute-done.1.second_ref = bf16[128,1280]{1,0:T(8,128)(2,1)S(1)} collective-permute-done((bf16[128,1280]{1,0:T(8,128)(2,1)S(1)}, bf16[128,1280]{1,0:T(8,128)(2,1)S(1)}, u32[]{:S(2)}, u32[]{:S(2)}) %collective-permute-start.1) | collective-permute-done | bytes 327712 | tf_op jit(solution)/shard_map/ppermute | solution.py:490
  19.1 1.6 %collective-permute-done.2.normed_ref = bf16[128,1280]{1,0:T(8,128)(2,1)S(1)} collective-permute-done((bf16[128,1280]{1,0:T(8,128)(2,1)S(1)}, bf16[128,1280]{1,0:T(8,128)(2,1)S(1)}, u32[]{:S(2)}, u32[]{:S(2)}) %collective-permute-start.2) | collective-permute-done | bytes 327712 | tf_op jit(solution)/shard_map/ppermute | solution.py:521
  20.7 1.2 %mlp.3 = bf16[128,1280]{1,0:T(8,128)(2,1)S(1)} custom-call(bf16[128,1280]{1,0:T(8,128)(2,1)S(1)} %collective-permute-done.2.normed_ref, bf16[1280,1280]{1,0:T(8,128)(2,1)S(1)} %get-tuple-element.36.w1_ref, bf16[1280,1280]{1,0:T(8,128)(2,1)S(1)} %get-tuple-element.37.w2_ref), custom_call_target="tpu_custom_call" | custom-call | flops 838860800 | bytes 6553600 | tf_op jit(solution)/shard_map/mlp/pallas_call | solution.py:194
  22.1 1.2 %mlp.2 = f32[128,1280]{1,0:T(8,128)S(1)} custom-call(bf16[128,1280]{1,0:T(8,128)(2,1)S(1)} %get-tuple-element.35.normed_ref, bf16[1280,1280]{1,0:T(8,128)(2,1)S(1)} %get-tuple-element.36.w1_ref, bf16[1280,1280]{1,0:T(8,128)(2,1)S(1)} %get-tuple-element.37.w2_ref), custom_call_target="tpu_custom_call" | custom-call | flops 838860800 | bytes 6553600 | tf_op jit(solution)/shard_map/mlp/pallas_call | solution.py:194
  23.6 1.8 %collective-permute-start.4 = (bf16[64,1280]{1,0:T(8,128)(2,1)S(1)}, bf16[64,1280]{1,0:T(8,128)(2,1)S(1)}, u32[]{:S(2)}, u32[]{:S(2)}) collective-permute-start(bf16[64,1280]{1,0:T(8,128)(2,1)S(1)} %get-tuple-element.52), channel_id=1, source_target_pairs={{0,2},{1,3},{2,0},{3,1},{4,6},{5,7},{6,4},{7,5},{8,10},{9,11},{10,... | collective-permute-start | bytes 491528 | tf_op jit(solution)/shard_map/ppermute | solution.py:490
  25.7 5.0 %collective-permute-done.4 = bf16[64,1280]{1,0:T(8,128)(2,1)S(1)} collective-permute-done((bf16[64,1280]{1,0:T(8,128)(2,1)S(1)}, bf16[64,1280]{1,0:T(8,128)(2,1)S(1)}, u32[]{:S(2)}, u32[]{:S(2)}) %collective-permute-start.4) | collective-permute-done | bytes 163872 | tf_op jit(solution)/shard_map/ppermute | solution.py:490
  31.6 1.2 %collective-permute-done.5 = bf16[64,512]{1,0:T(8,128)(2,1)S(1)} collective-permute-done((bf16[64,512]{1,0:T(8,128)(2,1)S(1)}, bf16[64,512]{1,0:T(8,128)(2,1)S(1)}, u32[]{:S(2)}, u32[]{:S(2)}) %collective-permute-start.5) | collective-permute-done | bytes 65568 | tf_op jit(solution)/shard_map/ppermute | solution.py:532
  32.8 1.8 %collective-permute-start.14 = (bf16[128,512]{1,0:T(8,128)(2,1)S(1)}, bf16[128,512]{1,0:T(8,128)(2,1)S(1)}, u32[]{:S(2)}, u32[]{:S(2)}) collective-permute-start(bf16[128,512]{1,0:T(8,128)(2,1)S(1)} %constant_dynamic-update-slice_fusion.refs_0_), channel_id=1, source_target_pairs={{0,8},{1,5},{2,10},{3,7},{4,12},{5,1},{6,14},{7,3},{8,0},{9,13},{1... | collective-permute-start | bytes 393224 | tf_op jit(solution)/shard_map/ppermute | solution.py:425
  34.6 1.5 %collective-permute-start.7 = (bf16[128,512]{1,0:T(8,128)(2,1)S(1)}, bf16[128,512]{1,0:T(8,128)(2,1)S(1)}, u32[]{:S(2)}, u32[]{:S(2)}) collective-permute-start(bf16[128,512]{1,0:T(8,128)(2,1)S(1)} %constant_dynamic-update-slice_fusion.refs_0_), channel_id=1, source_target_pairs={{0,4},{1,9},{2,6},{3,11},{4,0},{5,13},{6,2},{7,15},{8,12},{9,1},{1... | collective-permute-start | bytes 393224 | tf_op jit(solution)/shard_map/ppermute | solution.py:425
  36.1 2.6 %collective-permute-start.6 = (bf16[128,512]{1,0:T(8,128)(2,1)S(1)}, bf16[128,512]{1,0:T(8,128)(2,1)S(1)}, u32[]{:S(2)}, u32[]{:S(2)}) collective-permute-start(bf16[128,512]{1,0:T(8,128)(2,1)S(1)} %constant_dynamic-update-slice_fusion.refs_0_), channel_id=1, source_target_pairs={{0,16},{1,17},{2,18},{3,19},{4,20},{5,21},{6,22},{7,23},{8,24},{9,... | collective-permute-start | bytes 393224 | tf_op jit(solution)/shard_map/ppermute | solution.py:425
  39.5 1.2 %collective-permute-done.11 = bf16[64,512]{1,0:T(8,128)(2,1)S(1)} collective-permute-done((bf16[64,512]{1,0:T(8,128)(2,1)S(1)}, bf16[64,512]{1,0:T(8,128)(2,1)S(1)}, u32[]{:S(2)}, u32[]{:S(2)}) %collective-permute-start.11) | collective-permute-done | bytes 65568 | tf_op jit(solution)/shard_map/ppermute | solution.py:532
  42.1 2.8 %collective-permute-done.6.refs_0_ = bf16[128,512]{1,0:T(8,128)(2,1)S(1)} collective-permute-done((bf16[128,512]{1,0:T(8,128)(2,1)S(1)}, bf16[128,512]{1,0:T(8,128)(2,1)S(1)}, u32[]{:S(2)}, u32[]{:S(2)}) %collective-permute-start.6) | collective-permute-done | bytes 131104 | tf_op jit(solution)/shard_map/ppermute | solution.py:425
  45.1 1.3 %collective-permute-done.16.refs_5_ = bf16[128,512]{1,0:T(8,128)(2,1)S(1)} collective-permute-done((bf16[128,512]{1,0:T(8,128)(2,1)S(1)}, bf16[128,512]{1,0:T(8,128)(2,1)S(1)}, u32[]{:S(2)}, u32[]{:S(2)}) %collective-permute-start.16) | collective-permute-done | bytes 131104 | tf_op jit(solution)/shard_map/ppermute | solution.py:425
  47.6 2.9 %collective-permute-done.12.refs_1_ = bf16[128,512]{1,0:T(8,128)(2,1)S(1)} collective-permute-done((bf16[128,512]{1,0:T(8,128)(2,1)S(1)}, bf16[128,512]{1,0:T(8,128)(2,1)S(1)}, u32[]{:S(2)}, u32[]{:S(2)}) %collective-permute-start.12) | collective-permute-done | bytes 131104 | tf_op jit(solution)/shard_map/ppermute | solution.py:425
  50.9 1.3 %collective-permute-start.13 = (bf16[128,512]{1,0:T(8,128)(2,1)S(1)}, bf16[128,512]{1,0:T(8,128)(2,1)S(1)}, u32[]{:S(2)}, u32[]{:S(2)}) collective-permute-start(bf16[128,512]{1,0:T(8,128)(2,1)S(1)} %collective-permute-done.12.refs_1_), channel_id=1, source_target_pairs={{0,4},{1,9},{2,6},{3,11},{4,0},{5,13},{6,2},{7,15},{8,12},{9,1},{1... | collective-permute-start | bytes 393224 | tf_op jit(solution)/shard_map/ppermute | solution.py:425
  52.9 1.3 %cross.3.refs_8_ = f32[2,2,1024,256]{3,2,1,0:T(8,128)S(1)} custom-call(s32[4,128]{1,0:T(4,128)S(1)} %get-tuple-element.28.flags_ref, bf16[2,2,1024,128]{3,2,1,0:T(8,128)(2,1)S(1)} %get-tuple-element.29.__.q_ref, bf16[128,512]{1,0:T(8,128)(2,1)S(1)} %constant_dynamic-update-slice_fusion.refs_0_, ...), custom_call_target="tpu_custom_call" | custom-call | flops 1610612736 | bytes 2097152 | tf_op jit(solution)/shard_map/cross/pallas_call | solution.py:398
  54.2 4.3 %collective-permute-start.9 = (bf16[128,512]{1,0:T(8,128)(2,1)S(1)}, bf16[128,512]{1,0:T(8,128)(2,1)S(1)}, u32[]{:S(2)}, u32[]{:S(2)}) collective-permute-start(bf16[128,512]{1,0:T(8,128)(2,1)S(1)} %collective-permute-done.8.refs_4_), channel_id=1, source_target_pairs={{0,8},{1,5},{2,10},{3,7},{4,12},{5,1},{6,14},{7,3},{8,0},{9,13},{1... | collective-permute-start | bytes 393224 | tf_op jit(solution)/shard_map/ppermute | solution.py:425
  58.6 4.0 %cross.4.refs_2_ = f32[2,2,1024,256]{3,2,1,0:T(8,128)S(1)} custom-call(s32[4,128]{1,0:T(4,128)S(1)} %get-tuple-element.28.flags_ref, bf16[2,2,1024,128]{3,2,1,0:T(8,128)(2,1)S(1)} %get-tuple-element.29.__.q_ref, bf16[128,512]{1,0:T(8,128)(2,1)S(1)} %collective-permute-done.6.refs_0_, ...), custom_call_target="tpu_custom_call", output_to_operand_aliasing={{}: (10, {})} | custom-call | flops 2147483648 | bytes 2097152 | tf_op jit(solution)/shard_map/cross/pallas_call | solution.py:398
  63.5 1.7 %cross.5 = (bf16[256,2048]{1,0:T(8,128)(2,1)}, f32[2,2,1024,256]{3,2,1,0:T(8,128)S(1)}) custom-call(s32[4,128]{1,0:T(4,128)S(1)} %get-tuple-element.28.flags_ref, bf16[2,2,1024,128]{3,2,1,0:T(8,128)(2,1)S(1)} %get-tuple-element.29.__.q_ref, bf16[128,512]{1,0:T(8,128)(2,1)S(1)} %collective-permute-done.9.refs_0_, ...), custom_call_target="tpu_custom_call", output_to_operand_aliasing={{1}: (4, {})} | custom-call | flops 536870912 | bytes 2097152 | tf_op jit(solution)/shard_map/cross/pallas_call | solution.py:398
  (50 shorter events, 8.3 us)
Async XLA Ops:
  0.7 10.1 %copy-start = (bf16[256,2048]{1,0:T(8,128)(2,1)S(1)}, bf16[256,2048]{1,0:T(8,128)(2,1)}, u32[]{:S(2)}) copy-start(bf16[256,2048]{1,0:T(8,128)(2,1)} %text_ref.1) | copy-start | bytes 3145732
  0.7 10.1 %copy-start.3 = (f32[128]{0:T(128)S(1)}, f32[128]{0:T(128)}, u32[]{:S(2)}) copy-start(f32[128]{0:T(128)} %gain_ref.4) | copy-start | bytes 1540
  5.9 1.8 %collective-permute-start = (bf16[128,1280]{1,0:T(8,128)(2,1)S(1)}, bf16[128,1280]{1,0:T(8,128)(2,1)S(1)}, u32[]{:S(2)}, u32[]{:S(2)}) collective-permute-start(bf16[128,1280]{1,0:T(8,128)(2,1)S(1)} %get-tuple-element.31), channel_id=1, source_target_pairs={{0,1},{1,0},{2,3},{3,2},{4,5},{5,4},{6,7},{7,6},{8,9},{9,8},{10,11... | collective-permute-start | bytes 983048 | tf_op jit(solution)/shard_map/ppermute | solution.py:515
  7.7 11.0 %collective-permute-start.1 = (bf16[128,1280]{1,0:T(8,128)(2,1)S(1)}, bf16[128,1280]{1,0:T(8,128)(2,1)S(1)}, u32[]{:S(2)}, u32[]{:S(2)}) collective-permute-start(bf16[128,1280]{1,0:T(8,128)(2,1)S(1)} %add_convert_fusion._.first_ref), channel_id=1, source_target_pairs={{0,2},{1,3},{2,0},{3,1},{4,6},{5,7},{6,4},{7,5},{8,10},{9,11},{10,... | collective-permute-start | bytes 983048 | tf_op jit(solution)/shard_map/ppermute | solution.py:490
  19.0 1.7 %collective-permute-start.2 = (bf16[128,1280]{1,0:T(8,128)(2,1)S(1)}, bf16[128,1280]{1,0:T(8,128)(2,1)S(1)}, u32[]{:S(2)}, u32[]{:S(2)}) collective-permute-start(bf16[128,1280]{1,0:T(8,128)(2,1)S(1)} %get-tuple-element.35.normed_ref), channel_id=1, source_target_pairs={{0,1},{1,0},{2,3},{3,2},{4,5},{5,4},{6,7},{7,6},{8,9},{9,8},{10,11... | collective-permute-start | bytes 983048 | tf_op jit(solution)/shard_map/ppermute | solution.py:521
  21.9 1.7 %collective-permute-start.3 = (bf16[128,1280]{1,0:T(8,128)(2,1)S(1)}, bf16[128,1280]{1,0:T(8,128)(2,1)S(1)}, u32[]{:S(2)}, u32[]{:S(2)}) collective-permute-start(bf16[128,1280]{1,0:T(8,128)(2,1)S(1)} %mlp.3), channel_id=1, source_target_pairs={{0,1},{1,0},{2,3},{3,2},{4,5},{5,4},{6,7},{7,6},{8,9},{9,8},{10,11... | collective-permute-start | bytes 983048 | tf_op jit(solution)/shard_map/ppermute | solution.py:523
  23.6 7.1 %collective-permute-start.4 = (bf16[64,1280]{1,0:T(8,128)(2,1)S(1)}, bf16[64,1280]{1,0:T(8,128)(2,1)S(1)}, u32[]{:S(2)}, u32[]{:S(2)}) collective-permute-start(bf16[64,1280]{1,0:T(8,128)(2,1)S(1)} %get-tuple-element.52), channel_id=1, source_target_pairs={{0,2},{1,3},{2,0},{3,1},{4,6},{5,7},{6,4},{7,5},{8,10},{9,11},{10,... | collective-permute-start | bytes 491528 | tf_op jit(solution)/shard_map/ppermute | solution.py:490
  25.5 13.2 %collective-permute-start.10 = (bf16[64,1280]{1,0:T(8,128)(2,1)S(1)}, bf16[64,1280]{1,0:T(8,128)(2,1)S(1)}, u32[]{:S(2)}, u32[]{:S(2)}) collective-permute-start(bf16[64,1280]{1,0:T(8,128)(2,1)S(1)} %get-tuple-element.51), channel_id=1, source_target_pairs={{0,2},{1,3},{2,0},{3,1},{4,6},{5,7},{6,4},{7,5},{8,10},{9,11},{10,... | collective-permute-start | bytes 491528 | tf_op jit(solution)/shard_map/ppermute | solution.py:490
  31.5 1.3 %collective-permute-start.5 = (bf16[64,512]{1,0:T(8,128)(2,1)S(1)}, bf16[64,512]{1,0:T(8,128)(2,1)S(1)}, u32[]{:S(2)}, u32[]{:S(2)}) collective-permute-start(bf16[64,512]{1,0:T(8,128)(2,1)S(1)} %get-tuple-element.40), channel_id=1, source_target_pairs={{0,1},{1,0},{2,3},{3,2},{4,5},{5,4},{6,7},{7,6},{8,9},{9,8},{10,11... | collective-permute-start | bytes 196616 | tf_op jit(solution)/shard_map/ppermute | solution.py:532
  32.8 12.3 %collective-permute-start.14 = (bf16[128,512]{1,0:T(8,128)(2,1)S(1)}, bf16[128,512]{1,0:T(8,128)(2,1)S(1)}, u32[]{:S(2)}, u32[]{:S(2)}) collective-permute-start(bf16[128,512]{1,0:T(8,128)(2,1)S(1)} %constant_dynamic-update-slice_fusion.refs_0_), channel_id=1, source_target_pairs={{0,8},{1,5},{2,10},{3,7},{4,12},{5,1},{6,14},{7,3},{8,0},{9,13},{1... | collective-permute-start | bytes 393224 | tf_op jit(solution)/shard_map/ppermute | solution.py:425
  34.6 7.1 %collective-permute-start.7 = (bf16[128,512]{1,0:T(8,128)(2,1)S(1)}, bf16[128,512]{1,0:T(8,128)(2,1)S(1)}, u32[]{:S(2)}, u32[]{:S(2)}) collective-permute-start(bf16[128,512]{1,0:T(8,128)(2,1)S(1)} %constant_dynamic-update-slice_fusion.refs_0_), channel_id=1, source_target_pairs={{0,4},{1,9},{2,6},{3,11},{4,0},{5,13},{6,2},{7,15},{8,12},{9,1},{1... | collective-permute-start | bytes 393224 | tf_op jit(solution)/shard_map/ppermute | solution.py:425
  36.1 8.8 %collective-permute-start.6 = (bf16[128,512]{1,0:T(8,128)(2,1)S(1)}, bf16[128,512]{1,0:T(8,128)(2,1)S(1)}, u32[]{:S(2)}, u32[]{:S(2)}) collective-permute-start(bf16[128,512]{1,0:T(8,128)(2,1)S(1)} %constant_dynamic-update-slice_fusion.refs_0_), channel_id=1, source_target_pairs={{0,16},{1,17},{2,18},{3,19},{4,20},{5,21},{6,22},{7,23},{8,24},{9,... | collective-permute-start | bytes 393224 | tf_op jit(solution)/shard_map/ppermute | solution.py:425
  39.4 1.3 %collective-permute-start.11 = (bf16[64,512]{1,0:T(8,128)(2,1)S(1)}, bf16[64,512]{1,0:T(8,128)(2,1)S(1)}, u32[]{:S(2)}, u32[]{:S(2)}) collective-permute-start(bf16[64,512]{1,0:T(8,128)(2,1)S(1)} %get-tuple-element.44), channel_id=1, source_target_pairs={{0,1},{1,0},{2,3},{3,2},{4,5},{5,4},{6,7},{7,6},{8,9},{9,8},{10,11... | collective-permute-start | bytes 196616 | tf_op jit(solution)/shard_map/ppermute | solution.py:532
  40.7 5.7 %collective-permute-start.16 = (bf16[128,512]{1,0:T(8,128)(2,1)S(1)}, bf16[128,512]{1,0:T(8,128)(2,1)S(1)}, u32[]{:S(2)}, u32[]{:S(2)}) collective-permute-start(bf16[128,512]{1,0:T(8,128)(2,1)S(1)} %constant_dynamic-update-slice_fusion.2.refs_1_), channel_id=1, source_target_pairs={{0,4},{1,9},{2,6},{3,11},{4,0},{5,13},{6,2},{7,15},{8,12},{9,1},{1... | collective-permute-start | bytes 393224 | tf_op jit(solution)/shard_map/ppermute | solution.py:425
  41.2 10.9 %collective-permute-start.15 = (bf16[128,512]{1,0:T(8,128)(2,1)S(1)}, bf16[128,512]{1,0:T(8,128)(2,1)S(1)}, u32[]{:S(2)}, u32[]{:S(2)}) collective-permute-start(bf16[128,512]{1,0:T(8,128)(2,1)S(1)} %constant_dynamic-update-slice_fusion.2.refs_1_), channel_id=1, source_target_pairs={{0,8},{1,5},{2,10},{3,7},{4,12},{5,1},{6,14},{7,3},{8,0},{9,13},{1... | collective-permute-start | bytes 393224 | tf_op jit(solution)/shard_map/ppermute | solution.py:425
  41.7 8.9 %collective-permute-start.12 = (bf16[128,512]{1,0:T(8,128)(2,1)S(1)}, bf16[128,512]{1,0:T(8,128)(2,1)S(1)}, u32[]{:S(2)}, u32[]{:S(2)}) collective-permute-start(bf16[128,512]{1,0:T(8,128)(2,1)S(1)} %constant_dynamic-update-slice_fusion.2.refs_1_), channel_id=1, source_target_pairs={{0,16},{1,17},{2,18},{3,19},{4,20},{5,21},{6,22},{7,23},{8,24},{9,... | collective-permute-start | bytes 393224 | tf_op jit(solution)/shard_map/ppermute | solution.py:425
  44.9 6.0 %collective-permute-start.8 = (bf16[128,512]{1,0:T(8,128)(2,1)S(1)}, bf16[128,512]{1,0:T(8,128)(2,1)S(1)}, u32[]{:S(2)}, u32[]{:S(2)}) collective-permute-start(bf16[128,512]{1,0:T(8,128)(2,1)S(1)} %collective-permute-done.6.refs_0_), channel_id=1, source_target_pairs={{0,4},{1,9},{2,6},{3,11},{4,0},{5,13},{6,2},{7,15},{8,12},{9,1},{1... | collective-permute-start | bytes 393224 | tf_op jit(solution)/shard_map/ppermute | solution.py:425
  46.4 5.7 %collective-permute-start.18 = (bf16[128,512]{1,0:T(8,128)(2,1)S(1)}, bf16[128,512]{1,0:T(8,128)(2,1)S(1)}, u32[]{:S(2)}, u32[]{:S(2)}) collective-permute-start(bf16[128,512]{1,0:T(8,128)(2,1)S(1)} %collective-permute-done.14.refs_2_), channel_id=1, source_target_pairs={{0,4},{1,9},{2,6},{3,11},{4,0},{5,13},{6,2},{7,15},{8,12},{9,1},{1... | collective-permute-start | bytes 393224 | tf_op jit(solution)/shard_map/ppermute | solution.py:425
  47.0 11.6 %collective-permute-start.20 = (bf16[128,512]{1,0:T(8,128)(2,1)S(1)}, bf16[128,512]{1,0:T(8,128)(2,1)S(1)}, u32[]{:S(2)}, u32[]{:S(2)}) collective-permute-start(bf16[128,512]{1,0:T(8,128)(2,1)S(1)} %collective-permute-done.6.refs_0_), channel_id=1, source_target_pairs={{0,8},{1,5},{2,10},{3,7},{4,12},{5,1},{6,14},{7,3},{8,0},{9,13},{1... | collective-permute-start | bytes 393224 | tf_op jit(solution)/shard_map/ppermute | solution.py:425
  50.6 8.0 %collective-permute-start.21 = (bf16[128,512]{1,0:T(8,128)(2,1)S(1)}, bf16[128,512]{1,0:T(8,128)(2,1)S(1)}, u32[]{:S(2)}, u32[]{:S(2)}) collective-permute-start(bf16[128,512]{1,0:T(8,128)(2,1)S(1)} %collective-permute-done.12.refs_1_), channel_id=1, source_target_pairs={{0,8},{1,5},{2,10},{3,7},{4,12},{5,1},{6,14},{7,3},{8,0},{9,13},{1... | collective-permute-start | bytes 393224 | tf_op jit(solution)/shard_map/ppermute | solution.py:425
  50.9 7.6 %collective-permute-start.13 = (bf16[128,512]{1,0:T(8,128)(2,1)S(1)}, bf16[128,512]{1,0:T(8,128)(2,1)S(1)}, u32[]{:S(2)}, u32[]{:S(2)}) collective-permute-start(bf16[128,512]{1,0:T(8,128)(2,1)S(1)} %collective-permute-done.12.refs_1_), channel_id=1, source_target_pairs={{0,4},{1,9},{2,6},{3,11},{4,0},{5,13},{6,2},{7,15},{8,12},{9,1},{1... | collective-permute-start | bytes 393224 | tf_op jit(solution)/shard_map/ppermute | solution.py:425
  52.2 6.4 %collective-permute-start.19 = (bf16[128,512]{1,0:T(8,128)(2,1)S(1)}, bf16[128,512]{1,0:T(8,128)(2,1)S(1)}, u32[]{:S(2)}, u32[]{:S(2)}) collective-permute-start(bf16[128,512]{1,0:T(8,128)(2,1)S(1)} %collective-permute-done.15.refs_3_), channel_id=1, source_target_pairs={{0,4},{1,9},{2,6},{3,11},{4,0},{5,13},{6,2},{7,15},{8,12},{9,1},{1... | collective-permute-start | bytes 393224 | tf_op jit(solution)/shard_map/ppermute | solution.py:425
  54.2 8.4 %collective-permute-start.9 = (bf16[128,512]{1,0:T(8,128)(2,1)S(1)}, bf16[128,512]{1,0:T(8,128)(2,1)S(1)}, u32[]{:S(2)}, u32[]{:S(2)}) collective-permute-start(bf16[128,512]{1,0:T(8,128)(2,1)S(1)} %collective-permute-done.8.refs_4_), channel_id=1, source_target_pairs={{0,8},{1,5},{2,10},{3,7},{4,12},{5,1},{6,14},{7,3},{8,0},{9,13},{1... | collective-permute-start | bytes 393224 | tf_op jit(solution)/shard_map/ppermute | solution.py:425
  58.5 5.0 %collective-permute-start.17 = (bf16[128,512]{1,0:T(8,128)(2,1)S(1)}, bf16[128,512]{1,0:T(8,128)(2,1)S(1)}, u32[]{:S(2)}, u32[]{:S(2)}) collective-permute-start(bf16[128,512]{1,0:T(8,128)(2,1)S(1)} %collective-permute-done.13.refs_5_), channel_id=1, source_target_pairs={{0,8},{1,5},{2,10},{3,7},{4,12},{5,1},{6,14},{7,3},{8,0},{9,13},{1... | collective-permute-start | bytes 393224 | tf_op jit(solution)/shard_map/ppermute | solution.py:425
  (3 other events, 24.3 us)
